TPU v7x, 32 devices: a whole 2x2x4 slice. The times are simulated.
32 devices in a mesh: dp: 8 (over y, x, core), mp: 4 (over z).
Axes of the slice: x: 2, y: 2, z: 4, core: 2. Of those that a mesh axis runs over, the one named last changes fastest.
Arguments:
- inputs: bfloat16 [8192, 2048], P('dp'), may hold values from -6 to 6
- doc_ids: int32 [8, 1024], P('dp'), may hold values from 0 to 3, never falling along the last dimension, each value on 1 to 512 neighbouring positions
- pad_mask: int32 [8, 1024], P('dp'), may hold values from 0 to 1, as said below
- attn_gain: float32 [2048], replicated, may hold values from 0.5 to 1.5
- attn_shift: float32 [2048], replicated, may hold values from -4 to 4
- w_query: bfloat16 [2048, 2048], P(None, 'mp'), may hold values from -0.125 to 0.125
- b_query: float32 [2048], P('mp'), may hold values from -4 to 4
- w_keyval: bfloat16 [2048, 256], replicated, may hold values from -0.125 to 0.125
- b_value: float32 [128], replicated, may hold values from -4 to 4
- w_out: bfloat16 [2048, 2048], P('mp'), may hold values from -0.5 to 0.5
- b_out: float32 [2048], replicated, may hold values from -4 to 4
- mlp_gain: float32 [2048], replicated, may hold values from 0.5 to 1.5
- mlp_shift: float32 [2048], replicated, may hold values from -4 to 4
- w_up: bfloat16 [2048, 8192], P(None, 'mp'), may hold values from -0.125 to 0.125
- b_up: float32 [8192], P('mp'), may hold values from -4 to 4
- w_down: bfloat16 [8192, 2048], P('mp'), may hold values from -0.0625 to 0.0625
- b_down: float32 [2048], replicated, may hold values from -4 to 4
- cotangent: bfloat16 [8192, 2048], P('dp'), may hold values from -6 to 6
Outputs:
- outputs: bfloat16 [8192, 2048], P('dp')
- input_grad: bfloat16 [8192, 2048], P('dp')
- grad_attn_gain: float32 [2048], replicated
- grad_attn_shift: float32 [2048], replicated
- grad_w_query: float32 [2048, 2048], P('dp', 'mp')
- grad_b_query: float32 [2048], P('mp')
- grad_w_keyval: float32 [2048, 256], replicated
- grad_b_value: float32 [128], replicated
- grad_w_out: float32 [2048, 2048], P('mp', 'dp')
- grad_b_out: float32 [2048], replicated
- grad_mlp_gain: float32 [2048], replicated
- grad_mlp_shift: float32 [2048], replicated
- grad_w_up: float32 [2048, 8192], P('dp', 'mp')
- grad_b_up: float32 [8192], P('mp')
- grad_w_down: float32 [8192, 2048], P('mp', 'dp')
- grad_b_down: float32 [2048], replicated
Inputs may be any that keep to these rules, and one draw needn't show every extreme that they name: `doc_ids`: in each row the document numbers never fall and start at 0. `pad_mask`: in each row of 1024 tokens the ones come first, then zeros; a row's first token is a one.
All inputs are finite; a program needn't handle non-finite values.
Results may differ from a plain program's by a relative error of at most 0.012.
Values sent between devices are 32-bit elements; how exact they have to be, the bound alone decides.
A program may use at most 256 MiB of HBM per device.

v0:
```python
from functools import partial
import math

import jax
import jax.numpy as jnp
from jax import lax
from jax.sharding import PartitionSpec as P

EPS = 1e-05


def norm_rows(rows_in, gain, shift):
    center = rows_in - jnp.mean(rows_in, axis=-1, keepdims=True)
    spread = jnp.mean(center * center, axis=-1, keepdims=True)
    return center * lax.rsqrt(spread + EPS) * gain + shift


def project(left, right):
    return jnp.dot(left, right, preferred_element_type=jnp.float32)


def allow_pairs(first_row, count, doc_row, pad_row):
    query_place = first_row + jnp.arange(count, dtype=jnp.int32)
    key_place = jnp.arange(doc_row.shape[0], dtype=jnp.int32)
    query_doc = lax.dynamic_slice_in_dim(doc_row, first_row, count)
    return (
        (key_place[None, :] <= query_place[:, None])
        & (doc_row[None, :] == query_doc[:, None])
        & ((pad_row[None, :] == 1) | (key_place[None, :] == query_place[:, None]))
    )


def block_scores(query_row, keys, first_row, count, doc_row, pad_row):
    head_size = keys.shape[1]
    rows_q = lax.dynamic_slice_in_dim(query_row, first_row, count, 0)
    heads = rows_q.reshape(count, -1, head_size)
    scores = jnp.einsum("shd,td->hst", heads, keys, preferred_element_type=jnp.float32) * (
        1.0 / math.sqrt(head_size)
    )
    allowed = allow_pairs(first_row, count, doc_row, pad_row)
    return (jnp.where(allowed[None], scores, -1e30), heads)


def attend_row(query_row, keyval_row, doc_row, pad_row):
    head_size = keyval_row.shape[1] // 2
    keys = keyval_row[:, :head_size]
    values = keyval_row[:, head_size:]
    seq_len = query_row.shape[0]
    block = min(512, seq_len)

    def one_block(block_id):
        first_row = block_id * block
        scores, heads = block_scores(query_row, keys, first_row, block, doc_row, pad_row)
        row_max = jnp.max(scores, axis=-1, keepdims=True)
        raised = jnp.exp(scores - row_max)
        row_total = jnp.sum(raised, axis=-1, keepdims=True)
        weights = (raised / row_total).astype(jnp.bfloat16)
        mixed = jnp.einsum(
            "hst,td->shd", weights, values, preferred_element_type=jnp.float32
        ).reshape(block, -1)
        return (mixed.astype(jnp.bfloat16), (row_max + jnp.log(row_total))[..., 0])

    mixed, log_sums = lax.map(one_block, jnp.arange(seq_len // block, dtype=jnp.int32))
    return (mixed.reshape(seq_len, -1), log_sums)


def attend_back(query_row, keyval_row, doc_row, pad_row, log_sums, grad_row):
    head_size = keyval_row.shape[1] // 2
    keys = keyval_row[:, :head_size]
    values = keyval_row[:, head_size:]
    seq_len = query_row.shape[0]
    block = min(512, seq_len)
    scale = 1.0 / math.sqrt(head_size)

    def one_block(carry, block_id):
        d_keys, d_values = carry
        first_row = block_id * block
        scores, heads = block_scores(query_row, keys, first_row, block, doc_row, pad_row)
        grads_in = lax.dynamic_slice_in_dim(grad_row, first_row, block, 0).reshape(
            block, -1, head_size
        )
        probs = jnp.exp(scores - log_sums[block_id][..., None])
        d_probs = jnp.einsum("shd,td->hst", grads_in, values, preferred_element_type=jnp.float32)
        inner = jnp.sum(probs * d_probs, axis=-1, keepdims=True)
        d_scores = (probs * (d_probs - inner)).astype(jnp.bfloat16)
        d_query = (
            jnp.einsum("hst,td->shd", d_scores, keys, preferred_element_type=jnp.float32) * scale
        )
        d_keys = (
            d_keys
            + jnp.einsum("hst,shd->td", d_scores, heads, preferred_element_type=jnp.float32) * scale
        )
        d_values = d_values + jnp.einsum(
            "hst,shd->td", probs.astype(jnp.bfloat16), grads_in, preferred_element_type=jnp.float32
        )
        return ((d_keys, d_values), d_query.reshape(block, -1).astype(jnp.bfloat16))

    empty = jnp.zeros((seq_len, head_size), jnp.float32)
    (d_keys, d_values), d_query = lax.scan(
        one_block, (empty, empty), jnp.arange(seq_len // block, dtype=jnp.int32)
    )
    return (d_query.reshape(seq_len, -1), jnp.concatenate([d_keys, d_values], axis=1))


def shards(
    inputs,
    doc_ids,
    pad_mask,
    attn_gain,
    attn_shift,
    w_query,
    b_query,
    w_keyval,
    b_value,
    w_out,
    b_out,
    mlp_gain,
    mlp_shift,
    w_up,
    b_up,
    w_down,
    b_down,
    cotangent,
):
    row_count = doc_ids.shape[0]
    seq_len = doc_ids.shape[1]
    head_size = b_value.shape[0]
    inputs_f = inputs.astype(jnp.float32)
    bias_full = jnp.concatenate([jnp.zeros((head_size,), jnp.float32), b_value])

    def attn_inputs():
        normed_attn = norm_rows(inputs_f, attn_gain, attn_shift).astype(jnp.bfloat16)
        queries = (project(normed_attn, w_query) + b_query).astype(jnp.bfloat16)
        keyval = (project(normed_attn, w_keyval) + bias_full).astype(jnp.bfloat16)
        return (normed_attn, queries, keyval)

    def mlp_inputs(middle):
        normed_mlp = norm_rows(middle, mlp_gain, mlp_shift).astype(jnp.bfloat16)
        hidden = project(normed_mlp, w_up) + b_up
        acts = jax.nn.gelu(hidden, approximate=True).astype(jnp.bfloat16)
        return (normed_mlp, hidden, acts)

    normed_attn, queries, keyval = attn_inputs()
    query_rows = queries.reshape(row_count, seq_len, -1)
    keyval_rows = keyval.reshape(row_count, seq_len, -1)
    mixed_rows, log_sums = lax.map(
        lambda item: attend_row(*item), (query_rows, keyval_rows, doc_ids, pad_mask)
    )
    mixed = mixed_rows.reshape(inputs.shape[0], -1)
    attn_part = project(mixed, w_out)
    middle = inputs_f + lax.psum(attn_part, "mp") + b_out
    normed_mlp, hidden, acts = mlp_inputs(middle)
    feed = lax.psum(project(acts, w_down), "mp") + b_down
    outputs = (middle + feed).astype(jnp.bfloat16)
    cotangent_f = cotangent.astype(jnp.float32)
    normed_mlp, hidden, acts = mlp_inputs(middle)
    grad_w_down = jnp.einsum("tf,td->fd", acts, cotangent, preferred_element_type=jnp.float32)
    grad_b_down = jnp.sum(cotangent_f, axis=0)
    d_acts = jnp.einsum("td,fd->tf", cotangent, w_down, preferred_element_type=jnp.float32)
    gelu_out, gelu_pull = jax.vjp(partial(jax.nn.gelu, approximate=True), hidden)
    d_hidden = gelu_pull(d_acts)[0].astype(jnp.bfloat16)
    grad_b_up = jnp.sum(d_hidden.astype(jnp.float32), axis=0)
    grad_w_up = jnp.einsum("td,tf->df", normed_mlp, d_hidden, preferred_element_type=jnp.float32)
    d_normed_mlp = lax.psum(
        jnp.einsum("tf,df->td", d_hidden, w_up, preferred_element_type=jnp.float32), "mp"
    )
    norm_out, mlp_pull = jax.vjp(norm_rows, middle, mlp_gain, mlp_shift)
    d_middle_norm, grad_mlp_gain, grad_mlp_shift = mlp_pull(d_normed_mlp)
    d_middle = cotangent_f + d_middle_norm
    normed_attn, queries, keyval = attn_inputs()
    d_branch = d_middle.astype(jnp.bfloat16)
    grad_b_out = jnp.sum(d_branch.astype(jnp.float32), axis=0)
    grad_w_out = jnp.einsum("tq,td->qd", mixed, d_branch, preferred_element_type=jnp.float32)
    d_mixed = jnp.einsum("td,qd->tq", d_branch, w_out, preferred_element_type=jnp.float32).astype(
        jnp.bfloat16
    )
    query_rows = queries.reshape(row_count, seq_len, -1)
    keyval_rows = keyval.reshape(row_count, seq_len, -1)
    grad_rows = d_mixed.reshape(row_count, seq_len, -1)
    d_query_rows, d_keyval_rows = lax.map(
        lambda item: attend_back(*item),
        (query_rows, keyval_rows, doc_ids, pad_mask, log_sums, grad_rows),
    )
    d_queries = d_query_rows.reshape(inputs.shape[0], -1)
    d_keyval_sum = lax.psum(d_keyval_rows.reshape(inputs.shape[0], -1), "mp")
    grad_b_value = jnp.sum(d_keyval_sum[:, head_size:], axis=0)
    d_keyval = d_keyval_sum.astype(jnp.bfloat16)
    grad_b_query = jnp.sum(d_queries.astype(jnp.float32), axis=0)
    grad_w_query = jnp.einsum(
        "td,tq->dq", normed_attn, d_queries, preferred_element_type=jnp.float32
    )
    grad_w_keyval = jnp.einsum(
        "td,tk->dk", normed_attn, d_keyval, preferred_element_type=jnp.float32
    )
    query_part = jnp.einsum("tq,dq->td", d_queries, w_query, preferred_element_type=jnp.float32)
    d_normed_attn = lax.psum(query_part, "mp") + jnp.einsum(
        "tk,dk->td", d_keyval, w_keyval, preferred_element_type=jnp.float32
    )
    norm_in, attn_pull = jax.vjp(norm_rows, inputs_f, attn_gain, attn_shift)
    d_inputs_norm, grad_attn_gain, grad_attn_shift = attn_pull(d_normed_attn)
    input_grad = (d_middle + d_inputs_norm).astype(jnp.bfloat16)
    (
        grad_attn_gain,
        grad_attn_shift,
        grad_b_query,
        grad_w_keyval,
        grad_b_value,
        grad_b_out,
        grad_mlp_gain,
        grad_mlp_shift,
        grad_b_up,
        grad_b_down,
    ) = lax.psum(
        (
            grad_attn_gain,
            grad_attn_shift,
            grad_b_query,
            grad_w_keyval,
            grad_b_value,
            grad_b_out,
            grad_mlp_gain,
            grad_mlp_shift,
            grad_b_up,
            grad_b_down,
        ),
        "dp",
    )
    grad_w_query, grad_w_out, grad_w_up, grad_w_down = (
        lax.psum_scatter(grad_w_query, "dp", scatter_dimension=0, tiled=True),
        lax.psum_scatter(grad_w_out, "dp", scatter_dimension=1, tiled=True),
        lax.psum_scatter(grad_w_up, "dp", scatter_dimension=0, tiled=True),
        lax.psum_scatter(grad_w_down, "dp", scatter_dimension=1, tiled=True),
    )
    return (
        outputs,
        input_grad,
        grad_attn_gain,
        grad_attn_shift,
        grad_w_query,
        grad_b_query,
        grad_w_keyval,
        grad_b_value,
        grad_w_out,
        grad_b_out,
        grad_mlp_gain,
        grad_mlp_shift,
        grad_w_up,
        grad_b_up,
        grad_w_down,
        grad_b_down,
    )


def solution(mesh):
    return jax.shard_map(
        shards,
        mesh=mesh,
        in_specs=(
            P("dp", None),
            P("dp", None),
            P("dp", None),
            P(),
            P(),
            P(None, "mp"),
            P("mp"),
            P(),
            P(),
            P("mp", None),
            P(),
            P(),
            P(),
            P(None, "mp"),
            P("mp"),
            P("mp", None),
            P(),
            P("dp", None),
        ),
        out_specs=(
            P("dp", None),
            P("dp", None),
            P(),
            P(),
            P("dp", "mp"),
            P("mp"),
            P(),
            P(),
            P("mp", "dp"),
            P(),
            P(),
            P(),
            P("dp", "mp"),
            P("mp"),
            P("mp", "dp"),
            P(),
        ),
        check_vma=False,
    )
```

profile of v0, /device:TPU:0, one launch (start us, length us, event | category | flops | bytes accessed | tf_op | source)
XLA Modules:
  0.0 1810.7 jit_solution(8742808315754998242)
XLA Ops:
  7.3 3.0 convert_reduce_fusion
  10.3 3.5 fusion.55
  13.9 1.9 fusion.46
  15.8 2.0 copy-done.12
  17.8 1.2 fusion.59
  20.0 6.2 add_convert_fusion.3
  26.2 2.3 copy.47
  28.5 25.3 %while.46 = (s32[]{:T(128)}, bf16[2,512,512]{2,1,0:T(8,128)(2,1)}, f32[2,4,512]{2,1,0:T(4,128)S(1)}, s32[2]{0:T(128)S(1)}, s32[1024]{0:T(1024)S(1)}, /*index=5*/...) while((s32[]{:T(128)}, bf16[2,512,512]{2,1,0:T(8,128)(2,1)}, ...), condition=%wide.region_5.6_spmd, body=%wide.region_2.5_spmd.sunk | while | flops 1102315008 | bytes 32067796 | solution.py:63
  30.7 1.1 constant_dynamic-slice_fusion.6
  31.8 1.9 bitcast_reduce_fusion.2
  33.7 2.5 fusion.137
  36.2 3.9 fusion.138
  43.4 1.1 constant_dynamic-slice_fusion.6
  44.5 1.9 bitcast_reduce_fusion.2
  46.3 2.5 fusion.137
  48.8 3.9 fusion.138
  53.8 6.8 fusion.77
  60.9 293.4 %all-reduce.8.cloned.1.call-done = f32[1024,2048]{1,0:T(8,128)} async-done(((f32[1024,2048]{1,0:T(8,128)}), f32[1024,2048]{1,0:T(8,128)}) %all-reduce.8.cloned.1.call-update) | async-done | bytes 8388624 | tf_op jit(solution)/shard_map/psum | solution.py:151
  354.3 5.8 fusion.74
  361.2 15.4 fusion.69
  376.5 20.5 %convert_reduce_fusion.2 = (f32[2048]{0:T(1024)}, bf16[1024,2048]{1,0:T(8,128)(2,1)}) fusion(f32[1024,2048]{1,0:T(8,128)} %fusion.69, f32[2048]{0:T(1024)S(1)} %copy-done.52, bf16[1024,2048]{1,0:T(8,128)(2,1)} %param.39, bf16[2048,2048]{1,0:T(8,128)(2,1)} %param.37), kind=kOutput, calls=%fused_computation.86 | convolution fusion | flops 8638167040 | bytes 25182208 | tf_op jit(solution)/shard_map/td,fd->tf/dot_general | solution.py:159
  397.0 24.5 %fusion.78 = f32[1024,2048]{1,0:T(8,128)} fusion(bf16[1024,2048]{1,0:T(8,128)(2,1)} %get-tuple-element.324, bf16[2048,2048]{1,0:T(8,128)(2,1)} %param.35), kind=kOutput, calls=%fused_computation.127 | convolution fusion | flops 8589934592 | bytes 20971520 | tf_op jit(solution)/shard_map/tf,df->td/dot_general | solution.py:165
  421.8 17.9 fusion.67
  439.7 271.9 %all-reduce.10.cloned.1.call-done = f32[1024,2048]{1,0:T(8,128)} async-done(((f32[1024,2048]{1,0:T(8,128)}), f32[1024,2048]{1,0:T(8,128)}) %all-reduce.10.cloned.1.call-update) | async-done | bytes 8388624 | tf_op jit(solution)/shard_map/psum | solution.py:164
  711.6 8.1 multiply_reduce_fusion
  719.8 5.1 fusion.73
  725.5 3.1 convert_reduce_fusion.3
  728.7 1.9 copy-done.8
  730.6 3.3 convolution_convert_fusion
  733.9 42.2 %while.47 = (s32[]{:T(128)}, f32[1024,128]{1,0:T(8,128)S(1)}, f32[1024,128]{1,0:T(8,128)}, bf16[2,512,512]{1,2,0:T(8,128)(2,1)}, s32[2]{0:T(128)S(1)}, /*index=5...) while((s32[]{:T(128)}, f32[1024,128]{1,0:T(8,128)S(1)}, ...), condition=%wide.region_15.16_spmd.clone, body=%wide.region_13.15_spmd.clone.sunk | while | flops 2720136704 | bytes 87372184 | solution.py:99
  738.5 1.1 constant_dynamic-slice_fusion.8
  739.8 1.1 constant_dynamic-slice_fusion.7
  741.0 1.3 fusion.148
  742.2 2.9 fusion.153
  745.1 3.7 fusion.150
  748.8 2.4 fusion.151
  751.3 1.4 fusion.152
  752.7 1.5 fusion.154
  759.4 1.1 constant_dynamic-slice_fusion.8
  760.7 1.1 constant_dynamic-slice_fusion.7
  761.9 1.3 fusion.148
  763.2 2.9 fusion.153
  766.0 3.7 fusion.150
  769.8 2.4 fusion.151
  772.2 1.4 fusion.152
  773.6 1.5 fusion.154
  776.2 1.5 copy.53
  777.7 7.2 fusion.79
  787.2 6.6 fusion.81
  793.9 6.6 fusion.80
  800.5 16.4 fusion.68
  817.7 17.3 fusion.66
  836.4 547.2 %all-reduce.14.cloned.1.call-done = (f32[1024,2048]{1,0:T(8,128)}, f32[1024,2048]{1,0:T(8,128)}, f32[1024,256]{1,0:T(8,128)}) async-done(((f32[1024,2048]{1,0:T(8,128)}, f32[1024,2048]{1,0:T(8,128)}, f32[1024,256]{1,0:T(8,128)}), (f32[1024,2048]{1,0:T(8,128)}, f32[1024,2048]{1,0:T(8,128)}, f32[1024,256]{1,0:T(8,128)})) %all-reduce.14.cloned.1.call-update) | async-done | bytes 17825808 | tf_op jit(solution)/shard_map/psum | solution.py:153
  1383.6 6.4 fusion.70
  1390.1 3.9 fusion.47
  1395.9 2.7 fusion.60
  1398.6 12.9 convert_reduce_fusion.1
  1411.7 25.9 %all-reduce.1 = (f32[2048]{0:T(1024)}, f32[2048]{0:T(1024)}, f32[512]{0:T(512)}, f32[128]{0:T(128)}, f32[2048]{0:T(1024)}, /*index=5*/f32[2048]{0:T(1024)}, f32[2048]{0:T(1024)}, f32[2048]{0:T(1024)}, f32[2048]{0:T(1024)}) all-reduce(f32[2048]{0:T(1024)S(1)} %get-tuple-element.264, ...), channel_id=1, replica_groups=mesh['dp'=8,'mp'=4] {'dp'}, use_global_device_ids=true, to_apply=%region_21.22 | all-reduce | flops 14976 | bytes 119808 | tf_op jit(solution)/shard_map/psum | solution.py:213
  1437.6 10.2 add_convert_fusion.1
  1447.8 46.0 %reduce-scatter.5.cloned.1.call-done = f32[256,512]{1,0:T(8,128)} async-done(((f32[2048,512]{1,0:T(8,128)}), f32[256,512]{1,0:T(8,128)}) %reduce-scatter.5.cloned.1.call-update) | async-done | bytes 524304 | tf_op jit(solution)/shard_map/reduce_scatter | solution.py:229
  1493.8 120.4 %reduce-scatter.9.cloned.1.call-done = f32[256,2048]{1,0:T(8,128)} async-done(((f32[2048,2048]{1,0:T(8,128)}), f32[256,2048]{1,0:T(8,128)}) %reduce-scatter.9.cloned.1.call-update) | async-done | bytes 2097168 | tf_op jit(solution)/shard_map/reduce_scatter | solution.py:231
  1614.3 120.6 %reduce-scatter.11.cloned.1.call-done = f32[2048,256]{1,0:T(8,128)} async-done(((f32[2048,2048]{1,0:T(8,128)}), f32[2048,256]{1,0:T(8,128)}) %reduce-scatter.11.cloned.1.call-update) | async-done | bytes 2097168 | tf_op jit(solution)/shard_map/reduce_scatter | solution.py:232
  1734.8 65.6 %all-reduce.12.cloned.1.call-done = f32[2048,256]{1,0:T(8,128)} async-done(((f32[2048,256]{1,0:T(8,128)}), f32[2048,256]{1,0:T(8,128)}) %all-reduce.12.cloned.1.call-update) | async-done | bytes 2097168 | tf_op jit(solution)/shard_map/psum | solution.py:213
  1800.4 3.0 copy.100
  (188 shorter events, 20.7 us)
Async XLA Ops:
  7.2 46.6 %copy-start = (bf16[512,2048]{1,0:T(8,128)(2,1)S(1)}, bf16[512,2048]{1,0:T(8,128)(2,1)}, u32[]{:S(2)}) copy-start(bf16[512,2048]{1,0:T(8,128)(2,1)} %param.31) | copy-start | bytes 6291460
  7.2 6.6 copy-start.49
  7.2 6.7 copy-start.28
  7.2 6.7 copy-start.45
  7.2 347.1 %all-reduce.8.cloned.1.call-start = ((), (), s32[]{:S(2)}) async-start(), calls=%async_computation.4 | async-start | bytes 16777216 | tf_op jit(solution)/shard_map/psum | solution.py:151
  7.3 6.6 copy-start.3
  7.3 10.5 copy-start.19
  10.3 8.8 copy-start.26
  13.8 2.0 copy-start.38
  13.8 5.3 copy-start.30
  13.9 6.1 copy-start.54
  15.8 2.0 copy-start.12
  19.2 7.1 copy-start.10
  20.0 8.5 copy-start.21
  20.0 8.5 copy-start.25
  53.8 300.5 %copy-start.46 = (f32[2048]{0:T(1024)S(1)}, f32[2048]{0:T(1024)}, u32[]{:S(2)}) copy-start(f32[2048]{0:T(1024)} %param.32) | copy-start | bytes 24580
  60.6 650.9 %all-reduce.10.cloned.1.call-start = ((), (), s32[]{:S(2)}) async-start(), calls=%async_computation.5 | async-start | bytes 16777216 | tf_op jit(solution)/shard_map/psum | solution.py:164
  360.1 16.4 copy-start.2
  360.1 1.0 copy-start.40
  360.1 1.0 copy-start.50
  360.1 359.5 %copy-start.32 = (f32[1024]{0:T(1024)}, f32[1024]{0:T(1024)S(1)}, u32[]{:S(2)}) copy-start(f32[1024]{0:T(1024)S(1)} %broadcast_multiply_fusion) | copy-start | bytes 12292
  361.1 358.5 %copy-start.36 = (f32[1024]{0:T(1024)}, f32[1024]{0:T(1024)S(1)}, u32[]{:S(2)}) copy-start(f32[1024]{0:T(1024)S(1)} %fusion.64) | copy-start | bytes 12292
  361.2 15.4 copy-start.52
  421.6 962.0 %all-reduce.14.cloned.1.call-start = ((), (), s32[]{:S(2)}) async-start(), calls=%async_computation.11 | async-start | bytes 35651584 | tf_op jit(solution)/shard_map/psum | solution.py:153
  711.5 8.2 copy-start.7
  719.8 5.7 copy-start.9
  724.8 3.8 copy-start.5
  728.7 1.9 copy-start.8
  728.7 5.3 copy-start.11
  739.8 2.4 copy-start.22
  745.1 3.7 copy-start.23
  751.3 3.0 copy-start.14
  754.3 1.0 copy-start.15
  760.7 2.4 copy-start.22
  766.0 3.7 copy-start.23
  772.2 3.0 copy-start.14
  776.2 8.7 copy-start.24
  786.0 1.2 copy-start.18
  786.0 661.8 %reduce-scatter.7.cloned.1.call-start = ((), (), s32[]{:S(2)}) async-start(), calls=%async_computation.8 | async-start | bytes 4718592 | tf_op jit(solution)/shard_map/reduce_scatter | solution.py:230
  793.8 6.7 copy-start.33
  793.8 6.7 copy-start.37
  793.8 6.7 copy-start.41
  793.8 6.7 copy-start.51
  793.8 700.0 %reduce-scatter.5.cloned.1.call-start = ((), (), s32[]{:S(2)}) async-start(), calls=%async_computation.6 | async-start | bytes 4718592 | tf_op jit(solution)/shard_map/reduce_scatter | solution.py:229
  800.4 813.8 %reduce-scatter.9.cloned.1.call-start = ((), (), s32[]{:S(2)}) async-start(), calls=%async_computation.9 | async-start | bytes 18874368 | tf_op jit(solution)/shard_map/reduce_scatter | solution.py:231
  817.0 917.8 %reduce-scatter.11.cloned.1.call-start = ((), (), s32[]{:S(2)}) async-start(), calls=%async_computation.10 | async-start | bytes 18874368 | tf_op jit(solution)/shard_map/reduce_scatter | solution.py:232
  834.9 1.2 copy-start.16
  834.9 548.7 %copy-start.20 = (bf16[2048,256]{1,0:T(8,128)(2,1)S(1)}, bf16[2048,256]{1,0:T(8,128)(2,1)}, u32[]{:S(2)}) copy-start(bf16[2048,256]{1,0:T(8,128)(2,1)} %param.29) | copy-start | bytes 3145732
  834.9 548.7 %copy-start.27 = (f32[1024]{0:T(1024)S(1)}, f32[1024]{0:T(1024)}, u32[]{:S(2)}) copy-start(f32[1024]{0:T(1024)} %copy-done.26) | copy-start | bytes 12292
  835.0 548.7 %copy-start.29 = (f32[2048]{0:T(1024)S(1)}, f32[2048]{0:T(1024)}, u32[]{:S(2)}) copy-start(f32[2048]{0:T(1024)} %param.25) | copy-start | bytes 24580
  835.0 965.4 %all-reduce.12.cloned.1.call-start = ((), (), s32[]{:S(2)}) async-start(), calls=%async_computation.7 | async-start | bytes 4194304 | tf_op jit(solution)/shard_map/psum | solution.py:213
  1383.6 6.5 copy-start.39
  1383.6 6.5 copy-start.4
  1383.6 6.5 copy-start.31
  1390.1 4.4 copy-start.6
  1390.1 5.4 copy-start.13
  1390.1 5.8 copy-start.17
  1390.1 8.4 copy-start.35
  1398.6 13.1 copy-start.42
  1398.6 13.1 copy-start.43
  1398.6 13.1 copy-start.44
  1398.6 13.1 copy-start.48
  1398.6 39.0 %copy-start.47 = (f32[2048]{0:T(1024)S(1)}, f32[2048]{0:T(1024)}, u32[]{:S(2)}) copy-start(f32[2048]{0:T(1024)} %param.38) | copy-start | bytes 24580
  1437.6 365.8 %copy-start.1 = (bf16[512,2048]{1,0:T(8,128)(2,1)S(1)}, bf16[512,2048]{1,0:T(8,128)(2,1)}, u32[]{:S(2)}) copy-start(bf16[512,2048]{1,0:T(8,128)(2,1)} %param.31) | copy-start | bytes 6291460
  (3 other events, 2.3 us)
Sparse Core Ops, SparseCore 0:
  60.8 293.5 all-reduce.7
  421.7 289.8 all-reduce.9
  786.1 597.4 all-reduce.13
  1387.8 50.9 reduce-scatter.6
  1442.6 51.2 reduce-scatter.4
  1498.2 115.9 reduce-scatter.8
  1618.8 115.9 reduce-scatter.10
  1739.0 61.3 all-reduce.11
where the time goes:
time: 1820 us; the launch traced here: 1810 us
  waiting for transfers between devices  1470 us (81%)
  matrix products  192 us (11%)
  other arithmetic  73.1 us (4%)
  local copies, waits for them, and re-layouts  31 us (2%)
  blocking collectives  25.9 us (1%)
    psum x1, waiting for transfers between devices, shards(): feed = lax.psum(project(acts, w_down), 'mp') + b_down  547 us
    psum x1, waiting for transfers between devices, shards(): middle = inputs_f + lax.psum(attn_part, 'mp') + b_out  293 us
    psum x1, waiting for transfers between devices, shards(): lax.psum(jnp.einsum('tf,df->td', d_hidden, w_up, preferred_element_type=j...  272 us
    reduce_scatter x1, waiting for transfers between devices, shards(): lax.psum_scatter(grad_w_down, 'dp', scatter_dimension=1, tiled=True)  121 us
    reduce_scatter x1, waiting for transfers between devices, shards(): lax.psum_scatter(grad_w_up, 'dp', scatter_dimension=0, tiled=True)  120 us
    psum x1, waiting for transfers between devices, shards(): lax.psum((grad_attn_gain, grad_attn_shift, grad_b_query, grad_w_keyval, g...  65.6 us
    dot_general x5, matrix products, project(): return jnp.dot(left, right, preferred_element_type=jnp.float32)  47.5 us
    reduce_scatter x1, waiting for transfers between devices, shards(): lax.psum_scatter(grad_w_query, 'dp', scatter_dimension=0, tiled=True)  46 us
  transfers between devices with their start and end apart: 8, of which 7 were waited for; matrix products, arithmetic and copies ran while one was open for 6% of the time, Pallas kernels for 0%

commit v1 on v0

v1 whole, which is shorter than its diff:
```python
import functools
import math

import jax
import jax.numpy as jnp
from jax import lax
from jax.experimental import pallas as pl
from jax.experimental.pallas import tpu as pltpu
from jax.sharding import PartitionSpec as P

EPS = 1e-05
MESH = pl.DeviceIdType.MESH
F32 = jnp.float32
BF16 = jnp.bfloat16
VMEM_LIMIT = 60 * 2**20
HBM = pl.BlockSpec(memory_space=pl.ANY)


def norm_rows(rows_in, gain, shift):
    center = rows_in - jnp.mean(rows_in, axis=-1, keepdims=True)
    spread = jnp.mean(center * center, axis=-1, keepdims=True)
    return center * lax.rsqrt(spread + EPS) * gain + shift


def project(left, right):
    return jnp.dot(left, right, preferred_element_type=F32)


STRIP = 16
COLS = 512
BLOCK = 256
REACH = 3
GROUP = 4
NEG = -1e30


def key_window(c):
    first = max(0, c - REACH + 1) * BLOCK
    return first, (c + 1) * BLOCK - first


def mask_bias(code_col, doc_row, first_key, keys, first_query, queries):
    j = first_key + lax.broadcasted_iota(jnp.int32, (keys, queries), 0)
    i = first_query + lax.broadcasted_iota(jnp.int32, (keys, queries), 1)
    ok = ((j < i) & (code_col == doc_row)) | (j == i)
    return jnp.where(ok, 0.0, NEG)


def dot_t(a, b):
    return lax.dot_general(a, b, (((1,), (1,)), ((), ())), preferred_element_type=F32)


def rows_at(start, count):
    return pl.ds(pl.multiple_of(start, count), count)


def mp_partner(m, r):
    if r == 1:
        return m + 1 - 2 * lax.rem(m, 2)
    if r == 2:
        return m + 2 - 4 * lax.div(m, 2)
    return 3 - m


def flip_bit(d, bit):
    on = lax.rem(lax.div(d, bit), 2)
    return d + bit * (1 - 2 * on)


def front_kernel(
    heads,
    wq, wo, in_hbm, bq, w_kv, gain_ref, shift_ref, kv_bias, code_ref, doc_ref,
    wq_out, wo_out, normed_hbm, q_hbm, mixed_hbm, kv_ref, lse_ref,
    own_q, own_o, gq, go, sq, so, normed, q_ring, mixed_ring, vt, bias_ref, bq_all,
    load_sem, ship_sem, o_sem, ring_sem, z_send, z_recv, b_send, b_recv, n_send, n_recv,
):
    m = lax.axis_index("mp")
    d = lax.axis_index("dp")
    dc, dx, dy = flip_bit(d, 1), flip_bit(d, 2), flip_bit(d, 4)
    dxy = flip_bit(dx, 4)
    g = (gq, go)
    half = (gq.shape[2] // 2, go.shape[2] // 2)
    seq, width = normed.shape
    cols_q = q_ring.shape[2]
    hd = vt.shape[0]
    blocks = seq // BLOCK
    scale = 1.0 / math.sqrt(hd)
    planes = 4

    loads = [
        pltpu.make_async_copy(wq.at[d], own_q, load_sem.at[0]),
        pltpu.make_async_copy(wo.at[d], own_o, load_sem.at[1]),
        pltpu.make_async_copy(in_hbm, normed, load_sem.at[2]),
        pltpu.make_async_copy(wq, sq.at[m], load_sem.at[3]),
        pltpu.make_async_copy(wq, wq_out.at[m], load_sem.at[4]),
        pltpu.make_async_copy(wo, wo_out.at[m], load_sem.at[5]),
    ]
    for c in loads:
        c.start()
    bar = pltpu.get_barrier_semaphore()
    for r in (1, 2, 3):
        pl.semaphore_signal(bar, inc=1, device_id={"mp": mp_partner(m, r)}, device_id_type=MESH)
    for n in (dc, dx, dy):
        pl.semaphore_signal(bar, inc=1, device_id={"dp": n}, device_id_type=MESH)
    loads[0].wait()
    gq[m, d] = own_q[...].astype(F32)
    loads[1].wait()
    go[m, d] = own_o[...].astype(F32)
    bq_all[m] = bq[...]
    pl.semaphore_wait(bar, 6)

    def z_copy(w, r, eighth_of):
        ref = g[w].at[eighth_of, d]
        return pltpu.make_async_remote_copy(
            ref, ref, z_send.at[w, r - 1], z_recv.at[w, r - 1],
            device_id={"mp": mp_partner(m, r)}, device_id_type=MESH,
        )

    def z_send_copy(w, r):
        return z_copy(w, r, m)

    def z_land(w, r):
        return z_copy(w, r, mp_partner(m, r))

    def bias_copy(r, plane):
        return pltpu.make_async_remote_copy(
            bq_all.at[plane], bq_all.at[plane], b_send.at[r - 1], b_recv.at[r - 1],
            device_id={"mp": mp_partner(m, r)}, device_id_type=MESH,
        )

    sent_eighth = (d, d, d, dx, dy, dx, dy, dxy)
    landed_eighth = (dx, dy, dc, flip_bit(dx, 1), flip_bit(dy, 1), dxy, dxy, flip_bit(dxy, 1))
    sent_to = (dx, dy, dc, dc, dc, dy, dx, dc)

    def near(kind, w, r, eighths):
        q = mp_partner(m, r)
        ref = g[w].at[q, eighths[kind]]
        if kind == 5:
            ref = g[w].at[q, eighths[kind], pl.ds(0, half[w])]
        if kind == 6:
            ref = g[w].at[q, eighths[kind], pl.ds(half[w], half[w])]
        return pltpu.make_async_remote_copy(
            ref, ref, n_send.at[kind, w, r - 1], n_recv.at[kind, w, r - 1],
            device_id={"dp": sent_to[kind]}, device_id_type=MESH,
        )

    def go_near(kind, w, r):
        near(kind, w, r, sent_eighth).start()

    def landed(kind, w, r):
        near(kind, w, r, landed_eighth).wait_recv()

    shipped = []
    ring = so.shape[0]

    def ship(w, r, eighth):
        q = mp_partner(m, r)
        n = sum(1 for v, _ in shipped if v == w)
        if w == 0:
            sq[q, eighth] = gq[q, eighth].astype(BF16)
            c = pltpu.make_async_copy(sq.at[q, eighth], wq_out.at[q, eighth], ship_sem.at[n])
        else:
            slot = n % ring
            if n >= ring:
                [c for v, c in shipped if v == 1][n - ring].wait()
            so[slot] = go[q, eighth].astype(BF16)
            c = pltpu.make_async_copy(so.at[slot], wo_out.at[q, eighth], o_sem.at[slot])
        c.start()
        shipped.append((w, c))

    def store_q(q, c, slot):
        at = pl.ds(c * BLOCK, BLOCK)
        return pltpu.make_async_copy(
            q_ring.at[slot], q_hbm.at[at, rows_at(q * cols_q, cols_q)], ring_sem.at[0, slot]
        )

    def store_mixed(q, c, slot):
        at = pl.ds(c * BLOCK, BLOCK)
        return pltpu.make_async_copy(
            mixed_ring.at[slot], mixed_hbm.at[at, rows_at(q * cols_q, cols_q)], ring_sem.at[1, slot]
        )

    def set_bias(c):
        first, count = key_window(c)
        bias_ref[pl.ds(0, count), :] = mask_bias(
            code_ref[pl.ds(first, count), :], doc_ref[:, pl.ds(c * BLOCK, BLOCK)],
            first, count, c * BLOCK, BLOCK,
        )

    def attend_block(q, c, n):
        slot = lax.rem(n, 2) if not isinstance(n, int) else n % 2
        first, count = key_window(c)
        keys, at = pl.ds(first, count), pl.ds(c * BLOCK, BLOCK)

        def free():
            store_q(q, c, slot).wait()
            store_mixed(q, c, slot).wait()

        if not isinstance(n, int) or n >= 2:
            free()
        w = sq[q].reshape(width, cols_q)
        q_ring[slot] = (project(normed[at, :], w) + bq_all[q]).astype(BF16)
        store_q(q, c, slot).start()
        for u in range(cols_q // hd):
            head = pl.ds(u * hd, hd)
            s = dot_t(kv_ref[keys, pl.ds(0, hd)], q_ring[slot, :, head]) * scale
            s = s + bias_ref[pl.ds(0, count), :]
            top = jnp.max(s, axis=0, keepdims=True)
            e = jnp.exp(s - top)
            total = jnp.sum(e, axis=0, keepdims=True)
            probs = (e * (1.0 / total)).astype(BF16)
            mixed_ring[slot, :, head] = project(vt[:, keys], probs).T.astype(BF16)
            lse_ref[pl.ds(q * (cols_q // hd) + u, 1), at] = top + jnp.log(total)
        store_mixed(q, c, slot).start()

    def own_plane(c):
        set_bias(c)
        attend_block(m, c, c)

    def other_planes(c):
        set_bias(c)

        def one(r, carry):
            attend_block(lax.rem(m + r, planes), c, blocks + c * (planes - 1) + r - 1)
            return carry

        lax.fori_loop(1, planes, one, 0)

    stream = [(w, r) for w in (0, 1) for r in (1, 2, 3)]

    def stage(s):
        if s < len(stream):
            w, r = stream[s]
            z_land(w, r).wait_recv()
            if w == 0:
                z_send_copy(1, r).start()
            for kind in (0, 1, 2):
                go_near(kind, w, r)
            ship(w, r, d)
        if 1 <= s <= len(stream):
            w, r = stream[s - 1]
            landed(0, w, r)
            go_near(5, w, r)
            go_near(3, w, r)
            ship(w, r, dx)
            landed(1, w, r)
            go_near(6, w, r)
            go_near(4, w, r)
            ship(w, r, dy)
            landed(2, w, r)
            ship(w, r, dc)
        if 2 <= s <= len(stream) + 1:
            w, r = stream[s - 2]
            landed(5, w, r)
            landed(6, w, r)
            go_near(7, w, r)
            ship(w, r, dxy)
            for kind in (3, 4):
                landed(kind, w, r)
                ship(w, r, landed_eighth[kind])
            landed(7, w, r)
            ship(w, r, landed_eighth[7])

    for r in (1, 2, 3):
        z_send_copy(0, r).start()
    for r in (1, 2, 3):
        bias_copy(r, m).start()

    loads[2].wait()

    def norm_strip(i, carry):
        at = rows_at(i * STRIP, STRIP)
        normed[at, :] = norm_rows(normed[at, :].astype(F32), gain_ref[...], shift_ref[...]).astype(BF16)
        return carry

    lax.fori_loop(0, seq // STRIP, norm_strip, 0)
    keep_normed = pltpu.make_async_copy(normed, normed_hbm, load_sem.at[2])
    keep_normed.start()
    for c in range(blocks):
        at = pl.ds(c * BLOCK, BLOCK)
        kv = project(normed[at, :], w_kv[...]) + kv_bias[...]
        kv_ref[at, :] = kv.astype(BF16)
        vt[:, at] = kv[:, hd:].T.astype(BF16)
    loads[3].wait()

    stage(0)
    own_plane(0)
    stage(1)
    own_plane(1)
    own_plane(2)
    stage(2)
    own_plane(3)
    for r in (1, 2, 3):
        bias_copy(r, mp_partner(m, r)).wait_recv()
    stage(3)
    stage(4)
    other_planes(0)
    stage(5)
    other_planes(1)
    stage(6)
    other_planes(2)
    stage(7)
    other_planes(3)

    for slot in (0, 1):
        store_q(m, 0, slot).wait()
        store_mixed(m, 0, slot).wait()
    for w, r in stream:
        z_send_copy(w, r).wait_send()
        for kind in range(8):
            near(kind, w, r, sent_eighth).wait_send()
    for r in (1, 2, 3):
        bias_copy(r, m).wait_send()
    rows_o = [c for v, c in shipped if v == 1]
    for c in [c for v, c in shipped if v == 0] + rows_o[-ring:]:
        c.wait()
    keep_normed.wait()
    loads[4].wait()
    loads[5].wait()


def gather_by_sum(shard):
    blank = jnp.zeros((lax.axis_size("mp"),) + shard.shape, F32)
    half = shard.astype(F32) * 0.5
    own = lax.dynamic_update_index_in_dim(blank, half, lax.axis_index("mp"), 0)
    return lax.psum(own, "mp") * 2.0


def attention_front(
    inputs, w_query, b_query, w_keyval, kv_bias, w_out, gain, shift, codes, docs
):
    dp, mp = lax.axis_size("dp"), lax.axis_size("mp")
    width, cols = w_query.shape
    rows = w_out.shape[0]
    seq = inputs.shape[0]
    hd = w_keyval.shape[1] // 2
    code_col, doc_row = codes.reshape(seq, 1), docs.reshape(1, seq)
    if (dp, mp) != (8, 4):
        all_query, all_out, all_bias = (
            gather_by_sum(a).astype(a.dtype) for a in (w_query, w_out, b_query)
        )
        normed = norm_rows(inputs.astype(F32), gain, shift).astype(BF16)
        keyval = (project(normed, w_keyval) + kv_bias).astype(BF16)
        queries = jnp.concatenate(
            [project(normed, all_query[i]) + all_bias[i] for i in range(mp)], 1
        ).astype(BF16)
        mixed, lse = attend(queries, keyval, code_col, doc_row)
        return all_query, all_out.reshape(-1, width), normed, queries, mixed, keyval, lse
    wq = w_query.reshape(dp, width // dp, cols)
    wo = w_out.reshape(dp, rows // dp, width)
    dma = pltpu.SemaphoreType.DMA
    vmem = pl.BlockSpec(memory_space=pltpu.VMEM)
    full_q, full_o = (mp,) + wq.shape, (mp,) + wo.shape
    heads = mp * cols // hd
    shape = jax.ShapeDtypeStruct
    out_q, out_o, normed, queries, mixed, keyval, lse = pl.pallas_call(
        functools.partial(front_kernel, heads),
        out_shape=(
            shape(full_q, BF16),
            shape(full_o, BF16),
            shape((seq, width), BF16),
            shape((seq, mp * cols), BF16),
            shape((seq, mp * cols), BF16),
            shape((seq, 2 * hd), BF16),
            shape((heads, seq), F32),
        ),
        in_specs=[HBM] * 3 + [vmem] * 7,
        out_specs=(HBM,) * 5 + (vmem,) * 2,
        scratch_shapes=[
            pltpu.VMEM(wq.shape[1:], BF16),
            pltpu.VMEM(wo.shape[1:], BF16),
            pltpu.VMEM(full_q, F32),
            pltpu.VMEM(full_o, F32),
            pltpu.VMEM(full_q, BF16),
            pltpu.VMEM((4,) + wo.shape[1:], BF16),
            pltpu.VMEM((seq, width), BF16),
            pltpu.VMEM((2, BLOCK, cols), BF16),
            pltpu.VMEM((2, BLOCK, cols), BF16),
            pltpu.VMEM((hd, seq), BF16),
            pltpu.VMEM((REACH * BLOCK, BLOCK), F32),
            pltpu.VMEM((mp, 1, cols), F32),
            dma((6,)),
            dma((3 * dp,)),
            dma((4,)),
            dma((2, 2)),
            dma((2, 3)),
            dma((2, 3)),
            dma((3,)),
            dma((3,)),
            dma((8, 2, 3)),
            dma((8, 2, 3)),
        ],
        compiler_params=pltpu.CompilerParams(
            collective_id=0, has_side_effects=True, vmem_limit_bytes=VMEM_LIMIT
        ),
        name="attention_front",
    )(
        wq, wo, inputs, b_query.reshape(1, cols), w_keyval, gain.reshape(1, width),
        shift.reshape(1, width), kv_bias.reshape(1, 2 * hd), code_col, doc_row,
    )
    return (
        out_q.reshape(mp, width, cols), out_o.reshape(mp * rows, width),
        normed, queries, mixed, keyval, lse,
    )


PIECE = 32
CROSS_LATE = 2
LATE = 5
AHEAD = 3


class LineSum:
    scratch = staticmethod(
        lambda rows, width: [pltpu.VMEM((rows, width), F32)] * 3
        + [pltpu.SemaphoreType.DMA((rows // PIECE,))] * 5
    )

    def __init__(self, refs):
        self.part, self.total, self.cross, *sems = refs
        self.in_send, self.in_recv, self.over_send, self.over_recv, self.out_send = sems
        self.pieces = self.part.shape[0] // PIECE
        m = lax.axis_index("mp")
        self.is_end = (m == 0) | (m == 3)
        self.is_mid = (m == 1) | (m == 2)
        self.buddy = {"mp": mp_partner(m, 1)}
        self.across = {"mp": 3 - m}

    def greet(self, others=()):
        bar = pltpu.get_barrier_semaphore()
        pl.semaphore_signal(bar, inc=1, device_id=self.buddy, device_id_type=MESH)
        for other in others:
            pl.semaphore_signal(bar, inc=1, device_id=other, device_id_type=MESH)

        @pl.when(self.is_mid)
        def _():
            pl.semaphore_signal(bar, inc=1, device_id=self.across, device_id_type=MESH)

    def meet(self, others=()):
        bar = pltpu.get_barrier_semaphore()

        @pl.when(self.is_end)
        def _():
            pl.semaphore_wait(bar, 1 + len(others))

        @pl.when(self.is_mid)
        def _():
            pl.semaphore_wait(bar, 2 + len(others))

    def inward(self, k):
        at = rows_at(k * PIECE, PIECE)
        return pltpu.make_async_remote_copy(
            self.part.at[at], self.total.at[at], self.in_send.at[k], self.in_recv.at[k],
            device_id=self.buddy, device_id_type=MESH,
        )

    def over(self, k):
        at = rows_at(k * PIECE, PIECE)
        return pltpu.make_async_remote_copy(
            self.part.at[at], self.cross.at[at], self.over_send.at[k], self.over_recv.at[k],
            device_id=self.across, device_id_type=MESH,
        )

    def outward(self, k):
        at = rows_at(k * PIECE, PIECE)
        return pltpu.make_async_remote_copy(
            self.total.at[at], self.total.at[at], self.out_send.at[k], self.in_recv.at[k],
            device_id=self.buddy, device_id_type=MESH,
        )

    def tick(self, k):
        n = self.pieces

        @pl.when(self.is_end)
        def _():
            @pl.when(k < n)
            def _():
                @pl.when(k >= AHEAD)
                def _():
                    self.inward(k - AHEAD).wait_send()

                self.inward(k).start()

            @pl.when((k >= LATE) & (k < n + LATE))
            def _():
                self.outward(k - LATE).wait_recv()

        @pl.when(self.is_mid)
        def _():
            @pl.when(k < n)
            def _():
                at = rows_at(k * PIECE, PIECE)
                self.inward(k).wait_recv()
                self.part[at, :] += self.total[at, :]
                self.over(k).start()

            @pl.when((k >= CROSS_LATE) & (k < n + CROSS_LATE))
            def _():
                j = k - CROSS_LATE
                at = rows_at(j * PIECE, PIECE)
                self.over(j).wait_recv()
                self.total[at, :] = self.part[at, :] + self.cross[at, :]
                self.outward(j).start()

    def finish(self):
        n = self.pieces

        @pl.when(self.is_end)
        def _():
            for k in range(n - AHEAD, n):
                self.inward(k).wait_send()

        @pl.when(self.is_mid)
        def _():
            def sent(k, c):
                self.over(k).wait_send()
                self.outward(k).wait_send()
                return c

            lax.fori_loop(0, n, sent, 0)


def attend_kernel(seq, heads, q_ref, kv_ref, vt_ref, code_ref, doc_ref, mixed_ref, lse_ref, bias_ref):
    hd = vt_ref.shape[0]
    scale = 1.0 / math.sqrt(hd)
    for c in range(seq // BLOCK):

        @pl.when(pl.program_id(0) == c)
        def _(c=c):
            first, count = key_window(c)
            keys = pl.ds(first, count)
            bias_ref[pl.ds(0, count), :] = mask_bias(
                code_ref[keys, :], doc_ref[...], first, count, c * BLOCK, BLOCK
            )

            def some_heads(g, carry):
                for u in range(GROUP):
                    h = g * GROUP + u
                    cols = pl.ds(pl.multiple_of(h * hd, hd), hd)
                    s = dot_t(kv_ref[keys, pl.ds(0, hd)], q_ref[:, cols]) * scale
                    s = s + bias_ref[pl.ds(0, count), :]
                    top = jnp.max(s, axis=0, keepdims=True)
                    e = jnp.exp(s - top)
                    total = jnp.sum(e, axis=0, keepdims=True)
                    probs = (e * (1.0 / total)).astype(BF16)
                    mixed = project(vt_ref[:, keys], probs)
                    mixed_ref[:, cols] = mixed.T.astype(BF16)
                    lse_ref[pl.ds(h, 1), :] = top + jnp.log(total)
                return carry

            lax.fori_loop(0, heads // GROUP, some_heads, 0)


def attend(queries, keyval, code_col, doc_row):
    seq, width = queries.shape
    hd = keyval.shape[1] // 2
    heads = width // hd
    values_t = keyval[:, hd:].T
    whole = lambda *shape: pl.BlockSpec(shape, lambda c: (0,) * len(shape))
    return pl.pallas_call(
        functools.partial(attend_kernel, seq, heads),
        grid=(seq // BLOCK,),
        out_shape=(
            jax.ShapeDtypeStruct((seq, width), BF16),
            jax.ShapeDtypeStruct((heads, seq), F32),
        ),
        in_specs=[
            pl.BlockSpec((BLOCK, width), lambda c: (c, 0)),
            whole(seq, 2 * hd),
            whole(hd, seq),
            whole(seq, 1),
            pl.BlockSpec((1, BLOCK), lambda c: (0, c)),
        ],
        out_specs=(
            pl.BlockSpec((BLOCK, width), lambda c: (c, 0)),
            pl.BlockSpec((heads, BLOCK), lambda c: (0, c)),
        ),
        scratch_shapes=[pltpu.VMEM((REACH * BLOCK, BLOCK), F32)],
        compiler_params=pltpu.CompilerParams(vmem_limit_bytes=VMEM_LIMIT),
        name="attend",
    )(queries, keyval, values_t, code_col, doc_row)


def norm_back_rows(x, grad, gain):
    mean = jnp.mean(x, axis=-1, keepdims=True)
    center = x - mean
    scale = lax.rsqrt(jnp.mean(center * center, axis=-1, keepdims=True) + EPS)
    xhat = center * scale
    e = grad * gain
    weighted = grad * xhat
    d_in = scale * (
        e - jnp.mean(e, axis=-1, keepdims=True) - xhat * jnp.mean(e * xhat, axis=-1, keepdims=True)
    )
    return d_in, weighted


def fold_rows(x):
    return jnp.sum(x.reshape(-1, 8, x.shape[-1]), axis=0)


def mlp_attend_back_kernel(
    heads,
    dh_hbm, w_up_hbm, w_out_hbm, mid_hbm, cot_hbm, q_hbm,
    kv_ref, kt_ref, code_ref, doc_ref, lse_ref, gain_ref,
    d_mid_hbm, d_branch_hbm, dq_hbm, dkv_ref, sums_ref,
    w_up, w_out, dh, mid, cot, q, d_branch, d_mixed, dq, bias_ref, load_sem, out_sem, *line_refs,
):
    line = LineSum(line_refs)
    seq, width = line.part.shape
    hd = kt_ref.shape[0]
    chunks = seq // BLOCK
    pieces = BLOCK // PIECE
    count = REACH * BLOCK
    scale = 1.0 / math.sqrt(hd)

    def load(i, src, dst):
        return pltpu.make_async_copy(src, dst, load_sem.at[i])

    def load_dh(c):
        return load(2, dh_hbm.at[rows_at(c * BLOCK, BLOCK)], dh)

    def load_chunk(c):
        at = rows_at(c * BLOCK, BLOCK)
        return [
            load(3, mid_hbm.at[at], mid),
            load(4, cot_hbm.at[at], cot),
            load(5, q_hbm.at[at], q),
        ]

    def store(i, src, dst, c):
        return pltpu.make_async_copy(src, dst.at[rows_at(c * BLOCK, BLOCK)], out_sem.at[i])

    def stores(c, which=(0, 1, 2)):
        pairs = ((mid, d_mid_hbm), (d_branch, d_branch_hbm), (dq, dq_hbm))
        return [store(i, *pairs[i], c) for i in which]

    load(0, w_up_hbm, w_up).start()
    load_dh(0).start()
    load(1, w_out_hbm, w_out).start()
    line.greet()
    dkv_ref[...] = jnp.zeros_like(dkv_ref)
    sums_ref[...] = jnp.zeros_like(sums_ref)

    def produce(c):
        at = rows_at(c * BLOCK, BLOCK)
        load_dh(c).wait()

        def cols(n, carry):
            there = rows_at(n * COLS, COLS)
            line.part[at, there] = dot_t(dh[...], w_up[there, :])
            return carry

        lax.fori_loop(0, width // COLS, cols, 0)

        @pl.when(c + 1 < chunks)
        def _():
            load_dh(c + 1).start()

    def norm_step(c, half):
        def strip(i, carry):
            row = half * (BLOCK // 2) + i * STRIP
            at = rows_at(row, STRIP)
            grad = line.total[rows_at(c * BLOCK + row, STRIP), :]
            d_in, weighted = norm_back_rows(mid[at, :], grad, gain_ref[...])
            d_mid = cot[at, :].astype(F32) + d_in
            low = d_mid.astype(BF16)
            mid[at, :] = d_mid
            d_branch[at, :] = low
            sums_ref[0] += fold_rows(weighted)
            sums_ref[1] += fold_rows(grad)
            sums_ref[2] += fold_rows(low.astype(F32))
            return carry

        lax.fori_loop(0, BLOCK // 2 // STRIP, strip, 0)

    def mixed_step(c):
        def cols(n, carry):
            there = rows_at(n * COLS, COLS)
            d_mixed[:, there] = dot_t(d_branch[...], w_out[there, :]).astype(BF16)
            return carry

        lax.fori_loop(0, width // COLS, cols, 0)
        keys = pl.ds(pl.multiple_of(c * BLOCK, BLOCK), count)
        bias_ref[...] = mask_bias(
            code_ref[keys, :], doc_ref[:, rows_at(c * BLOCK, BLOCK)],
            (c - REACH + 1) * BLOCK, count, c * BLOCK, BLOCK,
        )

    def heads_step(c, g):
        keys = pl.ds(pl.multiple_of(c * BLOCK, BLOCK), count)
        queries = rows_at(c * BLOCK, BLOCK)
        dk = jnp.zeros((count, hd), F32)
        dv = jnp.zeros((count, hd), F32)
        for u in range(GROUP):
            h = g * GROUP + u
            cols = rows_at(h * hd, hd)
            qh = q[:, cols]
            dm = d_mixed[:, cols]
            s = dot_t(kv_ref[keys, pl.ds(0, hd)], qh) * scale + bias_ref[...]
            probs = jnp.exp(s - lse_ref[pl.ds(h, 1), queries])
            d_probs = dot_t(kv_ref[keys, pl.ds(hd, hd)], dm)
            t = probs * d_probs
            inner = jnp.sum(t, axis=0, keepdims=True)
            ds = (t - probs * inner).astype(BF16)
            dqh = project(kt_ref[:, keys], ds) * scale
            dq[:, cols] = dqh.T.astype(BF16)
            dk = dk + project(ds, qh)
            dv = dv + project(probs.astype(BF16), dm)
        dkv_ref[keys, pl.ds(0, hd)] += dk * scale
        dkv_ref[keys, pl.ds(hd, hd)] += dv

    load(0, w_up_hbm, w_up).wait()
    produce(0)
    line.meet()
    for k in range(3):
        line.tick(k)
    load(1, w_out_hbm, w_out).wait()

    def cycle(u, carry):
        c = u - 1
        base = u * pieces + 3

        @pl.when(u >= 2)
        def _():
            for i in stores(u - 2):
                i.wait()

        @pl.when(u >= 1)
        def _():
            for i in load_chunk(c):
                i.start()

        line.tick(base)

        @pl.when(u + 1 < chunks)
        def _():
            produce(u + 1)

        line.tick(base + 1)

        @pl.when(u >= 1)
        def _():
            for i in load_chunk(c):
                i.wait()
            norm_step(c, 0)

        line.tick(base + 2)

        @pl.when(u >= 1)
        def _():
            norm_step(c, 1)
            for i in stores(c, (0, 1)):
                i.start()

        line.tick(base + 3)

        @pl.when(u >= 1)
        def _():
            mixed_step(c)

        def some_heads(g, carry):
            line.tick(base + 4 + g)

            @pl.when(u >= 1)
            def _():
                heads_step(c, g)

            return carry

        lax.fori_loop(0, heads // GROUP, some_heads, 0)

        @pl.when(u >= 1)
        def _():
            stores(c, (2,))[0].start()

        return carry

    lax.fori_loop(0, chunks + 1, cycle, 0)
    for i in stores(chunks - 1):
        i.wait()
    line.finish()


def padded_keys(keyval):
    return jnp.pad(keyval, (((REACH - 1) * BLOCK, 0), (0, 0)))


def mlp_attend_back(d_hidden, w_up, w_out, middle, cotangent, queries, keyval, codes, docs, lse, gain):
    seq, width = queries.shape
    hd = keyval.shape[1] // 2
    heads = width // hd
    front = (REACH - 1) * BLOCK
    kv = padded_keys(keyval)
    code_col = jnp.pad(codes, (front, 0), constant_values=-2).reshape(-1, 1)
    vmem = pl.BlockSpec(memory_space=pltpu.VMEM)
    dma = pltpu.SemaphoreType.DMA
    block = lambda dtype: pltpu.VMEM((BLOCK, width), dtype)
    d_middle, d_branch, d_queries, d_kv, sums = pl.pallas_call(
        functools.partial(mlp_attend_back_kernel, heads),
        out_shape=(
            jax.ShapeDtypeStruct((seq, width), F32),
            jax.ShapeDtypeStruct((seq, width), BF16),
            jax.ShapeDtypeStruct((seq, width), BF16),
            jax.ShapeDtypeStruct(kv.shape, F32),
            jax.ShapeDtypeStruct((3, 8, width), F32),
        ),
        in_specs=[HBM] * 6 + [vmem] * 6,
        out_specs=(HBM, HBM, HBM, vmem, vmem),
        scratch_shapes=[
            pltpu.VMEM(w_up.shape, BF16),
            pltpu.VMEM(w_out.shape, BF16),
            pltpu.VMEM((BLOCK, d_hidden.shape[1]), BF16),
            block(F32),
            block(BF16),
            block(BF16),
            block(BF16),
            block(BF16),
            block(BF16),
            pltpu.VMEM((REACH * BLOCK, BLOCK), F32),
            dma((6,)),
            dma((3,)),
        ]
        + LineSum.scratch(seq, width),
        compiler_params=pltpu.CompilerParams(
            collective_id=1, has_side_effects=True, vmem_limit_bytes=VMEM_LIMIT
        ),
        cost_estimate=pl.CostEstimate(
            flops=200 * 10**9, bytes_accessed=2**25, transcendentals=0
        ),
        name="mlp_attend_back",
    )(
        d_hidden, w_up, w_out, middle, cotangent, queries,
        kv, kv[:, :hd].T, code_col, docs.reshape(1, seq), lse, gain.reshape(1, width),
    )
    return d_middle, d_branch, d_queries, d_kv[front:], jnp.sum(sums, axis=1)


def feed_kernel(
    rounds,
    acts_hbm, w_down_hbm, mid_hbm, dq_hbm, w_q_hbm, in_hbm, d_mid_hbm,
    dkv_ref, w_kv_ref, gain_ref, bias_ref,
    out_hbm, in_grad_hbm, sums_ref,
    w_down, w_q, acts, mid, dq, xs, d_mid, spread, low, in_grad, trade, trade_in,
    load_sem, out_sem, t_send, t_recv, *line_refs,
):
    line = LineSum(line_refs)
    seq, width = line.part.shape
    chunks = seq // BLOCK
    pieces = BLOCK // PIECE
    planes, _, cols_q = w_q.shape
    m = lax.axis_index("mp")
    d = lax.axis_index("dp")
    peers = [{"dp": flip_bit(d, 1 << r)} for r in range(rounds)]

    def load(i, src, dst):
        return pltpu.make_async_copy(src, dst, load_sem.at[i])

    def load_feed(c):
        at = rows_at(c * BLOCK, BLOCK)
        return [load(2, acts_hbm.at[at], acts), load(3, mid_hbm.at[at], mid)]

    def load_grad(c):
        at = rows_at(c * BLOCK, BLOCK)
        return [
            load(4, dq_hbm.at[at], dq),
            load(5, in_hbm.at[at], xs),
            load(6, d_mid_hbm.at[at], d_mid),
        ]

    def store(i, src, dst, c):
        return pltpu.make_async_copy(src, dst.at[rows_at(c * BLOCK, BLOCK)], out_sem.at[i])

    load(0, w_down_hbm, w_down).start()
    for i in load_feed(0):
        i.start()
    load(1, w_q_hbm, w_q).start()
    line.greet(peers)
    sums_ref[...] = jnp.zeros_like(sums_ref)

    def produce(c):
        at = rows_at(c * BLOCK, BLOCK)
        for i in load_feed(c):
            i.wait()

        def cols(n, carry):
            there = rows_at(n * COLS, COLS)
            line.part[at, there] = project(acts[...], w_down[:, there])
            return carry

        lax.fori_loop(0, width // COLS, cols, 0)

        @pl.when(m == 0)
        def _():
            line.part[at, :] += mid[...]

        @pl.when(c + 1 < chunks)
        def _():
            for i in load_feed(c + 1):
                i.start()

    def output_step(c):
        def strip(i, carry):
            at = rows_at(i * STRIP, STRIP)
            there = rows_at(c * BLOCK + i * STRIP, STRIP)
            low[at, :] = (line.total[there, :] + bias_ref[...]).astype(BF16)
            return carry

        lax.fori_loop(0, BLOCK // STRIP, strip, 0)

    def spread_step(c):
        rows = rows_at(c * BLOCK, BLOCK)

        def cols(n, carry):
            there = rows_at(n * COLS, COLS)
            total = dot_t(dkv_ref[rows, :], w_kv_ref[there, :])
            for i in range(planes):
                total = total + dot_t(dq[:, pl.ds(i * cols_q, cols_q)], w_q[i, there, :])
            spread[:, there] = total
            return carry

        lax.fori_loop(0, width // COLS, cols, 0)

    def norm_step(c, half):
        def strip(i, carry):
            at = rows_at(half * (BLOCK // 2) + i * STRIP, STRIP)
            grad = spread[at, :]
            d_in, weighted = norm_back_rows(xs[at, :].astype(F32), grad, gain_ref[...])
            in_grad[at, :] = (d_mid[at, :] + d_in).astype(BF16)
            sums_ref[0] += fold_rows(weighted)
            sums_ref[1] += fold_rows(grad)
            return carry

        lax.fori_loop(0, BLOCK // 2 // STRIP, strip, 0)

    def swap(r):
        return pltpu.make_async_remote_copy(
            trade.at[r], trade_in.at[r], t_send.at[r], t_recv.at[r],
            device_id=peers[r], device_id_type=MESH,
        )

    load(0, w_down_hbm, w_down).wait()
    produce(0)
    line.meet(peers)
    for k in range(3):
        line.tick(k)
    load(1, w_q_hbm, w_q).wait()

    def cycle(u, carry):
        c = u - 1
        base = u * pieces + 3

        @pl.when(u < chunks)
        def _():
            for i in load_grad(u):
                i.start()

        line.tick(base)

        @pl.when(u + 1 < chunks)
        def _():
            produce(u + 1)

        line.tick(base + 1)

        @pl.when(u >= 1)
        def _():
            @pl.when(u >= 2)
            def _():
                store(0, low, out_hbm, u - 2).wait()

            output_step(c)
            store(0, low, out_hbm, c).start()

        line.tick(base + 2)

        @pl.when(u < chunks)
        def _():
            for i in load_grad(u):
                i.wait()
            spread_step(u)

        line.tick(base + 3)
        line.tick(base + 4)

        @pl.when(u < chunks)
        def _():
            @pl.when(u >= 1)
            def _():
                store(1, in_grad, in_grad_hbm, u - 1).wait()

            norm_step(u, 0)

        line.tick(base + 5)
        line.tick(base + 6)

        @pl.when(u < chunks)
        def _():
            norm_step(u, 1)
            store(1, in_grad, in_grad_hbm, u).start()

        line.tick(base + 7)

        @pl.when(u == chunks - 1)
        def _():
            trade[0, 0:8] = sums_ref[0]
            trade[0, 8:16] = sums_ref[1]
            for r in range(rounds):
                swap(r).start()
                swap(r).wait()
                trade[r + 1] = trade[r] + trade_in[r]
            sums_ref[0] = trade[rounds, 0:8]
            sums_ref[1] = trade[rounds, 8:16]

        return carry

    lax.fori_loop(0, chunks + 1, cycle, 0)
    store(0, low, out_hbm, chunks - 1).wait()
    store(1, in_grad, in_grad_hbm, chunks - 1).wait()
    line.finish()


def feed_and_input_grad(
    acts, w_down, middle, b_down, d_queries, all_query, d_keyval, w_keyval, inputs, d_middle, gain
):
    seq, width = inputs.shape
    rounds = (lax.axis_size("dp") - 1).bit_length()
    vmem = pl.BlockSpec(memory_space=pltpu.VMEM)
    dma = pltpu.SemaphoreType.DMA
    block = lambda dtype: pltpu.VMEM((BLOCK, width), dtype)
    outputs, input_grad, sums = pl.pallas_call(
        functools.partial(feed_kernel, rounds),
        out_shape=(
            jax.ShapeDtypeStruct((seq, width), BF16),
            jax.ShapeDtypeStruct((seq, width), BF16),
            jax.ShapeDtypeStruct((2, 8, width), F32),
        ),
        in_specs=[HBM] * 7 + [vmem] * 4,
        out_specs=(HBM, HBM, vmem),
        scratch_shapes=[
            pltpu.VMEM(w_down.shape, BF16),
            pltpu.VMEM(all_query.shape, BF16),
            pltpu.VMEM((BLOCK, acts.shape[1]), BF16),
            block(F32),
            block(BF16),
            block(BF16),
            block(F32),
            block(F32),
            block(BF16),
            block(BF16),
            pltpu.VMEM((rounds + 1, 16, width), F32),
            pltpu.VMEM((rounds, 16, width), F32),
            dma((7,)),
            dma((2,)),
            dma((rounds,)),
            dma((rounds,)),
        ]
        + LineSum.scratch(seq, width),
        compiler_params=pltpu.CompilerParams(
            collective_id=2, has_side_effects=True, vmem_limit_bytes=VMEM_LIMIT
        ),
        cost_estimate=pl.CostEstimate(
            flops=200 * 10**9, bytes_accessed=2**25, transcendentals=0
        ),
        name="feed_and_input_grad",
    )(
        acts, w_down, middle, d_queries, all_query, inputs, d_middle,
        d_keyval, w_keyval, gain.reshape(1, width), b_down.reshape(1, width),
    )
    return outputs, input_grad, jnp.sum(sums, axis=1)


def sum_packed(table, vectors):
    width = table.shape[1]
    rows = [jnp.pad(v, (0, width - v.shape[0])).reshape(1, width) for v in vectors]
    total = lax.psum(jnp.concatenate([table] + rows, 0), "dp")
    head = table.shape[0]
    return total[:head], [total[head + i, : v.shape[0]] for i, v in enumerate(vectors)]


def shards(
    inputs,
    doc_ids,
    pad_mask,
    attn_gain,
    attn_shift,
    w_query,
    b_query,
    w_keyval,
    b_value,
    w_out,
    b_out,
    mlp_gain,
    mlp_shift,
    w_up,
    b_up,
    w_down,
    b_down,
    cotangent,
):
    seq = doc_ids.shape[1]
    hd = b_value.shape[0]
    width = inputs.shape[1]
    own_cols = w_query.shape[1]
    own = lax.axis_index("mp") * own_cols
    inputs_f = inputs.astype(F32)
    bias_full = jnp.concatenate([jnp.zeros((hd,), F32), b_value])
    docs = doc_ids[0]
    codes = jnp.where(pad_mask[0] == 1, docs, -1)

    all_query, all_out, normed_attn, queries, mixed, keyval, lse = attention_front(
        inputs, w_query, b_query, w_keyval, bias_full, w_out, attn_gain, attn_shift, codes, docs
    )
    middle = inputs_f + project(mixed, all_out) + b_out
    normed_mlp = norm_rows(middle, mlp_gain, mlp_shift).astype(BF16)
    hidden = project(normed_mlp, w_up) + b_up
    acts = jax.nn.gelu(hidden, approximate=True).astype(BF16)
    grad_w_down = jnp.einsum("tf,td->fd", acts, cotangent, preferred_element_type=F32)
    grad_b_down = jnp.sum(cotangent.astype(F32), axis=0)
    d_acts = jnp.einsum("td,fd->tf", cotangent, w_down, preferred_element_type=F32)
    _, gelu_pull = jax.vjp(functools.partial(jax.nn.gelu, approximate=True), hidden)
    d_hidden = gelu_pull(d_acts)[0].astype(BF16)
    grad_b_up = jnp.sum(d_hidden.astype(F32), axis=0)
    grad_w_up = jnp.einsum("td,tf->df", normed_mlp, d_hidden, preferred_element_type=F32)
    d_hidden, grad_w_up, grad_w_down = lax.optimization_barrier((d_hidden, grad_w_up, grad_w_down))
    grad_w_up = lax.psum_scatter(grad_w_up, "dp", scatter_dimension=0, tiled=True)
    grad_w_down = lax.psum_scatter(grad_w_down, "dp", scatter_dimension=1, tiled=True)

    d_middle, d_branch, d_queries, d_keyval_sum, sums = mlp_attend_back(
        d_hidden, w_up, all_out, middle, cotangent, queries, keyval, codes, docs, lse, mlp_gain
    )
    d_keyval_sum, grad_w_down, grad_w_up = lax.optimization_barrier(
        (d_keyval_sum, grad_w_down, grad_w_up)
    )
    grad_mlp_gain, grad_mlp_shift, grad_b_out = sums[0], sums[1], sums[2]
    own_mixed = lax.dynamic_slice_in_dim(mixed, own, own_cols, 1)
    grad_w_out = jnp.einsum("tq,td->qd", own_mixed, d_branch, preferred_element_type=F32)
    grad_b_value = jnp.sum(d_keyval_sum[:, hd:], axis=0)
    d_keyval = d_keyval_sum.astype(BF16)
    own_d_queries = lax.dynamic_slice_in_dim(d_queries, own, own_cols, 1)
    grad_b_query = jnp.sum(own_d_queries.astype(F32), axis=0)
    grad_w_query = jnp.einsum("td,tq->dq", normed_attn, own_d_queries, preferred_element_type=F32)
    grad_w_keyval = jnp.einsum("tk,td->kd", d_keyval, normed_attn, preferred_element_type=F32)
    small = (
        grad_b_query,
        grad_b_value,
        grad_b_out,
        grad_mlp_gain,
        grad_mlp_shift,
        grad_b_up,
        grad_b_down,
    )
    acts, small, grad_w_keyval, grad_w_out, grad_w_query = lax.optimization_barrier(
        (acts, small, grad_w_keyval, grad_w_out, grad_w_query)
    )
    grad_w_out = lax.psum_scatter(grad_w_out, "dp", scatter_dimension=1, tiled=True)
    grad_w_query = lax.psum_scatter(grad_w_query, "dp", scatter_dimension=0, tiled=True)
    grad_w_keyval, small = sum_packed(grad_w_keyval, small)
    grad_w_keyval = grad_w_keyval.T
    grad_b_query, grad_b_value, grad_b_out, grad_mlp_gain, grad_mlp_shift, grad_b_up, grad_b_down = small
    outputs, input_grad, sums = feed_and_input_grad(
        acts, w_down, middle, b_down, d_queries, all_query, d_keyval, w_keyval, inputs, d_middle, attn_gain
    )
    grad_attn_gain, grad_attn_shift = sums[0], sums[1]
    return (
        outputs,
        input_grad,
        grad_attn_gain,
        grad_attn_shift,
        grad_w_query,
        grad_b_query,
        grad_w_keyval,
        grad_b_value,
        grad_w_out,
        grad_b_out,
        grad_mlp_gain,
        grad_mlp_shift,
        grad_w_up,
        grad_b_up,
        grad_w_down,
        grad_b_down,
    )


def solution(mesh):
    return jax.shard_map(
        shards,
        mesh=mesh,
        in_specs=(
            P("dp", None),
            P("dp", None),
            P("dp", None),
            P(),
            P(),
            P(None, "mp"),
            P("mp"),
            P(),
            P(),
            P("mp", None),
            P(),
            P(),
            P(),
            P(None, "mp"),
            P("mp"),
            P("mp", None),
            P(),
            P("dp", None),
        ),
        out_specs=(
            P("dp", None),
            P("dp", None),
            P(),
            P(),
            P("dp", "mp"),
            P("mp"),
            P(),
            P(),
            P("mp", "dp"),
            P(),
            P(),
            P(),
            P("dp", "mp"),
            P("mp"),
            P("mp", "dp"),
            P(),
        ),
        check_vma=False,
    )
```

time: 1820 us -> 759 us (0.42)
  waiting for transfers between devices: 1470 us -> 1.79 us
  Pallas kernels: 0 us -> 606 us
  matrix products: 192 us -> 93.8 us
  other arithmetic: 73.1 us -> 8.17 us
  blocking collectives: 25.9 us -> 0 us
    psum x4 -> x1, waiting for transfers between devices: 1180 us -> 0.01 us  [sum_packed(): total = lax.psum(jnp.concatenate([table] + rows, 0), 'dp')]
    pallas_call x0 -> x3, Pallas kernels: none -> 606 us  [the longest x1 236 us: mlp_attend_back(): pl.pallas_call(functools.partial(mlp_attend_back_kernel, heads), out_shap...]
    reduce_scatter x1, waiting for transfers between devices: 121 us -> 0.01 us  [shards(): lax.psum_scatter(grad_w_down, 'dp', scatter_dimension=1, tiled=True)]
    reduce_scatter x1, waiting for transfers between devices: 120 us -> 0.01 us  [shards(): lax.psum_scatter(grad_w_up, 'dp', scatter_dimension=0, tiled=True)]
    dot_general x29 -> x8, matrix products: 192 us -> 93.8 us  [the longest x2 25.3 us: project(): return jnp.dot(left, right, preferred_element_type=F32)]
    reduce_scatter x1, waiting for transfers between devices: 46 us -> 0.01 us  [shards(): lax.psum_scatter(grad_w_query, 'dp', scatter_dimension=0, tiled=True)]
    reduce_sum x11 -> x5, other arithmetic: 47.1 us -> 6.44 us  [the longest x1 2.9 us: shards(): grad_b_down = jnp.sum(cotangent.astype(F32), axis=0)]
    psum x1 -> x0, blocking collectives: 25.9 us -> none  [shards(): lax.psum((grad_attn_gain, grad_attn_shift, grad_b_query, grad_w_keyval, g...]
  transfers between devices with their start and end apart: 8 -> 5, of which waited for: 7 -> 0; matrix products, arithmetic and copies ran while one was open for 6% -> 4% of each run, Pallas kernels for 0% -> 60%
where the time goes in v1:
time: 759 us; the launch traced here: 750 us
  Pallas kernels  606 us (80%)
  matrix products  93.8 us (12%)
  local copies, waits for them, and re-layouts  26.2 us (3%)
  between operations  14.5 us (2%)
  other arithmetic  8.17 us (1%)
    pallas_call x1, Pallas kernels, mlp_attend_back(): pl.pallas_call(functools.partial(mlp_attend_back_kernel, heads), out_shap...  236 us
    pallas_call x1, Pallas kernels, feed_and_input_grad(): pl.pallas_call(functools.partial(feed_kernel, rounds), out_shape=(jax.Sha...  213 us
    pallas_call x1, Pallas kernels, attention_front(): pl.pallas_call(functools.partial(front_kernel, heads), out_shape=(shape(f...  157 us
    dot_general x2, matrix products, project(): return jnp.dot(left, right, preferred_element_type=F32)  25.3 us
    dot_general x1, matrix products, shards(): jnp.einsum('td,fd->tf', cotangent, w_down, preferred_element_type=F32)  21.1 us
  transfers between devices with their start and end apart: 5, of which 0 were waited for; matrix products, arithmetic and copies ran while one was open for 4% of the time, Pallas kernels for 60%

profile of v1, /device:TPU:0, one launch (start us, length us, event | category | flops | bytes accessed | tf_op | source)
XLA Modules:
  0.0 750.4 jit_solution(8061409613410849657)
XLA Ops:
  7.2 0.0 copy-start.6
  7.2 0.0 reduce-scatter.5.cloned.1.call-start
  7.2 0.7 compare_select_fusion
  7.9 1.0 copy.37.code_ref
  9.0 1.2 concatenate.6
  10.2 156.9 %attention_front.1 = (bf16[4,8,256,512]{3,2,1,0:T(8,128)(2,1)}, bf16[4,8,64,2048]{3,2,1,0:T(8,128)(2,1)}, bf16[1024,2048]{1,0:T(8,128)(2,1)}, bf16[1024,2048]{1,...) custom-call(bf16[8,256,512]{2,1,0:T(8,128)(2,1)} %bitcast.48, ...), custom_call_target="tpu_custom_call" | custom-call | tf_op jit(solution)/shard_map/attention_front/pallas_call | solution.py:356
  167.1 0.0 slice-start
  167.1 0.0 copy-done.6
  167.1 0.0 slice-start.1
  167.1 14.0 %fusion.19 = (f32[1024]{0:T(1024)S(1)}, f32[1024,2048]{1,0:T(8,128)S(1)}) fusion(f32[2048]{0:T(1024)S(1)} %copy-done.6, bf16[1024,2048]{1,0:T(8,128)(2,1)} %get-tuple-element.48, bf16[2048,2048]{1,0:T(8,128)(2,1)} %bitcast.72, bf16[1024,2048]{1,0:T(8,128)(2,1)} %in_hbm.3), kind=kOutput, calls=%fused_computation.34 | convolution fusion | flops 8598322176 | bytes 25178112 | tf_op jit(solution)/shard_map/dot_general | solution.py:26
  181.1 0.0 copy-start
  181.1 0.0 copy-start.8
  181.1 0.0 copy-start.9
  181.1 1.0 multiply_reduce_fusion
  182.1 0.0 slice-done
  182.1 0.0 slice-done.1
  182.1 0.0 copy-done.8
  182.1 0.0 copy-done.9
  182.1 0.0 copy-start.1
  182.2 0.0 copy-start.7
  182.2 11.3 %fusion.14 = f32[1024,2048]{1,0:T(8,128)} fusion(bf16[2048,2048]{1,0:T(8,128)(2,1)S(1)} %bitcast.70, f32[1024,2048]{1,0:T(8,128)S(1)} %get-tuple-element.126.mid_hbm, f32[2048]{0:T(1024)S(1)} %copy-done.8, f32[2048]{0:T(1024)S(1)} %copy-done.9, f32[1024]{0:T(1024)S(1)} %add_rsqrt_fusion, f32[1024]{0:T(1024)S(1)} %broadcast_multiply_fusion), kind=kOutput, calls=%fused_computation.30 | convolution fusion | flops 8600420352 | bytes 25190400 | tf_op jit(solution)/shard_map/dot_general | solution.py:26
  193.5 0.0 copy-done.7
  193.5 21.1 %convert_reduce_fusion.1 = (f32[2048]{0:T(1024)}, bf16[1024,2048]{1,0:T(8,128)(2,1)}, bf16[1024,2048]{1,0:T(8,128)(2,1)}) fusion(f32[1024,2048]{1,0:T(8,128)} %fusion.14, f32[2048]{0:T(1024)S(1)} %copy-done.7, bf16[1024,2048]{1,0:T(8,128)(2,1)S(1)} %copy-done.1, bf16[2048,2048]{1,0:T(8,128)(2,1)} %w_down_hbm.1), kind=kOutput, calls=%fused_computation.10 | convolution fusion | flops 8642361344 | bytes 29376512 | tf_op jit(solution)/shard_map/td,fd->tf/dot_general | solution.py:1119
  214.7 14.9 %fusion.13 = f32[2048,2048]{1,0:T(8,128)} fusion(bf16[1024,2048]{1,0:T(8,128)(2,1)} %get-tuple-element.50.dh_hbm, f32[1024,2048]{1,0:T(8,128)S(1)} %get-tuple-element.126.mid_hbm, f32[2048]{0:T(1024)S(1)} %copy-done.8, f32[2048]{0:T(1024)S(1)} %copy-done.9, f32[1024]{0:T(1024)S(1)} %add_rsqrt_fusion, f32[1024]{0:T(1024)S(1)} %broadcast_multiply_fusion), kind=kOutput, calls=%fused_computation.29 | convolution fusion | flops 8600420352 | bytes 29384704 | tf_op jit(solution)/shard_map/td,tf->df/dot_general | solution.py:1123
  229.6 15.2 %fusion.20 = f32[2048,2048]{1,0:T(8,128)} fusion(bf16[1024,2048]{1,0:T(8,128)(2,1)} %get-tuple-element.62.acts_hbm, bf16[1024,2048]{1,0:T(8,128)(2,1)} %cot_hbm.1), kind=kOutput, calls=%fused_computation.35 | convolution fusion | flops 8589934592 | bytes 25165824 | tf_op jit(solution)/shard_map/tf,td->fd/dot_general | solution.py:1117
  244.8 0.0 reduce-scatter.5.cloned.1.call-update
  244.8 0.0 reduce-scatter.7.cloned.1.call-start
  244.8 0.7 reduce-scatter.7.cloned.1.call-update
  245.5 0.0 all-reduce.7.cloned.1.call-start
  245.6 0.2 copy-done.4
  245.8 0.2 copy.38
  246.0 0.2 copy.42
  246.3 1.1 reshape.147.code_ref
  247.4 0.9 pad.17.clone.kv_ref
  248.3 0.8 slice_bitcast_fusion.1.kt_ref
  249.1 235.8 %mlp_attend_back.1 = (f32[1024,2048]{1,0:T(8,128)}, bf16[1024,2048]{1,0:T(8,128)(2,1)}, bf16[1024,2048]{1,0:T(8,128)(2,1)}, f32[1536,256]{1,0:T(8,128)}, f32[3,8,2048]{2,1,0:T(8,128)}) custom-call(bf16[1024,2048]{1,0:T(8,128)(2,1)} %get-tuple-element.50.dh_hbm, bf16[2048,2048]{1,0:T(8,128)(2,1)} %w_up_hbm.1, bf16[2048,2048]{1,0:T(8,128)(2,1)} %bitcast.73, ...), custom_call_target="tpu_custom_call" | custom-call | flops 199999995904 | bytes 33554432 | tf_op jit(solution)/shard_map/mlp_attend_back/pallas_call | solution.py:798
  484.9 1.3 slice.49
  486.2 1.0 reduce_sum.76
  487.2 1.4 convert_reduce_fusion.2
  488.6 2.9 convert_reduce_fusion
  491.5 6.9 fusion.9
  498.4 6.8 fusion.7
  505.3 0.1 convert_element_type.37.dkv_ref
  505.3 0.0 copy-start.3
  505.3 0.1 slice_reduce_fusion
  505.5 3.5 fusion.21
  509.0 0.0 copy-done.5
  509.0 3.8 concatenate.7
  512.8 0.0 all-reduce.7.cloned.1.call-update
  512.8 0.0 reduce-scatter.11.cloned.1.call-start
  512.9 0.5 reduce-scatter.11.cloned.1.call-update
  513.4 0.0 reduce-scatter.9.cloned.1.call-start
  513.5 0.5 reduce-scatter.9.cloned.1.call-update
  514.0 213.2 %feed_and_input_grad.1 = (bf16[1024,2048]{1,0:T(8,128)(2,1)}, bf16[1024,2048]{1,0:T(8,128)(2,1)}, f32[2,8,2048]{2,1,0:T(8,128)}) custom-call(bf16[1024,2048]{1,0:T(8,128)(2,1)} %get-tuple-element.62.acts_hbm, bf16[2048,2048]{1,0:T(8,128)(2,1)} %w_down_hbm.1, f32[1024,2048]{1,0:T(8,128)} %copy-done, bf16[1024,2048]{1,0:T(8,128)(2,1)} %get-tuple-element.54.dq_hbm, ...), custom_call_target="tpu_custom_call" | custom-call | flops 199999995904 | bytes 33554432 | tf_op jit(solution)/shard_map/feed_and_input_grad/pallas_call | solution.py:1030
  727.2 1.0 reduce_sum.79
  728.2 0.6 fusion.18
  728.8 1.7 slice_bitcast_fusion
  730.5 1.8 copy.41
  732.3 1.3 slice.69
  733.6 1.2 slice_bitcast_fusion.2
  734.8 1.7 fusion.16
  736.5 0.0 reduce-scatter.9.cloned.1.call-done
  736.5 4.9 copy.46
  741.5 2.0 copy.47
  (18 shorter events, 0.1 us)
Async XLA Ops:
  7.2 159.9 %copy-start.6 = (f32[2048]{0:T(1024)S(1)}, f32[2048]{0:T(1024)}, u32[]{:S(2)}) copy-start(f32[2048]{0:T(1024)} %param.28) | copy-start | bytes 24580
  7.2 498.1 %reduce-scatter.5.cloned.1.call-start = ((), (), s32[]{:S(2)}) async-start(), calls=%async_computation.4 | async-start | bytes 18874368 | tf_op jit(solution)/shard_map/reduce_scatter | solution.py:1126
  167.1 15.0 %slice-start = ((s8[8388608]{0:T(1024)(128)(4,1)}), s8[4194304]{0:T(1024)(128)(4,1)S(1)}, s32[]{:S(2)}) async-start(s8[8388608]{0:T(1024)(128)(4,1)} %bitcast.69), calls=%async_computation.9 | async-start | bytes 8388608
  167.1 15.0 %slice-start.1 = ((s8[8388608]{0:T(1024)(128)(4,1)}), s8[4194304]{0:T(1024)(128)(4,1)S(1)}, s32[]{:S(2)}) async-start(s8[8388608]{0:T(1024)(128)(4,1)} %bitcast.69), calls=%async_computation.10 | async-start | bytes 8388608
  181.1 33.6 %copy-start = (f32[1024,2048]{1,0:T(8,128)}, f32[1024,2048]{1,0:T(8,128)S(1)}, u32[]{:S(2)}) copy-start(f32[1024,2048]{1,0:T(8,128)S(1)} %get-tuple-element.126.mid_hbm) | copy-start | bytes 25165828
  181.1 1.0 copy-start.8
  181.1 1.0 copy-start.9
  182.1 11.4 %copy-start.1 = (bf16[1024,2048]{1,0:T(8,128)(2,1)S(1)}, bf16[1024,2048]{1,0:T(8,128)(2,1)}, u32[]{:S(2)}) copy-start(bf16[1024,2048]{1,0:T(8,128)(2,1)} %cot_hbm.1) | copy-start | bytes 12582916
  182.2 11.4 %copy-start.7 = (f32[2048]{0:T(1024)S(1)}, f32[2048]{0:T(1024)}, u32[]{:S(2)}) copy-start(f32[2048]{0:T(1024)} %param.32) | copy-start | bytes 24580
  244.8 1.0 copy-start.4
  244.8 260.5 %reduce-scatter.7.cloned.1.call-start = ((), (), s32[]{:S(2)}) async-start(), calls=%async_computation.5 | async-start | bytes 18874368 | tf_op jit(solution)/shard_map/reduce_scatter | solution.py:1125
  245.5 483.2 %all-reduce.7.cloned.1.call-start = ((), (), s32[]{:S(2)}) async-start(), calls=%async_computation.7 | async-start | bytes 4325376 | tf_op jit(solution)/shard_map/psum | solution.py:1075
  498.4 10.6 %copy-start.5 = (f32[2048]{0:T(1024)S(1)}, f32[2048]{0:T(1024)}, u32[]{:S(2)}) copy-start(f32[2048]{0:T(1024)} %get-tuple-element.75) | copy-start | bytes 24580
  505.3 8.1 %copy-start.3 = (bf16[1024,256]{1,0:T(8,128)(2,1)}, bf16[1024,256]{1,0:T(8,128)(2,1)S(1)}, u32[]{:S(2)}) copy-start(bf16[1024,256]{1,0:T(8,128)(2,1)S(1)} %convert_element_type.37.dkv_ref) | copy-start | bytes 1572868
  512.8 223.7 %reduce-scatter.11.cloned.1.call-start = ((), (), s32[]{:S(2)}) async-start(), calls=%async_computation.8 | async-start | bytes 4718592 | tf_op jit(solution)/shard_map/reduce_scatter | solution.py:1155
  513.4 223.1 %reduce-scatter.9.cloned.1.call-start = ((), (), s32[]{:S(2)}) async-start(), calls=%async_computation.6 | async-start | bytes 4718592 | tf_op jit(solution)/shard_map/reduce_scatter | solution.py:1156
  736.5 5.0 copy-start.2
Sparse Core Ops, SparseCore 0:
  244.9 124.1 reduce-scatter.4
  373.3 116.0 reduce-scatter.6
  512.9 60.9 all-reduce.6
  577.7 50.7 reduce-scatter.10
  632.7 51.3 reduce-scatter.8

commit v2 on v1

--- a/solution.py
+++ b/solution.py
@@ -32,6 +32,7 @@
 REACH = 3
 GROUP = 4
 NEG = -1e30
+FRONT = (REACH - 1) * BLOCK
 
 
 def key_window(c):
@@ -69,15 +70,24 @@
 
 def front_kernel(
     heads,
-    wq, wo, in_hbm, bq, w_kv, gain_ref, shift_ref, kv_bias, code_ref, doc_ref,
-    wq_out, wo_out, normed_hbm, q_hbm, mixed_hbm, kv_ref, lse_ref,
-    own_q, own_o, gq, go, sq, so, normed, q_ring, mixed_ring, vt, bias_ref, bq_all,
-    load_sem, ship_sem, o_sem, ring_sem, z_send, z_recv, b_send, b_recv, n_send, n_recv,
+    wq, wo, in_hbm, cot_hbm, w_down_hbm, bq, w_kv, gain_ref, shift_ref, bv_ref, code_ref, doc_ref,
+    wq_out, wo_out, normed_hbm, q_hbm, mixed_hbm, d_acts_hbm, kv_ref, kt_ref, lse_ref,
+    own_q, own_o, gq, go, sq, so, normed, q_ring, mixed_ring, vt, bias_ref, bq_all, cot, down, d_acts,
+    load_sem, cot_sem, down_sem, d_acts_sem, ship_sem, o_sem, ring_sem, z_send, z_recv, b_send, b_recv, n_send, n_recv,
 ):
     m = lax.axis_index("mp")
     d = lax.axis_index("dp")
     dc, dx, dy = flip_bit(d, 1), flip_bit(d, 2), flip_bit(d, 4)
     dxy = flip_bit(dx, 4)
+    is_mid = (m == 1) | (m == 2)
+    buddy, across = {"mp": mp_partner(m, 1)}, {"mp": 3 - m}
+    upper = lax.div(m, 2)
+    inner = lax.rem(m + upper, 2)
+
+    def plane_at(s):
+        q = (1 - inner, 2, 3)[s]
+        return q + upper * (3 - 2 * q)
+
     g = (gq, go)
     half = (gq.shape[2] // 2, go.shape[2] // 2)
     seq, width = normed.shape
@@ -109,18 +119,36 @@
     bq_all[m] = bq[...]
     pl.semaphore_wait(bar, 6)
 
-    def z_copy(w, r, eighth_of):
-        ref = g[w].at[eighth_of, d]
+    def z_copy(w, plane, to, i):
+        ref = g[w].at[plane, d]
         return pltpu.make_async_remote_copy(
-            ref, ref, z_send.at[w, r - 1], z_recv.at[w, r - 1],
-            device_id={"mp": mp_partner(m, r)}, device_id_type=MESH,
+            ref, ref, z_send.at[w, i], z_recv.at[w, plane], device_id=to, device_id_type=MESH
         )
 
-    def z_send_copy(w, r):
-        return z_copy(w, r, m)
-
-    def z_land(w, r):
-        return z_copy(w, r, mp_partner(m, r))
+    def z_own(w, wait=False):
+        def go_or_wait(c):
+            if wait:
+                c.wait_send()
+            else:
+                c.start()
+
+        go_or_wait(z_copy(w, m, buddy, 0))
+
+        @pl.when(is_mid)
+        def _():
+            go_or_wait(z_copy(w, m, across, 1))
+
+    def z_forward(w, s, wait=False):
+        @pl.when(is_mid)
+        def _():
+            c = z_copy(w, plane_at(s), across if s == 0 else buddy, 2 + s)
+            if wait:
+                c.wait_send()
+            else:
+                c.start()
+
+    def z_land(w, s):
+        z_copy(w, plane_at(s), buddy, 0).wait_recv()
 
     def bias_copy(r, plane):
         return pltpu.make_async_remote_copy(
@@ -133,14 +161,14 @@
     sent_to = (dx, dy, dc, dc, dc, dy, dx, dc)
 
     def near(kind, w, r, eighths):
-        q = mp_partner(m, r)
+        q = plane_at(r)
         ref = g[w].at[q, eighths[kind]]
         if kind == 5:
             ref = g[w].at[q, eighths[kind], pl.ds(0, half[w])]
         if kind == 6:
             ref = g[w].at[q, eighths[kind], pl.ds(half[w], half[w])]
         return pltpu.make_async_remote_copy(
-            ref, ref, n_send.at[kind, w, r - 1], n_recv.at[kind, w, r - 1],
+            ref, ref, n_send.at[kind, w, r], n_recv.at[kind, w, r],
             device_id={"dp": sent_to[kind]}, device_id_type=MESH,
         )
 
@@ -154,7 +182,7 @@
     ring = so.shape[0]
 
     def ship(w, r, eighth):
-        q = mp_partner(m, r)
+        q = plane_at(r)
         n = sum(1 for v, _ in shipped if v == w)
         if w == 0:
             sq[q, eighth] = gq[q, eighth].astype(BF16)
@@ -183,14 +211,14 @@
     def set_bias(c):
         first, count = key_window(c)
         bias_ref[pl.ds(0, count), :] = mask_bias(
-            code_ref[pl.ds(first, count), :], doc_ref[:, pl.ds(c * BLOCK, BLOCK)],
+            code_ref[pl.ds(FRONT + first, count), :], doc_ref[:, pl.ds(c * BLOCK, BLOCK)],
             first, count, c * BLOCK, BLOCK,
         )
 
     def attend_block(q, c, n):
         slot = lax.rem(n, 2) if not isinstance(n, int) else n % 2
         first, count = key_window(c)
-        keys, at = pl.ds(first, count), pl.ds(c * BLOCK, BLOCK)
+        keys, at = pl.ds(FRONT + first, count), pl.ds(c * BLOCK, BLOCK)
 
         def free():
             store_q(q, c, slot).wait()
@@ -209,63 +237,121 @@
             e = jnp.exp(s - top)
             total = jnp.sum(e, axis=0, keepdims=True)
             probs = (e * (1.0 / total)).astype(BF16)
-            mixed_ring[slot, :, head] = project(vt[:, keys], probs).T.astype(BF16)
+            mixed_ring[slot, :, head] = project(vt[:, pl.ds(first, count)], probs).T.astype(BF16)
             lse_ref[pl.ds(q * (cols_q // hd) + u, 1), at] = top + jnp.log(total)
         store_mixed(q, c, slot).start()
+
+    bands = w_down_hbm.shape[0] // down.shape[1]
+
+    def load_cot(i):
+        at = rows_at(lax.rem(i, blocks) * BLOCK, BLOCK)
+        slot = lax.rem(i, 2)
+        return pltpu.make_async_copy(cot_hbm.at[at], cot.at[slot], cot_sem.at[slot])
+
+    def load_down(n):
+        at = pl.ds(n * down.shape[1], down.shape[1])
+        return pltpu.make_async_copy(w_down_hbm.at[at], down.at[n % 2], down_sem.at[n % 2])
+
+    def store_d_acts(n, i):
+        slot = lax.rem(i, 2)
+        rows = rows_at(lax.rem(i, blocks) * BLOCK, BLOCK)
+        cols = pl.ds(n * down.shape[1], down.shape[1])
+        return pltpu.make_async_copy(
+            d_acts.at[slot], d_acts_hbm.at[rows, cols], d_acts_sem.at[slot]
+        )
+
+    def d_acts_band(n):
+        load_down(n).wait()
+        if n + 1 < bands:
+            load_down(n + 1).start()
+
+        def one(i, carry):
+            slot = lax.rem(i, 2)
+            load_cot(i).wait()
+
+            @pl.when(i + 1 < bands * blocks)
+            def _():
+                load_cot(i + 1).start()
+
+            @pl.when(i >= 2)
+            def _():
+                store_d_acts(n, i).wait()
+
+            d_acts[slot] = dot_t(cot[slot], down[n % 2])
+            store_d_acts(n, i).start()
+            return carry
+
+        lax.fori_loop(n * blocks, (n + 1) * blocks, one, 0)
 
     def own_plane(c):
         set_bias(c)
         attend_block(m, c, c)
 
-    def other_planes(c):
-        set_bias(c)
+    def other_planes(c, first, end):
+        if first == 1:
+            set_bias(c)
 
         def one(r, carry):
             attend_block(lax.rem(m + r, planes), c, blocks + c * (planes - 1) + r - 1)
             return carry
 
-        lax.fori_loop(1, planes, one, 0)
-
-    stream = [(w, r) for w in (0, 1) for r in (1, 2, 3)]
-
-    def stage(s):
-        if s < len(stream):
-            w, r = stream[s]
-            z_land(w, r).wait_recv()
-            if w == 0:
-                z_send_copy(1, r).start()
-            for kind in (0, 1, 2):
-                go_near(kind, w, r)
-            ship(w, r, d)
-        if 1 <= s <= len(stream):
-            w, r = stream[s - 1]
-            landed(0, w, r)
-            go_near(5, w, r)
-            go_near(3, w, r)
-            ship(w, r, dx)
-            landed(1, w, r)
-            go_near(6, w, r)
-            go_near(4, w, r)
-            ship(w, r, dy)
-            landed(2, w, r)
-            ship(w, r, dc)
-        if 2 <= s <= len(stream) + 1:
-            w, r = stream[s - 2]
-            landed(5, w, r)
-            landed(6, w, r)
-            go_near(7, w, r)
-            ship(w, r, dxy)
-            for kind in (3, 4):
-                landed(kind, w, r)
-                ship(w, r, landed_eighth[kind])
-            landed(7, w, r)
-            ship(w, r, landed_eighth[7])
-
-    for r in (1, 2, 3):
-        z_send_copy(0, r).start()
+        lax.fori_loop(first, end, one, 0)
+
+    stream = [(w, r) for w in (0, 1) for r in range(3)]
+
+    def pass_on(i):
+        w, s = stream[i]
+
+        @pl.when(is_mid)
+        def _():
+            z_land(w, s)
+            z_forward(w, s)
+
+        if i == 2:
+            z_own(1)
+
+    def from_line(i):
+        w, s = stream[i]
+
+        @pl.when(jnp.logical_not(is_mid))
+        def _():
+            z_land(w, s)
+
+        for kind in (0, 1, 2):
+            go_near(kind, w, s)
+        ship(w, s, d)
+
+    def from_near(i):
+        w, s = stream[i]
+        landed(0, w, s)
+        go_near(5, w, s)
+        go_near(3, w, s)
+        ship(w, s, dx)
+        landed(1, w, s)
+        go_near(6, w, s)
+        go_near(4, w, s)
+        ship(w, s, dy)
+        landed(2, w, s)
+        ship(w, s, dc)
+
+    def from_far(i):
+        w, s = stream[i]
+        landed(5, w, s)
+        landed(6, w, s)
+        go_near(7, w, s)
+        ship(w, s, dxy)
+        for kind in (3, 4):
+            landed(kind, w, s)
+            ship(w, s, landed_eighth[kind])
+        landed(7, w, s)
+        ship(w, s, landed_eighth[7])
+
+    z_own(0)
     for r in (1, 2, 3):
         bias_copy(r, m).start()
 
+    load_down(0).start()
+    load_cot(0).start()
     loads[2].wait()
 
     def norm_strip(i, carry):
@@ -276,37 +362,67 @@
     lax.fori_loop(0, seq // STRIP, norm_strip, 0)
     keep_normed = pltpu.make_async_copy(normed, normed_hbm, load_sem.at[2])
     keep_normed.start()
+    kv_ref[pl.ds(0, FRONT), :] = jnp.zeros((FRONT, 2 * hd), BF16)
+    kt_ref[:, pl.ds(0, FRONT)] = jnp.zeros((hd, FRONT), BF16)
     for c in range(blocks):
-        at = pl.ds(c * BLOCK, BLOCK)
-        kv = project(normed[at, :], w_kv[...]) + kv_bias[...]
-        kv_ref[at, :] = kv.astype(BF16)
-        vt[:, at] = kv[:, hd:].T.astype(BF16)
+        at, put = pl.ds(c * BLOCK, BLOCK), pl.ds(FRONT + c * BLOCK, BLOCK)
+        kv = project(normed[at, :], w_kv[...])
+        keys, values = kv[:, :hd], kv[:, hd:] + bv_ref[...]
+        kv_ref[put, pl.ds(0, hd)] = keys.astype(BF16)
+        kv_ref[put, pl.ds(hd, hd)] = values.astype(BF16)
+        kt_ref[:, put] = keys.T.astype(BF16)
+        vt[:, at] = values.T.astype(BF16)
     loads[3].wait()
+
+    def stage(s):
+        if s == 0:
+            pass_on(0)
+        if s + 1 < len(stream):
+            pass_on(s + 1)
+        if s < len(stream):
+            from_line(s)
+        if 1 <= s <= len(stream):
+            from_near(s - 1)
+        if s >= 2:
+            from_far(s - 2)
 
     stage(0)
     own_plane(0)
+    own_plane(1)
     stage(1)
-    own_plane(1)
     own_plane(2)
+    own_plane(3)
     stage(2)
-    own_plane(3)
+    for n in range(bands // 2):
+        d_acts_band(n)
+    stage(3)
+    for n in range(bands // 2, bands):
+        d_acts_band(n)
     for r in (1, 2, 3):
         bias_copy(r, mp_partner(m, r)).wait_recv()
-    stage(3)
     stage(4)
-    other_planes(0)
-    stage(5)
-    other_planes(1)
-    stage(6)
-    other_planes(2)
-    stage(7)
-    other_planes(3)
-
+    other_planes(0, 1, planes)
+    other_planes(1, 1, planes)
+    from_line(5)
+    other_planes(2, 1, 2)
+    from_near(4)
+    other_planes(2, 2, planes)
+    from_far(3)
+    other_planes(3, 1, 2)
+    from_near(5)
+    other_planes(3, 2, planes)
+    from_far(4)
+    from_far(5)
+
+    for i in (0, 1):
+        store_d_acts(0, i).wait()
     for slot in (0, 1):
         store_q(m, 0, slot).wait()
         store_mixed(m, 0, slot).wait()
+    for w in (0, 1):
+        z_own(w, wait=True)
     for w, r in stream:
-        z_send_copy(w, r).wait_send()
+        z_forward(w, r, wait=True)
         for kind in range(8):
             near(kind, w, r, sent_eighth).wait_send()
     for r in (1, 2, 3):
@@ -327,25 +443,28 @@
 
 
 def attention_front(
-    inputs, w_query, b_query, w_keyval, kv_bias, w_out, gain, shift, codes, docs
+    inputs, w_query, b_query, w_keyval, b_value, w_out, gain, shift, code_col, doc_row, cotangent, w_down
 ):
     dp, mp = lax.axis_size("dp"), lax.axis_size("mp")
     width, cols = w_query.shape
     rows = w_out.shape[0]
     seq = inputs.shape[0]
     hd = w_keyval.shape[1] // 2
-    code_col, doc_row = codes.reshape(seq, 1), docs.reshape(1, seq)
     if (dp, mp) != (8, 4):
         all_query, all_out, all_bias = (
             gather_by_sum(a).astype(a.dtype) for a in (w_query, w_out, b_query)
         )
         normed = norm_rows(inputs.astype(F32), gain, shift).astype(BF16)
+        kv_bias = jnp.concatenate([jnp.zeros((hd,), F32), b_value])
         keyval = (project(normed, w_keyval) + kv_bias).astype(BF16)
         queries = jnp.concatenate(
             [project(normed, all_query[i]) + all_bias[i] for i in range(mp)], 1
         ).astype(BF16)
-        mixed, lse = attend(queries, keyval, code_col, doc_row)
-        return all_query, all_out.reshape(-1, width), normed, queries, mixed, keyval, lse
+        mixed, lse = attend(queries, keyval, code_col[FRONT:], doc_row)
+        keyval = jnp.pad(keyval, ((FRONT, 0), (0, 0)))
+        keys_t = keyval[:, :hd].T
+        d_acts = jnp.einsum("td,fd->tf", cotangent, w_down, preferred_element_type=F32)
+        return all_query, all_out.reshape(-1, width), normed, queries, mixed, d_acts, keyval, keys_t, lse
     wq = w_query.reshape(dp, width // dp, cols)
     wo = w_out.reshape(dp, rows // dp, width)
     dma = pltpu.SemaphoreType.DMA
@@ -353,7 +472,7 @@
     full_q, full_o = (mp,) + wq.shape, (mp,) + wo.shape
     heads = mp * cols // hd
     shape = jax.ShapeDtypeStruct
-    out_q, out_o, normed, queries, mixed, keyval, lse = pl.pallas_call(
+    out_q, out_o, normed, queries, mixed, d_acts, keyval, keys_t, lse = pl.pallas_call(
         functools.partial(front_kernel, heads),
         out_shape=(
             shape(full_q, BF16),
@@ -361,11 +480,13 @@
             shape((seq, width), BF16),
             shape((seq, mp * cols), BF16),
             shape((seq, mp * cols), BF16),
-            shape((seq, 2 * hd), BF16),
+            shape((seq, w_down.shape[0]), F32),
+            shape((FRONT + seq, 2 * hd), BF16),
+            shape((hd, FRONT + seq), BF16),
             shape((heads, seq), F32),
         ),
-        in_specs=[HBM] * 3 + [vmem] * 7,
-        out_specs=(HBM,) * 5 + (vmem,) * 2,
+        in_specs=[HBM] * 5 + [vmem] * 7,
+        out_specs=(HBM,) * 6 + (vmem,) * 3,
         scratch_shapes=[
             pltpu.VMEM(wq.shape[1:], BF16),
             pltpu.VMEM(wo.shape[1:], BF16),
@@ -379,12 +500,18 @@
             pltpu.VMEM((hd, seq), BF16),
             pltpu.VMEM((REACH * BLOCK, BLOCK), F32),
             pltpu.VMEM((mp, 1, cols), F32),
+            pltpu.VMEM((2, BLOCK, width), BF16),
+            pltpu.VMEM((2, COLS, width), BF16),
+            pltpu.VMEM((2, BLOCK, COLS), F32),
             dma((6,)),
+            dma((2,)),
+            dma((2,)),
+            dma((2,)),
             dma((3 * dp,)),
             dma((4,)),
             dma((2, 2)),
-            dma((2, 3)),
-            dma((2, 3)),
+            dma((2, 5)),
+            dma((2, mp)),
             dma((3,)),
             dma((3,)),
             dma((8, 2, 3)),
@@ -395,31 +522,33 @@
         ),
         name="attention_front",
     )(
-        wq, wo, inputs, b_query.reshape(1, cols), w_keyval, gain.reshape(1, width),
-        shift.reshape(1, width), kv_bias.reshape(1, 2 * hd), code_col, doc_row,
+        wq, wo, inputs, cotangent, w_down, b_query.reshape(1, cols), w_keyval, gain.reshape(1, width),
+        shift.reshape(1, width), b_value.reshape(1, hd), code_col, doc_row,
     )
     return (
         out_q.reshape(mp, width, cols), out_o.reshape(mp * rows, width),
-        normed, queries, mixed, keyval, lse,
+        normed, queries, mixed, d_acts, keyval, keys_t, lse,
     )
 
 
 PIECE = 32
-CROSS_LATE = 2
-LATE = 5
-AHEAD = 3
+SLOT = 1
+CROSS_LATE = 2 * SLOT
+LATE = 5 * SLOT
+AHEAD = 3 * SLOT
 
 
 class LineSum:
     scratch = staticmethod(
-        lambda rows, width: [pltpu.VMEM((rows, width), F32)] * 3
-        + [pltpu.SemaphoreType.DMA((rows // PIECE,))] * 5
+        lambda rows, pieces, width: [pltpu.VMEM((rows, width), F32)] * 3
+        + [pltpu.SemaphoreType.DMA((pieces,))] * 5
     )
 
     def __init__(self, refs):
         self.part, self.total, self.cross, *sems = refs
         self.in_send, self.in_recv, self.over_send, self.over_recv, self.out_send = sems
-        self.pieces = self.part.shape[0] // PIECE
+        self.slots = self.part.shape[0] // PIECE
+        self.pieces = self.in_send.shape[0]
         m = lax.axis_index("mp")
         self.is_end = (m == 0) | (m == 3)
         self.is_mid = (m == 1) | (m == 2)
@@ -447,26 +576,34 @@
         def _():
             pl.semaphore_wait(bar, 2 + len(others))
 
+    def at(self, k):
+        slot = k if self.slots == self.pieces else k % self.slots
+        return rows_at(slot * PIECE, PIECE)
+
     def inward(self, k):
-        at = rows_at(k * PIECE, PIECE)
+        at = self.at(k)
         return pltpu.make_async_remote_copy(
             self.part.at[at], self.total.at[at], self.in_send.at[k], self.in_recv.at[k],
             device_id=self.buddy, device_id_type=MESH,
         )
 
     def over(self, k):
-        at = rows_at(k * PIECE, PIECE)
+        at = self.at(k)
         return pltpu.make_async_remote_copy(
             self.part.at[at], self.cross.at[at], self.over_send.at[k], self.over_recv.at[k],
             device_id=self.across, device_id_type=MESH,
         )
 
     def outward(self, k):
-        at = rows_at(k * PIECE, PIECE)
+        at = self.at(k)
         return pltpu.make_async_remote_copy(
             self.total.at[at], self.total.at[at], self.out_send.at[k], self.in_recv.at[k],
             device_id=self.buddy, device_id_type=MESH,
         )
+
+    def slot(self, i):
+        for j in range(SLOT):
+            self.tick(i * SLOT + j)
 
     def tick(self, k):
         n = self.pieces
@@ -489,7 +626,7 @@
         def _():
             @pl.when(k < n)
             def _():
-                at = rows_at(k * PIECE, PIECE)
+                at = self.at(k)
                 self.inward(k).wait_recv()
                 self.part[at, :] += self.total[at, :]
                 self.over(k).start()
@@ -497,19 +634,12 @@
             @pl.when((k >= CROSS_LATE) & (k < n + CROSS_LATE))
             def _():
                 j = k - CROSS_LATE
-                at = rows_at(j * PIECE, PIECE)
+                at = self.at(j)
                 self.over(j).wait_recv()
                 self.total[at, :] = self.part[at, :] + self.cross[at, :]
                 self.outward(j).start()
 
-    def finish(self):
-        n = self.pieces
-
-        @pl.when(self.is_end)
-        def _():
-            for k in range(n - AHEAD, n):
-                self.inward(k).wait_send()
-
+    def free(self, first, count):
         @pl.when(self.is_mid)
         def _():
             def sent(k, c):
@@ -517,7 +647,17 @@
                 self.outward(k).wait_send()
                 return c
 
-            lax.fori_loop(0, n, sent, 0)
+            lax.fori_loop(first, first + count, sent, 0)
+
+    def finish(self, freed=0):
+        n = self.pieces
+
+        @pl.when(self.is_end)
+        def _():
+            for k in range(n - AHEAD, n):
+                self.inward(k).wait_send()
+
+        self.free(freed, n - freed)
 
 
 def attend_kernel(seq, heads, q_ref, kv_ref, vt_ref, code_ref, doc_ref, mixed_ref, lse_ref, bias_ref):
@@ -600,16 +740,16 @@
 
 def mlp_attend_back_kernel(
     heads,
-    dh_hbm, w_up_hbm, w_out_hbm, mid_hbm, cot_hbm, q_hbm,
+    dh_hbm, w_up_hbm, w_out_hbm, mid_hbm, cot_hbm, q_hbm, acts_hbm, w_down_hbm,
     kv_ref, kt_ref, code_ref, doc_ref, lse_ref, gain_ref,
-    d_mid_hbm, d_branch_hbm, dq_hbm, dkv_ref, sums_ref,
+    d_mid_hbm, d_branch_hbm, dq_hbm, feed_hbm, dkv_ref, sums_ref,
     w_up, w_out, dh, mid, cot, q, d_branch, d_mixed, dq, bias_ref, load_sem, out_sem, *line_refs,
 ):
     line = LineSum(line_refs)
     seq, width = line.part.shape
     hd = kt_ref.shape[0]
     chunks = seq // BLOCK
-    pieces = BLOCK // PIECE
+    slots = BLOCK // (PIECE * SLOT)
     count = REACH * BLOCK
     scale = 1.0 / math.sqrt(hd)
 
@@ -637,6 +777,8 @@
     load(0, w_up_hbm, w_up).start()
     load_dh(0).start()
     load(1, w_out_hbm, w_out).start()
+    load_acts = load(2, acts_hbm.at[pl.ds(0, BLOCK)], dh)
+    load_down = load(0, w_down_hbm, w_up)
     line.greet()
     dkv_ref[...] = jnp.zeros_like(dkv_ref)
     sums_ref[...] = jnp.zeros_like(sums_ref)
@@ -655,6 +797,24 @@
         @pl.when(c + 1 < chunks)
         def _():
             load_dh(c + 1).start()
+
+        @pl.when(c + 1 == chunks)
+        def _():
+            load_acts.start()
+            load_down.start()
+
+    def produce_feed():
+        at = pl.ds(0, BLOCK)
+        load_acts.wait()
+        load_down.wait()
+        line.free(0, BLOCK // PIECE)
+
+        def cols(n, carry):
+            there = rows_at(n * COLS, COLS)
+            line.part[at, there] = project(dh[...], w_up[:, there])
+            return carry
+
+        lax.fori_loop(0, width // COLS, cols, 0)
 
     def norm_step(c, half):
         def strip(i, carry):
@@ -662,13 +822,15 @@
             at = rows_at(row, STRIP)
             grad = line.total[rows_at(c * BLOCK + row, STRIP), :]
             d_in, weighted = norm_back_rows(mid[at, :], grad, gain_ref[...])
-            d_mid = cot[at, :].astype(F32) + d_in
+            cot_rows = cot[at, :].astype(F32)
+            d_mid = cot_rows + d_in
             low = d_mid.astype(BF16)
             mid[at, :] = d_mid
             d_branch[at, :] = low
             sums_ref[0] += fold_rows(weighted)
             sums_ref[1] += fold_rows(grad)
             sums_ref[2] += fold_rows(low.astype(F32))
+            sums_ref[3] += fold_rows(cot_rows)
             return carry
 
         lax.fori_loop(0, BLOCK // 2 // STRIP, strip, 0)
@@ -713,12 +875,12 @@
     produce(0)
     line.meet()
     for k in range(3):
-        line.tick(k)
+        line.slot(k)
     load(1, w_out_hbm, w_out).wait()
 
     def cycle(u, carry):
         c = u - 1
-        base = u * pieces + 3
+        base = u * slots + 3
 
         @pl.when(u >= 2)
         def _():
@@ -730,13 +892,17 @@
             for i in load_chunk(c):
                 i.start()
 
-        line.tick(base)
+        line.slot(base)
 
         @pl.when(u + 1 < chunks)
         def _():
             produce(u + 1)
 
-        line.tick(base + 1)
+        @pl.when(u + 1 == chunks)
+        def _():
+            produce_feed()
+
+        line.slot(base + 1)
 
         @pl.when(u >= 1)
         def _():
@@ -744,7 +910,7 @@
                 i.wait()
             norm_step(c, 0)
 
-        line.tick(base + 2)
+        line.slot(base + 2)
 
         @pl.when(u >= 1)
         def _():
@@ -752,14 +918,14 @@
             for i in stores(c, (0, 1)):
                 i.start()
 
-        line.tick(base + 3)
+        line.slot(base + 3)
 
         @pl.when(u >= 1)
         def _():
             mixed_step(c)
 
         def some_heads(g, carry):
-            line.tick(base + 4 + g)
+            line.slot(base + 4 + g)
 
             @pl.when(u >= 1)
             def _():
@@ -773,39 +939,46 @@
         def _():
             stores(c, (2,))[0].start()
 
+            def strip(i, carry):
+                sums_ref[4] += fold_rows(dq[rows_at(i * STRIP, STRIP), :].astype(F32))
+                return carry
+
+            lax.fori_loop(0, BLOCK // STRIP, strip, 0)
+
         return carry
 
     lax.fori_loop(0, chunks + 1, cycle, 0)
+    for k in range((chunks + 1) * slots + 3, (line.pieces + LATE) // SLOT):
+        line.slot(k)
+    keep_feed = pltpu.make_async_copy(line.total.at[pl.ds(0, BLOCK)], feed_hbm, out_sem.at[3])
+    keep_feed.start()
     for i in stores(chunks - 1):
         i.wait()
-    line.finish()
-
-
-def padded_keys(keyval):
-    return jnp.pad(keyval, (((REACH - 1) * BLOCK, 0), (0, 0)))
-
-
-def mlp_attend_back(d_hidden, w_up, w_out, middle, cotangent, queries, keyval, codes, docs, lse, gain):
+    keep_feed.wait()
+    line.finish(BLOCK // PIECE)
+
+
+def mlp_attend_back(
+    d_hidden, w_up, w_out, middle, cotangent, queries, acts, w_down,
+    keyval, keys_t, code_col, doc_row, lse, gain,
+):
     seq, width = queries.shape
-    hd = keyval.shape[1] // 2
-    heads = width // hd
-    front = (REACH - 1) * BLOCK
-    kv = padded_keys(keyval)
-    code_col = jnp.pad(codes, (front, 0), constant_values=-2).reshape(-1, 1)
+    heads = width // keys_t.shape[0]
     vmem = pl.BlockSpec(memory_space=pltpu.VMEM)
     dma = pltpu.SemaphoreType.DMA
     block = lambda dtype: pltpu.VMEM((BLOCK, width), dtype)
-    d_middle, d_branch, d_queries, d_kv, sums = pl.pallas_call(
+    return pl.pallas_call(
         functools.partial(mlp_attend_back_kernel, heads),
         out_shape=(
             jax.ShapeDtypeStruct((seq, width), F32),
             jax.ShapeDtypeStruct((seq, width), BF16),
             jax.ShapeDtypeStruct((seq, width), BF16),
-            jax.ShapeDtypeStruct(kv.shape, F32),
-            jax.ShapeDtypeStruct((3, 8, width), F32),
+            jax.ShapeDtypeStruct((BLOCK, width), F32),
+            jax.ShapeDtypeStruct(keyval.shape, F32),
+            jax.ShapeDtypeStruct((5, 8, width), F32),
         ),
-        in_specs=[HBM] * 6 + [vmem] * 6,
-        out_specs=(HBM, HBM, HBM, vmem, vmem),
+        in_specs=[HBM] * 8 + [vmem] * 6,
+        out_specs=(HBM, HBM, HBM, HBM, vmem, vmem),
         scratch_shapes=[
             pltpu.VMEM(w_up.shape, BF16),
             pltpu.VMEM(w_out.shape, BF16),
@@ -818,9 +991,9 @@
             block(BF16),
             pltpu.VMEM((REACH * BLOCK, BLOCK), F32),
             dma((6,)),
-            dma((3,)),
+            dma((4,)),
         ]
-        + LineSum.scratch(seq, width),
+        + LineSum.scratch(seq, (seq + BLOCK) // PIECE, width),
         compiler_params=pltpu.CompilerParams(
             collective_id=1, has_side_effects=True, vmem_limit_bytes=VMEM_LIMIT
         ),
@@ -829,24 +1002,25 @@
         ),
         name="mlp_attend_back",
     )(
-        d_hidden, w_up, w_out, middle, cotangent, queries,
-        kv, kv[:, :hd].T, code_col, docs.reshape(1, seq), lse, gain.reshape(1, width),
+        d_hidden, w_up, w_out, middle, cotangent, queries, acts, w_down,
+        keyval, keys_t, code_col, doc_row, lse, gain.reshape(1, width),
     )
-    return d_middle, d_branch, d_queries, d_kv[front:], jnp.sum(sums, axis=1)
 
 
 def feed_kernel(
     rounds,
-    acts_hbm, w_down_hbm, mid_hbm, dq_hbm, w_q_hbm, in_hbm, d_mid_hbm,
-    dkv_ref, w_kv_ref, gain_ref, bias_ref,
-    out_hbm, in_grad_hbm, sums_ref,
-    w_down, w_q, acts, mid, dq, xs, d_mid, spread, low, in_grad, trade, trade_in,
-    load_sem, out_sem, t_send, t_recv, *line_refs,
+    acts_hbm, w_down_hbm, mid_hbm, dq_hbm, w_q_hbm, in_hbm, d_mid_hbm, table_hbm,
+    dkv_ref, w_kv_ref, gain_ref, bias_ref, sums_in, vectors_in,
+    out_hbm, in_grad_hbm, table_out, vectors_out,
+    w_down, w_q, acts, mid, dq, xs, d_mid, spread, low, in_grad, sums, trade, trade_in, table, table_in, table_all,
+    load_sem, out_sem, t_send, t_recv, h_send, h_recv, d_send, d_recv, *line_refs,
 ):
     line = LineSum(line_refs)
-    seq, width = line.part.shape
-    chunks = seq // BLOCK
-    pieces = BLOCK // PIECE
+    rows, width = line.part.shape
+    seq = rows + BLOCK
+    blocks = seq // BLOCK
+    chunks = rows // BLOCK
+    slots = BLOCK // (PIECE * SLOT)
     planes, _, cols_q = w_q.shape
     m = lax.axis_index("mp")
     d = lax.axis_index("dp")
@@ -856,7 +1030,7 @@
         return pltpu.make_async_copy(src, dst, load_sem.at[i])
 
     def load_feed(c):
-        at = rows_at(c * BLOCK, BLOCK)
+        at = rows_at((c + 1) * BLOCK, BLOCK)
         return [load(2, acts_hbm.at[at], acts), load(3, mid_hbm.at[at], mid)]
 
     def load_grad(c):
@@ -870,12 +1044,16 @@
     def store(i, src, dst, c):
         return pltpu.make_async_copy(src, dst.at[rows_at(c * BLOCK, BLOCK)], out_sem.at[i])
 
+    load_table = load(7, table_hbm, table)
     load(0, w_down_hbm, w_down).start()
     for i in load_feed(0):
         i.start()
+    load_table.start()
     load(1, w_q_hbm, w_q).start()
+    for i in load_grad(0):
+        i.start()
     line.greet(peers)
-    sums_ref[...] = jnp.zeros_like(sums_ref)
+    sums[...] = jnp.zeros_like(sums)
 
     def produce(c):
         at = rows_at(c * BLOCK, BLOCK)
@@ -908,11 +1086,11 @@
         lax.fori_loop(0, BLOCK // STRIP, strip, 0)
 
     def spread_step(c):
-        rows = rows_at(c * BLOCK, BLOCK)
+        here = rows_at(c * BLOCK, BLOCK)
 
         def cols(n, carry):
             there = rows_at(n * COLS, COLS)
-            total = dot_t(dkv_ref[rows, :], w_kv_ref[there, :])
+            total = dot_t(dkv_ref[here, :], w_kv_ref[there, :])
             for i in range(planes):
                 total = total + dot_t(dq[:, pl.ds(i * cols_q, cols_q)], w_q[i, there, :])
             spread[:, there] = total
@@ -926,8 +1104,8 @@
             grad = spread[at, :]
             d_in, weighted = norm_back_rows(xs[at, :].astype(F32), grad, gain_ref[...])
             in_grad[at, :] = (d_mid[at, :] + d_in).astype(BF16)
-            sums_ref[0] += fold_rows(weighted)
-            sums_ref[1] += fold_rows(grad)
+            sums[0] += fold_rows(weighted)
+            sums[1] += fold_rows(grad)
             return carry
 
         lax.fori_loop(0, BLOCK // 2 // STRIP, strip, 0)
@@ -938,104 +1116,181 @@
             device_id=peers[r], device_id_type=MESH,
         )
 
+    def vectors_first():
+        trade[0] = jnp.zeros_like(trade.at[0])
+        for i in range(2):
+            trade[0, i : i + 1] = jnp.sum(sums[i], axis=0, keepdims=True)
+        for i in range(sums_in.shape[0]):
+            trade[0, 2 + i : 3 + i] = jnp.sum(sums_in[i], axis=0, keepdims=True)
+        at = 2 + sums_in.shape[0]
+        trade[0, at : at + vectors_in.shape[0]] = vectors_in[...]
+        swap(0).start()
+
+    def vectors_next(r):
+        swap(r).wait()
+        trade[r + 1] = trade[r] + trade_in[r]
+        if r + 1 < rounds:
+            swap(r + 1).start()
+        else:
+            vectors_out[...] = trade[r + 1]
+
+    bits = [lax.rem(lax.div(d, 1 << r), 2) for r in range(rounds)]
+    base = [0]
+    size = [table.shape[0]]
+    for r in range(rounds):
+        size.append(size[r] // 2)
+        base.append(base[r] + bits[r] * size[r + 1])
+
+    def part_of(start, count):
+        return pl.ds(pl.multiple_of(start, 8), count)
+
+    def halve(r):
+        away = part_of(base[r] + (1 - bits[r]) * size[r + 1], size[r + 1])
+        into = pl.ds(size[0] - size[r], size[r + 1])
+        return pltpu.make_async_remote_copy(
+            table.at[away], table_in.at[into], h_send.at[r], h_recv.at[r],
+            device_id=peers[r], device_id_type=MESH,
+        )
+
+    def double(r, mine):
+        start = base[r] + (bits[r] if mine else 1 - bits[r]) * size[r + 1]
+        at = part_of(start, size[r + 1])
+        return pltpu.make_async_remote_copy(
+            table_all.at[at], table_all.at[at], d_send.at[r], d_recv.at[r],
+            device_id=peers[r], device_id_type=MESH,
+        )
+
+    store_table = pltpu.make_async_copy(table_all, table_out, out_sem.at[2])
+
+    def table_step(i):
+        if i == 0:
+            load_table.wait()
+        elif i <= rounds:
+            r = i - 1
+            halve(r).wait()
+            at = part_of(base[r + 1], size[r + 1])
+            whole = table_all if i == rounds else table
+            whole[at, :] = table[at, :] + table_in[pl.ds(size[0] - size[r], size[r + 1]), :]
+        else:
+            r = 2 * rounds - i
+            double(r, True).wait_send()
+            double(r, False).wait_recv()
+        if i < rounds:
+            halve(i).start()
+        elif i < 2 * rounds:
+            double(2 * rounds - 1 - i, True).start()
+        else:
+            store_table.start()
+
     load(0, w_down_hbm, w_down).wait()
     produce(0)
     line.meet(peers)
     for k in range(3):
-        line.tick(k)
+        line.slot(k)
     load(1, w_q_hbm, w_q).wait()
+
+    def grads(u, first):
+        v = 2 * u + (0 if first else 1)
+
+        def one():
+            @pl.when(v < blocks)
+            def _():
+                for i in load_grad(v):
+                    i.wait()
+                spread_step(v)
+
+        def two():
+            @pl.when(v < blocks)
+            def _():
+                @pl.when(v >= 1)
+                def _():
+                    store(1, in_grad, in_grad_hbm, v - 1).wait()
+
+                norm_step(v, 0)
+
+        def three():
+            @pl.when(v < blocks)
+            def _():
+                norm_step(v, 1)
+                store(1, in_grad, in_grad_hbm, v).start()
+
+                @pl.when(v + 1 < blocks)
+                def _():
+                    for i in load_grad(v + 1):
+                        i.start()
+
+        return one, two, three
 
     def cycle(u, carry):
         c = u - 1
-        base = u * pieces + 3
-
-        @pl.when(u < chunks)
-        def _():
-            for i in load_grad(u):
-                i.start()
-
-        line.tick(base)
-
-        @pl.when(u + 1 < chunks)
-        def _():
-            produce(u + 1)
-
-        line.tick(base + 1)
-
-        @pl.when(u >= 1)
-        def _():
-            @pl.when(u >= 2)
+        base_tick = u * slots + 3
+
+        def produce_step():
+            @pl.when(u + 1 < chunks)
             def _():
-                store(0, low, out_hbm, u - 2).wait()
-
-            output_step(c)
-            store(0, low, out_hbm, c).start()
-
-        line.tick(base + 2)
-
-        @pl.when(u < chunks)
-        def _():
-            for i in load_grad(u):
-                i.wait()
-            spread_step(u)
-
-        line.tick(base + 3)
-        line.tick(base + 4)
-
-        @pl.when(u < chunks)
-        def _():
+                produce(u + 1)
+
+        def out_step():
             @pl.when(u >= 1)
             def _():
-                store(1, in_grad, in_grad_hbm, u - 1).wait()
-
-            norm_step(u, 0)
-
-        line.tick(base + 5)
-        line.tick(base + 6)
-
-        @pl.when(u < chunks)
-        def _():
-            norm_step(u, 1)
-            store(1, in_grad, in_grad_hbm, u).start()
-
-        line.tick(base + 7)
-
-        @pl.when(u == chunks - 1)
-        def _():
-            trade[0, 0:8] = sums_ref[0]
-            trade[0, 8:16] = sums_ref[1]
-            for r in range(rounds):
-                swap(r).start()
-                swap(r).wait()
-                trade[r + 1] = trade[r] + trade_in[r]
-            sums_ref[0] = trade[rounds, 0:8]
-            sums_ref[1] = trade[rounds, 8:16]
-
+                @pl.when(u >= 2)
+                def _():
+                    store(0, low, out_hbm, u - 2).wait()
+
+                output_step(c)
+                store(0, low, out_hbm, c).start()
+
+        steps = [produce_step, out_step, *grads(u, True), *grads(u, False)]
+        for i, step in enumerate(steps):
+            line.slot(base_tick + i)
+            for v in range(chunks + 1):
+                at = v * slots + i
+                extra = []
+                if at % 2 == 0 and at // 2 <= 2 * rounds:
+                    extra.append(functools.partial(table_step, at // 2))
+                late = at - (blocks // 2) * slots
+                if late == 0:
+                    extra.append(vectors_first)
+                elif 0 < late <= rounds:
+                    extra.append(functools.partial(vectors_next, late - 1))
+                if extra:
+
+                    @pl.when(u == v)
+                    def _(extra=extra):
+                        for e in extra:
+                            e()
+
+            step()
         return carry
 
     lax.fori_loop(0, chunks + 1, cycle, 0)
     store(0, low, out_hbm, chunks - 1).wait()
-    store(1, in_grad, in_grad_hbm, chunks - 1).wait()
+    store(1, in_grad, in_grad_hbm, blocks - 1).wait()
+    store_table.wait()
     line.finish()
 
 
 def feed_and_input_grad(
-    acts, w_down, middle, b_down, d_queries, all_query, d_keyval, w_keyval, inputs, d_middle, gain
+    acts, w_down, middle, b_down, d_queries, all_query, d_keyval, w_keyval, inputs, d_middle, gain,
+    table, sums, vectors,
 ):
     seq, width = inputs.shape
     rounds = (lax.axis_size("dp") - 1).bit_length()
     vmem = pl.BlockSpec(memory_space=pltpu.VMEM)
     dma = pltpu.SemaphoreType.DMA
     block = lambda dtype: pltpu.VMEM((BLOCK, width), dtype)
-    outputs, input_grad, sums = pl.pallas_call(
+    rest = seq - BLOCK
+    shape = jax.ShapeDtypeStruct
+    return pl.pallas_call(
         functools.partial(feed_kernel, rounds),
         out_shape=(
-            jax.ShapeDtypeStruct((seq, width), BF16),
-            jax.ShapeDtypeStruct((seq, width), BF16),
-            jax.ShapeDtypeStruct((2, 8, width), F32),
+            shape((rest, width), BF16),
+            shape((seq, width), BF16),
+            shape(table.shape, F32),
+            shape((16, width), F32),
         ),
-        in_specs=[HBM] * 7 + [vmem] * 4,
-        out_specs=(HBM, HBM, vmem),
+        in_specs=[HBM] * 8 + [vmem] * 6,
+        out_specs=(HBM, HBM, HBM, vmem),
         scratch_shapes=[
             pltpu.VMEM(w_down.shape, BF16),
             pltpu.VMEM(all_query.shape, BF16),
@@ -1047,14 +1302,22 @@
             block(F32),
             block(BF16),
             block(BF16),
+            pltpu.VMEM((2, 8, width), F32),
             pltpu.VMEM((rounds + 1, 16, width), F32),
             pltpu.VMEM((rounds, 16, width), F32),
-            dma((7,)),
-            dma((2,)),
+            pltpu.VMEM(table.shape, F32),
+            pltpu.VMEM(table.shape, F32),
+            pltpu.VMEM(table.shape, F32),
+            dma((8,)),
+            dma((3,)),
+            dma((rounds,)),
+            dma((rounds,)),
+            dma((rounds,)),
+            dma((rounds,)),
             dma((rounds,)),
             dma((rounds,)),
         ]
-        + LineSum.scratch(seq, width),
+        + LineSum.scratch(rest, rest // PIECE, width),
         compiler_params=pltpu.CompilerParams(
             collective_id=2, has_side_effects=True, vmem_limit_bytes=VMEM_LIMIT
         ),
@@ -1063,18 +1326,9 @@
         ),
         name="feed_and_input_grad",
     )(
-        acts, w_down, middle, d_queries, all_query, inputs, d_middle,
-        d_keyval, w_keyval, gain.reshape(1, width), b_down.reshape(1, width),
+        acts, w_down, middle, d_queries, all_query, inputs, d_middle, table,
+        d_keyval, w_keyval, gain.reshape(1, width), b_down.reshape(1, width), sums, vectors,
     )
-    return outputs, input_grad, jnp.sum(sums, axis=1)
-
-
-def sum_packed(table, vectors):
-    width = table.shape[1]
-    rows = [jnp.pad(v, (0, width - v.shape[0])).reshape(1, width) for v in vectors]
-    total = lax.psum(jnp.concatenate([table] + rows, 0), "dp")
-    head = table.shape[0]
-    return total[:head], [total[head + i, : v.shape[0]] for i, v in enumerate(vectors)]
 
 
 def shards(
@@ -1103,20 +1357,20 @@
     own_cols = w_query.shape[1]
     own = lax.axis_index("mp") * own_cols
     inputs_f = inputs.astype(F32)
-    bias_full = jnp.concatenate([jnp.zeros((hd,), F32), b_value])
     docs = doc_ids[0]
     codes = jnp.where(pad_mask[0] == 1, docs, -1)
-
-    all_query, all_out, normed_attn, queries, mixed, keyval, lse = attention_front(
-        inputs, w_query, b_query, w_keyval, bias_full, w_out, attn_gain, attn_shift, codes, docs
+    code_col = jnp.pad(codes, (FRONT, 0), constant_values=-2).reshape(-1, 1)
+    doc_row = docs.reshape(1, seq)
+
+    all_query, all_out, normed_attn, queries, mixed, d_acts, keyval, keys_t, lse = attention_front(
+        inputs, w_query, b_query, w_keyval, b_value, w_out, attn_gain, attn_shift, code_col, doc_row,
+        cotangent, w_down,
     )
     middle = inputs_f + project(mixed, all_out) + b_out
     normed_mlp = norm_rows(middle, mlp_gain, mlp_shift).astype(BF16)
     hidden = project(normed_mlp, w_up) + b_up
     acts = jax.nn.gelu(hidden, approximate=True).astype(BF16)
     grad_w_down = jnp.einsum("tf,td->fd", acts, cotangent, preferred_element_type=F32)
-    grad_b_down = jnp.sum(cotangent.astype(F32), axis=0)
-    d_acts = jnp.einsum("td,fd->tf", cotangent, w_down, preferred_element_type=F32)
     _, gelu_pull = jax.vjp(functools.partial(jax.nn.gelu, approximate=True), hidden)
     d_hidden = gelu_pull(d_acts)[0].astype(BF16)
     grad_b_up = jnp.sum(d_hidden.astype(F32), axis=0)
@@ -1125,42 +1379,38 @@
     grad_w_up = lax.psum_scatter(grad_w_up, "dp", scatter_dimension=0, tiled=True)
     grad_w_down = lax.psum_scatter(grad_w_down, "dp", scatter_dimension=1, tiled=True)
 
-    d_middle, d_branch, d_queries, d_keyval_sum, sums = mlp_attend_back(
-        d_hidden, w_up, all_out, middle, cotangent, queries, keyval, codes, docs, lse, mlp_gain
+    d_middle, d_branch, d_queries, feed_first, d_keyval_sum, sums = mlp_attend_back(
+        d_hidden, w_up, all_out, middle, cotangent, queries, acts, w_down,
+        keyval, keys_t, code_col, doc_row, lse, mlp_gain,
     )
     d_keyval_sum, grad_w_down, grad_w_up = lax.optimization_barrier(
         (d_keyval_sum, grad_w_down, grad_w_up)
     )
-    grad_mlp_gain, grad_mlp_shift, grad_b_out = sums[0], sums[1], sums[2]
+    d_keyval_sum = d_keyval_sum[FRONT:]
     own_mixed = lax.dynamic_slice_in_dim(mixed, own, own_cols, 1)
     grad_w_out = jnp.einsum("tq,td->qd", own_mixed, d_branch, preferred_element_type=F32)
     grad_b_value = jnp.sum(d_keyval_sum[:, hd:], axis=0)
     d_keyval = d_keyval_sum.astype(BF16)
     own_d_queries = lax.dynamic_slice_in_dim(d_queries, own, own_cols, 1)
-    grad_b_query = jnp.sum(own_d_queries.astype(F32), axis=0)
     grad_w_query = jnp.einsum("td,tq->dq", normed_attn, own_d_queries, preferred_element_type=F32)
     grad_w_keyval = jnp.einsum("tk,td->kd", d_keyval, normed_attn, preferred_element_type=F32)
-    small = (
-        grad_b_query,
-        grad_b_value,
-        grad_b_out,
-        grad_mlp_gain,
-        grad_mlp_shift,
-        grad_b_up,
-        grad_b_down,
-    )
-    acts, small, grad_w_keyval, grad_w_out, grad_w_query = lax.optimization_barrier(
-        (acts, small, grad_w_keyval, grad_w_out, grad_w_query)
+    vectors = jnp.stack([grad_b_up, jnp.pad(grad_b_value, (0, width - hd))])
+    vectors, grad_w_keyval, grad_w_out, grad_w_query = lax.optimization_barrier(
+        (vectors, grad_w_keyval, grad_w_out, grad_w_query)
     )
     grad_w_out = lax.psum_scatter(grad_w_out, "dp", scatter_dimension=1, tiled=True)
     grad_w_query = lax.psum_scatter(grad_w_query, "dp", scatter_dimension=0, tiled=True)
-    grad_w_keyval, small = sum_packed(grad_w_keyval, small)
+    out_rest, input_grad, grad_w_keyval, totals = feed_and_input_grad(
+        acts, w_down, middle, b_down, d_queries, all_query, d_keyval, w_keyval, inputs, d_middle, attn_gain,
+        grad_w_keyval, sums, vectors,
+    )
+    out_first = (middle[:BLOCK] + feed_first + b_down).astype(BF16)
+    outputs = jnp.concatenate([out_first, out_rest], 0)
     grad_w_keyval = grad_w_keyval.T
-    grad_b_query, grad_b_value, grad_b_out, grad_mlp_gain, grad_mlp_shift, grad_b_up, grad_b_down = small
-    outputs, input_grad, sums = feed_and_input_grad(
-        acts, w_down, middle, b_down, d_queries, all_query, d_keyval, w_keyval, inputs, d_middle, attn_gain
-    )
-    grad_attn_gain, grad_attn_shift = sums[0], sums[1]
+    grad_attn_gain, grad_attn_shift, grad_mlp_gain, grad_mlp_shift = (totals[i] for i in range(4))
+    grad_b_out, grad_b_down, grad_b_query, grad_b_up = (totals[i] for i in range(4, 8))
+    grad_b_query = lax.dynamic_slice_in_dim(grad_b_query, own, own_cols, 0)
+    grad_b_value = totals[8, :hd]
     return (
         outputs,
         input_grad,

time: 759 us -> 699 us (0.921)
  Pallas kernels: 606 us -> 564 us
  local copies, waits for them, and re-layouts: 26.2 us -> 13.4 us
  matrix products: 93.8 us -> 86.1 us
    pallas_call x1, Pallas kernels: 213 us -> 173 us  [feed_and_input_grad(): pl.pallas_call(functools.partial(feed_kernel, rounds), out_shape=(shape((...]
    pallas_call x1, Pallas kernels: 157 us -> 133 us  [attention_front(): pl.pallas_call(functools.partial(front_kernel, heads), out_shape=(shape(f...]
    pallas_call x1, Pallas kernels: 236 us -> 258 us  [mlp_attend_back(): pl.pallas_call(functools.partial(mlp_attend_back_kernel, heads), out_shap...]
    dot_general x1 -> x0, matrix products: 21.1 us -> none  [shards(): jnp.einsum('td,fd->tf', cotangent, w_down, preferred_element_type=F32)]
    dot_general x2, matrix products: 25.3 us -> 37.4 us  [project(): return jnp.dot(left, right, preferred_element_type=F32)]
  transfers between devices with their start and end apart: 5 -> 4, of which waited for: 0 -> 0; matrix products, arithmetic and copies ran while one was open for 4% -> 4% of each run, Pallas kernels for 60% -> 63%
where the time goes in v2:
time: 699 us; the launch traced here: 689 us
  Pallas kernels  564 us (81%)
  matrix products  86.1 us (12%)
  between operations  14.4 us (2%)
  local copies, waits for them, and re-layouts  13.4 us (2%)
  other arithmetic  10.5 us (2%)
    pallas_call x1, Pallas kernels, mlp_attend_back(): pl.pallas_call(functools.partial(mlp_attend_back_kernel, heads), out_shap...  258 us
    pallas_call x1, Pallas kernels, feed_and_input_grad(): pl.pallas_call(functools.partial(feed_kernel, rounds), out_shape=(shape((...  173 us
    pallas_call x1, Pallas kernels, attention_front(): pl.pallas_call(functools.partial(front_kernel, heads), out_shape=(shape(f...  133 us
    dot_general x2, matrix products, project(): return jnp.dot(left, right, preferred_element_type=F32)  37.4 us
    dot_general x1, matrix products, shards(): jnp.einsum('tf,td->fd', acts, cotangent, preferred_element_type=F32)  15.4 us
    dot_general x1, matrix products, shards(): jnp.einsum('td,tf->df', normed_mlp, d_hidden, preferred_element_type=F32)  14.7 us
  transfers between devices with their start and end apart: 4, of which 0 were waited for; matrix products, arithmetic and copies ran while one was open for 4% of the time, Pallas kernels for 63%

profile of v2, /device:TPU:0, one launch (start us, length us, event | category | flops | bytes accessed | tf_op | source)
XLA Modules:
  0.0 689.5 jit_solution(13668783484055248129)
XLA Ops:
  7.2 0.0 reduce-scatter.5.cloned.1.call-start
  7.2 0.7 compare_select_fusion
  7.9 1.2 reshape.93.code_ref
  9.1 0.0 copy-start.5
  9.1 132.8 %attention_front.1 = (bf16[4,8,256,512]{3,2,1,0:T(8,128)(2,1)}, bf16[4,8,64,2048]{3,2,1,0:T(8,128)(2,1)}, bf16[1024,2048]{1,0:T(8,128)(2,1)}, bf16[1024,2048]{1,...) custom-call(bf16[8,256,512]{2,1,0:T(8,128)(2,1)} %bitcast.33, ...), custom_call_target="tpu_custom_call" | custom-call | tf_op jit(solution)/shard_map/attention_front/pallas_call | solution.py:475
  141.9 0.0 copy-done.5
  141.9 13.4 %fusion.19 = (f32[1024]{0:T(1024)S(1)}, f32[1024,2048]{1,0:T(8,128)S(1)}) fusion(f32[2048]{0:T(1024)S(1)} %copy-done.5, bf16[1024,2048]{1,0:T(8,128)(2,1)} %get-tuple-element.45, bf16[2048,2048]{1,0:T(8,128)(2,1)} %bitcast.54, bf16[1024,2048]{1,0:T(8,128)(2,1)} %in_hbm.3), kind=kOutput, calls=%fused_computation.35 | convolution fusion | flops 8598322176 | bytes 25178112 | tf_op jit(solution)/shard_map/dot_general | solution.py:26
  155.3 0.0 copy-start
  155.3 0.0 copy-start.6
  155.3 0.0 copy-start.7
  155.3 0.0 copy-start.8
  155.3 1.0 multiply_reduce_fusion
  156.3 0.0 copy-done.6
  156.3 0.0 copy-done.7
  156.3 0.0 copy-done.8
  156.3 24.0 %convert_reduce_fusion = (f32[2048]{0:T(1024)}, bf16[1024,2048]{1,0:T(8,128)(2,1)}, bf16[1024,2048]{1,0:T(8,128)(2,1)}) fusion(f32[1024,2048]{1,0:T(8,128)} %get-tuple-element.47, f32[2048]{0:T(1024)S(1)} %copy-done.6, bf16[2048,2048]{1,0:T(8,128)(2,1)} %w_up_hbm.1, f32[1024,2048]{1,0:T(8,128)S(1)} %get-tuple-element.118.mid_hbm, f32[2048]{0:T(1024)S(1)} %copy-done.7, ...), kind=kOutput, calls=%fused_computation.9 | convolution fusion | flops 8652847104 | bytes 33595392 | tf_op jit(solution)/shard_map/dot_general | solution.py:26
  180.3 0.0 copy-done
  180.3 14.7 %fusion.15 = f32[2048,2048]{1,0:T(8,128)} fusion(bf16[1024,2048]{1,0:T(8,128)(2,1)} %get-tuple-element.48.dh_hbm, f32[1024,2048]{1,0:T(8,128)S(1)} %get-tuple-element.118.mid_hbm, f32[2048]{0:T(1024)S(1)} %copy-done.7, f32[2048]{0:T(1024)S(1)} %copy-done.8, f32[1024]{0:T(1024)S(1)} %add_rsqrt_fusion, f32[1024]{0:T(1024)S(1)} %broadcast_multiply_fusion), kind=kOutput, calls=%fused_computation.32 | convolution fusion | flops 8600420352 | bytes 29384704 | tf_op jit(solution)/shard_map/td,tf->df/dot_general | solution.py:1377
  195.1 15.4 %fusion.22 = f32[2048,2048]{1,0:T(8,128)} fusion(bf16[1024,2048]{1,0:T(8,128)(2,1)} %get-tuple-element.108.acts_hbm, bf16[1024,2048]{1,0:T(8,128)(2,1)} %cot_hbm.3), kind=kOutput, calls=%fused_computation.38 | convolution fusion | flops 8589934592 | bytes 25165824 | tf_op jit(solution)/shard_map/tf,td->fd/dot_general | solution.py:1373
  210.5 0.0 reduce-scatter.5.cloned.1.call-update
  210.5 0.0 reduce-scatter.7.cloned.1.call-start
  210.5 0.7 reduce-scatter.7.cloned.1.call-update
  211.2 0.0 reduce-scatter.9.cloned.1.call-start
  211.3 258.3 %mlp_attend_back.1 = (f32[1024,2048]{1,0:T(8,128)}, bf16[1024,2048]{1,0:T(8,128)(2,1)}, bf16[1024,2048]{1,0:T(8,128)(2,1)}, f32[256,2048]{1,0:T(8,128)}, f32[1536,256]{1,0:T(8,128)}, /*index=5*/f32[5,8,2048]{2,1,0:T(8,128)}) custom-call(bf16[1024,2048]{1,0:T(8,128)(2,1)} %get-tuple-element.48.dh_hbm, bf16[2048,2048]{1,0:T(8,128)(2,1)} %w_up_hbm.1, ...), custom_call_target="tpu_custom_call" | custom-call | flops 199999995904 | bytes 33554432 | tf_op jit(solution)/shard_map/mlp_attend_back/pallas_call | solution.py:970
  469.6 6.8 fusion.11
  476.4 0.0 copy-start.2
  476.4 0.0 copy-start.4
  476.4 7.0 %fusion.9 = f32[2048,512]{1,0:T(8,128)} fusion(bf16[1024,2048]{1,0:T(8,128)(2,1)} %get-tuple-element.61, bf16[1024,2048]{1,0:T(8,128)(2,1)} %get-tuple-element.54.dq_hbm, s32[]{:T(128)S(6)} %select_n.14), kind=kOutput, calls=%fused_computation.19 | convolution fusion | flops 2147483648 | bytes 9437188 | tf_op jit(solution)/shard_map/td,tq->dq/dot_general | solution.py:1395
  483.4 0.0 copy-start.3
  483.4 0.0 reduce-scatter.5.cloned.1.call-done
  483.4 0.0 reduce-scatter.7.cloned.1.call-done
  483.4 0.0 copy-done.2
  483.4 0.1 slice_reduce_fusion
  483.6 4.8 fusion.20.table_hbm
  488.4 0.0 copy-done.4
  488.4 0.6 pad_maximum_fusion.1.vectors_in
  489.0 0.0 reduce-scatter.9.cloned.1.call-update
  489.0 0.0 reduce-scatter.11.cloned.1.call-start
  489.1 0.0 copy-done.3
  489.1 3.6 fusion.8
  492.7 0.9 slice.60.dkv_ref
  493.5 0.0 reduce-scatter.11.cloned.1.call-update
  493.5 0.0 copy-start.1
  493.6 173.1 %feed_and_input_grad.1 = (bf16[768,2048]{1,0:T(8,128)(2,1)}, bf16[1024,2048]{1,0:T(8,128)(2,1)}, f32[256,2048]{1,0:T(8,128)}, f32[16,2048]{1,0:T(8,128)}) custom-call(bf16[1024,2048]{1,0:T(8,128)(2,1)} %get-tuple-element.108.acts_hbm, bf16[2048,2048]{1,0:T(8,128)(2,1)} %w_down_hbm.5, f32[1024,2048]{1,0:T(8,128)} %copy-done, ...), custom_call_target="tpu_custom_call" | custom-call | flops 199999995904 | bytes 33554432 | tf_op jit(solution)/shard_map/feed_and_input_grad/pallas_call | solution.py:1284
  666.7 2.9 copy.37
  669.5 1.9 fusion.18
  671.4 0.6 constant_dynamic-slice_fusion
  672.0 1.2 slice_bitcast_fusion
  673.2 0.0 copy-done.1
  673.2 4.5 pad_maximum_fusion
  677.7 0.0 reduce-scatter.9.cloned.1.call-done
  677.7 0.0 reduce-scatter.11.cloned.1.call-done
  677.7 4.8 copy.39
  (4 shorter events, 0.0 us)
Async XLA Ops:
  7.2 476.3 %reduce-scatter.5.cloned.1.call-start = ((), (), s32[]{:S(2)}) async-start(), calls=%async_computation.4 | async-start | bytes 18874368 | tf_op jit(solution)/shard_map/reduce_scatter | solution.py:1380
  9.1 132.8 %copy-start.5 = (f32[2048]{0:T(1024)S(1)}, f32[2048]{0:T(1024)}, u32[]{:S(2)}) copy-start(f32[2048]{0:T(1024)} %param.28) | copy-start | bytes 24580
  155.3 25.1 %copy-start = (f32[1024,2048]{1,0:T(8,128)}, f32[1024,2048]{1,0:T(8,128)S(1)}, u32[]{:S(2)}) copy-start(f32[1024,2048]{1,0:T(8,128)S(1)} %get-tuple-element.118.mid_hbm) | copy-start | bytes 25165828
  155.3 1.0 copy-start.6
  155.3 1.0 copy-start.7
  155.3 1.0 copy-start.8
  210.5 273.0 %reduce-scatter.7.cloned.1.call-start = ((), (), s32[]{:S(2)}) async-start(), calls=%async_computation.5 | async-start | bytes 18874368 | tf_op jit(solution)/shard_map/reduce_scatter | solution.py:1379
  211.2 466.5 %reduce-scatter.9.cloned.1.call-start = ((), (), s32[]{:S(2)}) async-start(), calls=%async_computation.6 | async-start | bytes 4718592 | tf_op jit(solution)/shard_map/reduce_scatter | solution.py:1402
  476.4 7.0 %copy-start.2 = (f32[1536,256]{1,0:T(8,128)S(1)}, f32[1536,256]{1,0:T(8,128)}, u32[]{:S(2)}) copy-start(f32[1536,256]{1,0:T(8,128)} %get-tuple-element.60) | copy-start | bytes 4718596
  476.4 11.9 %copy-start.4 = (f32[2048]{0:T(1024)S(1)}, f32[2048]{0:T(1024)}, u32[]{:S(2)}) copy-start(f32[2048]{0:T(1024)} %get-tuple-element.106) | copy-start | bytes 24580
  483.4 5.6 copy-start.3
  489.0 188.7 %reduce-scatter.11.cloned.1.call-start = ((), (), s32[]{:S(2)}) async-start(), calls=%async_computation.7 | async-start | bytes 4718592 | tf_op jit(solution)/shard_map/reduce_scatter | solution.py:1401
  493.5 179.7 %copy-start.1 = (bf16[256,2048]{1,0:T(8,128)(2,1)S(1)}, bf16[256,2048]{1,0:T(8,128)(2,1)}, u32[]{:S(2)}) copy-start(bf16[256,2048]{1,0:T(8,128)(2,1)} %fusion.8) | copy-start | bytes 3145732
Sparse Core Ops, SparseCore 0:
  210.6 118.0 reduce-scatter.4
  332.9 116.1 reduce-scatter.6
  489.1 55.3 reduce-scatter.8
  548.7 59.1 reduce-scatter.10

commit v3 on v2

--- a/solution.py
+++ b/solution.py
@@ -734,19 +734,28 @@
     return d_in, weighted
 
 
+def dot_down(a, b):
+    return lax.dot_general(a, b, (((0,), (0,)), ((), ())), preferred_element_type=F32)
+
+
 def fold_rows(x):
     return jnp.sum(x.reshape(-1, 8, x.shape[-1]), axis=0)
 
 
 def mlp_attend_back_kernel(
     heads,
-    dh_hbm, w_up_hbm, w_out_hbm, mid_hbm, cot_hbm, q_hbm, acts_hbm, w_down_hbm,
+    dh_hbm, w_up_hbm, w_out_hbm, mid_hbm, cot_hbm, q_hbm, acts_hbm, w_down_hbm, normed_hbm, mixed_hbm,
     kv_ref, kt_ref, code_ref, doc_ref, lse_ref, gain_ref,
-    d_mid_hbm, d_branch_hbm, dq_hbm, feed_hbm, dkv_ref, sums_ref,
-    w_up, w_out, dh, mid, cot, q, d_branch, d_mixed, dq, bias_ref, load_sem, out_sem, *line_refs,
+    d_mid_hbm, dq_hbm, feed_hbm, grads_hbm, dkv_ref, sums_ref,
+    w_up, w_out, dh, mid, cot, q, normed, mixed, d_branch, d_mixed, dq, grads, bias_ref,
+    load_sem, out_sem, *line_refs,
 ):
     line = LineSum(line_refs)
-    seq, width = line.part.shape
+    seq, width = q_hbm.shape
+    m = lax.axis_index("mp")
+    own_cols = mixed.shape[1]
+    own = rows_at(m * own_cols, own_cols)
+    ring = line.part.shape[0] // BLOCK
     hd = kt_ref.shape[0]
     chunks = seq // BLOCK
     slots = BLOCK // (PIECE * SLOT)
@@ -765,13 +774,18 @@
             load(3, mid_hbm.at[at], mid),
             load(4, cot_hbm.at[at], cot),
             load(5, q_hbm.at[at], q),
+            load(6, normed_hbm.at[at], normed),
+            load(7, mixed_hbm.at[at, own], mixed),
         ]
+
+    def block_at(c):
+        return rows_at((c % ring) * BLOCK, BLOCK)
 
     def store(i, src, dst, c):
         return pltpu.make_async_copy(src, dst.at[rows_at(c * BLOCK, BLOCK)], out_sem.at[i])
 
-    def stores(c, which=(0, 1, 2)):
-        pairs = ((mid, d_mid_hbm), (d_branch, d_branch_hbm), (dq, dq_hbm))
+    def stores(c, which=(0, 1)):
+        pairs = ((mid, d_mid_hbm), (dq, dq_hbm))
         return [store(i, *pairs[i], c) for i in which]
 
     load(0, w_up_hbm, w_up).start()
@@ -779,12 +793,14 @@
     load(1, w_out_hbm, w_out).start()
     load_acts = load(2, acts_hbm.at[pl.ds(0, BLOCK)], dh)
     load_down = load(0, w_down_hbm, w_up)
+    load_mid = load(3, mid_hbm.at[pl.ds(0, BLOCK)], mid)
     line.greet()
     dkv_ref[...] = jnp.zeros_like(dkv_ref)
     sums_ref[...] = jnp.zeros_like(sums_ref)
+    grads[...] = jnp.zeros_like(grads)
 
     def produce(c):
-        at = rows_at(c * BLOCK, BLOCK)
+        at = block_at(c)
         load_dh(c).wait()
 
         def cols(n, carry):
@@ -804,10 +820,10 @@
             load_down.start()
 
     def produce_feed():
-        at = pl.ds(0, BLOCK)
+        at = block_at(chunks)
         load_acts.wait()
         load_down.wait()
-        line.free(0, BLOCK // PIECE)
+        load_mid.wait()
 
         def cols(n, carry):
             there = rows_at(n * COLS, COLS)
@@ -816,11 +832,25 @@
 
         lax.fori_loop(0, width // COLS, cols, 0)
 
+        @pl.when(m == 0)
+        def _():
+            line.part[at, :] += mid[...]
+
+    def add_grads(first, left, right):
+        at = pl.ds(first, own_cols)
+
+        def cols(n, carry):
+            there = rows_at(n * COLS, COLS)
+            grads[at, there] += dot_down(left, right[:, there])
+            return carry
+
+        lax.fori_loop(0, width // COLS, cols, 0)
+
     def norm_step(c, half):
         def strip(i, carry):
             row = half * (BLOCK // 2) + i * STRIP
             at = rows_at(row, STRIP)
-            grad = line.total[rows_at(c * BLOCK + row, STRIP), :]
+            grad = line.total[rows_at((c % ring) * BLOCK + row, STRIP), :]
             d_in, weighted = norm_back_rows(mid[at, :], grad, gain_ref[...])
             cot_rows = cot[at, :].astype(F32)
             d_mid = cot_rows + d_in
@@ -887,20 +917,28 @@
             for i in stores(u - 2):
                 i.wait()
 
+        @pl.when(u + 1 == chunks)
+        def _():
+            load_mid.start()
+
+        line.slot(base)
+
+        @pl.when(u >= 2)
+        def _():
+            line.free((u - 2) * (BLOCK // PIECE), BLOCK // PIECE)
+
+        @pl.when(u + 1 < chunks)
+        def _():
+            produce(u + 1)
+
+        @pl.when(u + 1 == chunks)
+        def _():
+            produce_feed()
+
         @pl.when(u >= 1)
         def _():
             for i in load_chunk(c):
                 i.start()
-
-        line.slot(base)
-
-        @pl.when(u + 1 < chunks)
-        def _():
-            produce(u + 1)
-
-        @pl.when(u + 1 == chunks)
-        def _():
-            produce_feed()
 
         line.slot(base + 1)
 
@@ -915,14 +953,14 @@
         @pl.when(u >= 1)
         def _():
             norm_step(c, 1)
-            for i in stores(c, (0, 1)):
-                i.start()
+            stores(c, (0,))[0].start()
 
         line.slot(base + 3)
 
         @pl.when(u >= 1)
         def _():
             mixed_step(c)
+            add_grads(own_cols, mixed[...], d_branch)
 
         def some_heads(g, carry):
             line.slot(base + 4 + g)
@@ -937,7 +975,8 @@
 
         @pl.when(u >= 1)
         def _():
-            stores(c, (2,))[0].start()
+            stores(c, (1,))[0].start()
+            add_grads(0, dq[:, own], normed)
 
             def strip(i, carry):
                 sums_ref[4] += fold_rows(dq[rows_at(i * STRIP, STRIP), :].astype(F32))
@@ -950,16 +989,19 @@
     lax.fori_loop(0, chunks + 1, cycle, 0)
     for k in range((chunks + 1) * slots + 3, (line.pieces + LATE) // SLOT):
         line.slot(k)
-    keep_feed = pltpu.make_async_copy(line.total.at[pl.ds(0, BLOCK)], feed_hbm, out_sem.at[3])
+    keep_grads = pltpu.make_async_copy(grads, grads_hbm, out_sem.at[3])
+    keep_grads.start()
+    keep_feed = pltpu.make_async_copy(line.total.at[block_at(chunks)], feed_hbm, out_sem.at[2])
     keep_feed.start()
     for i in stores(chunks - 1):
         i.wait()
     keep_feed.wait()
-    line.finish(BLOCK // PIECE)
+    keep_grads.wait()
+    line.finish((chunks - 1) * (BLOCK // PIECE))
 
 
 def mlp_attend_back(
-    d_hidden, w_up, w_out, middle, cotangent, queries, acts, w_down,
+    d_hidden, w_up, w_out, middle, cotangent, queries, acts, w_down, normed, mixed, own_cols,
     keyval, keys_t, code_col, doc_row, lse, gain,
 ):
     seq, width = queries.shape
@@ -972,12 +1014,12 @@
         out_shape=(
             jax.ShapeDtypeStruct((seq, width), F32),
             jax.ShapeDtypeStruct((seq, width), BF16),
-            jax.ShapeDtypeStruct((seq, width), BF16),
             jax.ShapeDtypeStruct((BLOCK, width), F32),
+            jax.ShapeDtypeStruct((2 * own_cols, width), F32),
             jax.ShapeDtypeStruct(keyval.shape, F32),
             jax.ShapeDtypeStruct((5, 8, width), F32),
         ),
-        in_specs=[HBM] * 8 + [vmem] * 6,
+        in_specs=[HBM] * 10 + [vmem] * 6,
         out_specs=(HBM, HBM, HBM, HBM, vmem, vmem),
         scratch_shapes=[
             pltpu.VMEM(w_up.shape, BF16),
@@ -987,13 +1029,16 @@
             block(BF16),
             block(BF16),
             block(BF16),
+            pltpu.VMEM((BLOCK, own_cols), BF16),
             block(BF16),
             block(BF16),
+            block(BF16),
+            pltpu.VMEM((2 * own_cols, width), F32),
             pltpu.VMEM((REACH * BLOCK, BLOCK), F32),
-            dma((6,)),
+            dma((8,)),
             dma((4,)),
         ]
-        + LineSum.scratch(seq, (seq + BLOCK) // PIECE, width),
+        + LineSum.scratch(min(3 * BLOCK, seq), (seq + BLOCK) // PIECE, width),
         compiler_params=pltpu.CompilerParams(
             collective_id=1, has_side_effects=True, vmem_limit_bytes=VMEM_LIMIT
         ),
@@ -1002,17 +1047,17 @@
         ),
         name="mlp_attend_back",
     )(
-        d_hidden, w_up, w_out, middle, cotangent, queries, acts, w_down,
+        d_hidden, w_up, w_out, middle, cotangent, queries, acts, w_down, normed, mixed,
         keyval, keys_t, code_col, doc_row, lse, gain.reshape(1, width),
     )
 
 
 def feed_kernel(
     rounds,
-    acts_hbm, w_down_hbm, mid_hbm, dq_hbm, w_q_hbm, in_hbm, d_mid_hbm, table_hbm,
-    dkv_ref, w_kv_ref, gain_ref, bias_ref, sums_in, vectors_in,
+    acts_hbm, w_down_hbm, mid_hbm, dq_hbm, w_q_hbm, in_hbm, d_mid_hbm, normed_hbm, first_hbm,
+    dkv_f_ref, w_kv_ref, gain_ref, bias_ref, sums_in, b_up_in,
     out_hbm, in_grad_hbm, table_out, vectors_out,
-    w_down, w_q, acts, mid, dq, xs, d_mid, spread, low, in_grad, sums, trade, trade_in, table, table_in, table_all,
+    w_down, w_q, acts, mid, dq, xs, d_mid, spread, low, in_grad, normed, dkv_ref, sums, trade, trade_in, table, table_in, table_all,
     load_sem, out_sem, t_send, t_recv, h_send, h_recv, d_send, d_recv, *line_refs,
 ):
     line = LineSum(line_refs)
@@ -1044,16 +1089,22 @@
     def store(i, src, dst, c):
         return pltpu.make_async_copy(src, dst.at[rows_at(c * BLOCK, BLOCK)], out_sem.at[i])
 
-    load_table = load(7, table_hbm, table)
+    def load_normed(c):
+        return load(7, normed_hbm.at[rows_at(c * BLOCK, BLOCK)], normed)
+
+    load_first = load(8, first_hbm, spread)
     load(0, w_down_hbm, w_down).start()
     for i in load_feed(0):
         i.start()
-    load_table.start()
+    load_first.start()
+    load_normed(0).start()
     load(1, w_q_hbm, w_q).start()
     for i in load_grad(0):
         i.start()
     line.greet(peers)
     sums[...] = jnp.zeros_like(sums)
+    dkv_ref[...] = dkv_f_ref[pl.ds(FRONT, seq), :].astype(BF16)
+    hd = dkv_ref.shape[1] // 2
 
     def produce(c):
         at = rows_at(c * BLOCK, BLOCK)
@@ -1076,11 +1127,11 @@
             for i in load_feed(c + 1):
                 i.start()
 
-    def output_step(c):
+    def output_step(source, c):
         def strip(i, carry):
             at = rows_at(i * STRIP, STRIP)
             there = rows_at(c * BLOCK + i * STRIP, STRIP)
-            low[at, :] = (line.total[there, :] + bias_ref[...]).astype(BF16)
+            low[at, :] = (source[there, :] + bias_ref[...]).astype(BF16)
             return carry
 
         lax.fori_loop(0, BLOCK // STRIP, strip, 0)
@@ -1123,7 +1174,9 @@
         for i in range(sums_in.shape[0]):
             trade[0, 2 + i : 3 + i] = jnp.sum(sums_in[i], axis=0, keepdims=True)
         at = 2 + sums_in.shape[0]
-        trade[0, at : at + vectors_in.shape[0]] = vectors_in[...]
+        trade[0, at : at + 1] = b_up_in[...]
+        d_values = dkv_f_ref[pl.ds(FRONT, seq), pl.ds(hd, hd)]
+        trade[0, at + 1 : at + 2, 0:hd] = jnp.sum(d_values, axis=0, keepdims=True)
         swap(0).start()
 
     def vectors_next(r):
@@ -1134,6 +1187,19 @@
         else:
             vectors_out[...] = trade[r + 1]
 
+    def table_block(c):
+        load_normed(c).wait()
+
+        def cols(n, carry):
+            there = rows_at(n * COLS, COLS)
+            part = dot_down(dkv_ref[pl.ds(c * BLOCK, BLOCK), :], normed[:, there])
+            table[:, there] = part if c == 0 else table[:, there] + part
+            return carry
+
+        lax.fori_loop(0, width // COLS, cols, 0)
+        if c + 1 < blocks:
+            load_normed(c + 1).start()
+
     bits = [lax.rem(lax.div(d, 1 << r), 2) for r in range(rounds)]
     base = [0]
     size = [table.shape[0]]
@@ -1163,15 +1229,13 @@
     store_table = pltpu.make_async_copy(table_all, table_out, out_sem.at[2])
 
     def table_step(i):
-        if i == 0:
-            load_table.wait()
-        elif i <= rounds:
+        if 1 <= i <= rounds:
             r = i - 1
             halve(r).wait()
             at = part_of(base[r + 1], size[r + 1])
             whole = table_all if i == rounds else table
             whole[at, :] = table[at, :] + table_in[pl.ds(size[0] - size[r], size[r + 1]), :]
-        else:
+        elif i > rounds:
             r = 2 * rounds - i
             double(r, True).wait_send()
             double(r, False).wait_recv()
@@ -1231,14 +1295,17 @@
                 produce(u + 1)
 
         def out_step():
+            @pl.when(u == 0)
+            def _():
+                load_first.wait()
+                output_step(spread, 0)
+                store(0, low, out_hbm, 0).start()
+
             @pl.when(u >= 1)
             def _():
-                @pl.when(u >= 2)
-                def _():
-                    store(0, low, out_hbm, u - 2).wait()
-
-                output_step(c)
-                store(0, low, out_hbm, c).start()
+                store(0, low, out_hbm, u - 1).wait()
+                output_step(line.total, c)
+                store(0, low, out_hbm, u).start()
 
         steps = [produce_step, out_step, *grads(u, True), *grads(u, False)]
         for i, step in enumerate(steps):
@@ -1246,8 +1313,10 @@
             for v in range(chunks + 1):
                 at = v * slots + i
                 extra = []
-                if at % 2 == 0 and at // 2 <= 2 * rounds:
-                    extra.append(functools.partial(table_step, at // 2))
+                if at % 2 == 0 and at // 2 < blocks:
+                    extra.append(functools.partial(table_block, at // 2))
+                if at % 2 == 0 and 0 <= at // 2 - blocks <= 2 * rounds:
+                    extra.append(functools.partial(table_step, at // 2 - blocks))
                 late = at - (blocks // 2) * slots
                 if late == 0:
                     extra.append(vectors_first)
@@ -1264,15 +1333,15 @@
         return carry
 
     lax.fori_loop(0, chunks + 1, cycle, 0)
-    store(0, low, out_hbm, chunks - 1).wait()
+    store(0, low, out_hbm, chunks).wait()
     store(1, in_grad, in_grad_hbm, blocks - 1).wait()
     store_table.wait()
     line.finish()
 
 
 def feed_and_input_grad(
-    acts, w_down, middle, b_down, d_queries, all_query, d_keyval, w_keyval, inputs, d_middle, gain,
-    table, sums, vectors,
+    acts, w_down, middle, b_down, d_queries, all_query, d_keyval_sum, w_keyval, inputs, d_middle, gain,
+    normed, feed_first, sums, b_up,
 ):
     seq, width = inputs.shape
     rounds = (lax.axis_size("dp") - 1).bit_length()
@@ -1281,15 +1350,16 @@
     block = lambda dtype: pltpu.VMEM((BLOCK, width), dtype)
     rest = seq - BLOCK
     shape = jax.ShapeDtypeStruct
+    table = (w_keyval.shape[1], width)
     return pl.pallas_call(
         functools.partial(feed_kernel, rounds),
         out_shape=(
-            shape((rest, width), BF16),
             shape((seq, width), BF16),
-            shape(table.shape, F32),
+            shape((seq, width), BF16),
+            shape(table, F32),
             shape((16, width), F32),
         ),
-        in_specs=[HBM] * 8 + [vmem] * 6,
+        in_specs=[HBM] * 9 + [vmem] * 6,
         out_specs=(HBM, HBM, HBM, vmem),
         scratch_shapes=[
             pltpu.VMEM(w_down.shape, BF16),
@@ -1302,13 +1372,15 @@
             block(F32),
             block(BF16),
             block(BF16),
+            block(BF16),
+            pltpu.VMEM((seq, w_keyval.shape[1]), BF16),
             pltpu.VMEM((2, 8, width), F32),
             pltpu.VMEM((rounds + 1, 16, width), F32),
             pltpu.VMEM((rounds, 16, width), F32),
-            pltpu.VMEM(table.shape, F32),
-            pltpu.VMEM(table.shape, F32),
-            pltpu.VMEM(table.shape, F32),
-            dma((8,)),
+            pltpu.VMEM(table, F32),
+            pltpu.VMEM(table, F32),
+            pltpu.VMEM(table, F32),
+            dma((9,)),
             dma((3,)),
             dma((rounds,)),
             dma((rounds,)),
@@ -1326,8 +1398,9 @@
         ),
         name="feed_and_input_grad",
     )(
-        acts, w_down, middle, d_queries, all_query, inputs, d_middle, table,
-        d_keyval, w_keyval, gain.reshape(1, width), b_down.reshape(1, width), sums, vectors,
+        acts, w_down, middle, d_queries, all_query, inputs, d_middle, normed, feed_first,
+        d_keyval_sum, w_keyval, gain.reshape(1, width), b_down.reshape(1, width), sums,
+        b_up.reshape(1, width),
     )
 
 
@@ -1379,33 +1452,17 @@
     grad_w_up = lax.psum_scatter(grad_w_up, "dp", scatter_dimension=0, tiled=True)
     grad_w_down = lax.psum_scatter(grad_w_down, "dp", scatter_dimension=1, tiled=True)
 
-    d_middle, d_branch, d_queries, feed_first, d_keyval_sum, sums = mlp_attend_back(
-        d_hidden, w_up, all_out, middle, cotangent, queries, acts, w_down,
+    d_middle, d_queries, feed_first, grads, d_keyval_sum, sums = mlp_attend_back(
+        d_hidden, w_up, all_out, middle, cotangent, queries, acts, w_down, normed_attn, mixed, own_cols,
         keyval, keys_t, code_col, doc_row, lse, mlp_gain,
     )
-    d_keyval_sum, grad_w_down, grad_w_up = lax.optimization_barrier(
-        (d_keyval_sum, grad_w_down, grad_w_up)
+    grads, grad_w_down, grad_w_up = lax.optimization_barrier((grads, grad_w_down, grad_w_up))
+    grads = lax.psum_scatter(grads, "dp", scatter_dimension=1, tiled=True)
+    outputs, input_grad, grad_w_keyval, totals = feed_and_input_grad(
+        acts, w_down, middle, b_down, d_queries, all_query, d_keyval_sum, w_keyval, inputs, d_middle,
+        attn_gain, normed_attn, feed_first, sums, grad_b_up,
     )
-    d_keyval_sum = d_keyval_sum[FRONT:]
-    own_mixed = lax.dynamic_slice_in_dim(mixed, own, own_cols, 1)
-    grad_w_out = jnp.einsum("tq,td->qd", own_mixed, d_branch, preferred_element_type=F32)
-    grad_b_value = jnp.sum(d_keyval_sum[:, hd:], axis=0)
-    d_keyval = d_keyval_sum.astype(BF16)
-    own_d_queries = lax.dynamic_slice_in_dim(d_queries, own, own_cols, 1)
-    grad_w_query = jnp.einsum("td,tq->dq", normed_attn, own_d_queries, preferred_element_type=F32)
-    grad_w_keyval = jnp.einsum("tk,td->kd", d_keyval, normed_attn, preferred_element_type=F32)
-    vectors = jnp.stack([grad_b_up, jnp.pad(grad_b_value, (0, width - hd))])
-    vectors, grad_w_keyval, grad_w_out, grad_w_query = lax.optimization_barrier(
-        (vectors, grad_w_keyval, grad_w_out, grad_w_query)
-    )
-    grad_w_out = lax.psum_scatter(grad_w_out, "dp", scatter_dimension=1, tiled=True)
-    grad_w_query = lax.psum_scatter(grad_w_query, "dp", scatter_dimension=0, tiled=True)
-    out_rest, input_grad, grad_w_keyval, totals = feed_and_input_grad(
-        acts, w_down, middle, b_down, d_queries, all_query, d_keyval, w_keyval, inputs, d_middle, attn_gain,
-        grad_w_keyval, sums, vectors,
-    )
-    out_first = (middle[:BLOCK] + feed_first + b_down).astype(BF16)
-    outputs = jnp.concatenate([out_first, out_rest], 0)
+    grad_w_query, grad_w_out = grads[:own_cols].T, grads[own_cols:]
     grad_w_keyval = grad_w_keyval.T
     grad_attn_gain, grad_attn_shift, grad_mlp_gain, grad_mlp_shift = (totals[i] for i in range(4))
     grad_b_out, grad_b_down, grad_b_query, grad_b_up = (totals[i] for i in range(4, 8))

time: 699 us -> 673 us (0.963)
  matrix products: 86.1 us -> 67.7 us
  other arithmetic: 10.5 us -> 1.68 us
    dot_general x3 -> x0, matrix products: 18.6 us -> none  [the longest x1 6.99 us: shards(): jnp.einsum('td,tq->dq', normed_attn, own_d_queries, preferred_element_typ...]
  transfers between devices with their start and end apart: 4 -> 3, of which waited for: 0 -> 0; matrix products, arithmetic and copies ran while one was open for 4% -> 1% of each run, Pallas kernels for 63% -> 65%
where the time goes in v3:
time: 673 us; the launch traced here: 663 us
  Pallas kernels  561 us (83%)
  matrix products  67.7 us (10%)
  local copies, waits for them, and re-layouts  17.7 us (3%)
  between operations  14.3 us (2%)
    pallas_call x1, Pallas kernels, mlp_attend_back(): pl.pallas_call(functools.partial(mlp_attend_back_kernel, heads), out_shap...  262 us
    pallas_call x1, Pallas kernels, feed_and_input_grad(): pl.pallas_call(functools.partial(feed_kernel, rounds), out_shape=(shape((...  166 us
    pallas_call x1, Pallas kernels, attention_front(): pl.pallas_call(functools.partial(front_kernel, heads), out_shape=(shape(f...  133 us
    dot_general x2, matrix products, project(): return jnp.dot(left, right, preferred_element_type=F32)  37.4 us
    dot_general x1, matrix products, shards(): jnp.einsum('tf,td->fd', acts, cotangent, preferred_element_type=F32)  15.5 us
    dot_general x1, matrix products, shards(): jnp.einsum('td,tf->df', normed_mlp, d_hidden, preferred_element_type=F32)  14.8 us
  transfers between devices with their start and end apart: 3, of which 0 were waited for; matrix products, arithmetic and copies ran while one was open for 1% of the time, Pallas kernels for 65%

profile of v3, /device:TPU:0, one launch (start us, length us, event | category | flops | bytes accessed | tf_op | source)
XLA Modules:
  0.0 663.3 jit_solution(2104849577622411447)
XLA Ops:
  7.2 0.0 reduce-scatter.4.cloned.1.call-start
  7.2 0.7 compare_select_fusion
  7.9 1.2 reshape.99.code_ref
  9.1 0.0 copy-start.2
  9.1 132.8 %attention_front.1 = (bf16[4,8,256,512]{3,2,1,0:T(8,128)(2,1)}, bf16[4,8,64,2048]{3,2,1,0:T(8,128)(2,1)}, bf16[1024,2048]{1,0:T(8,128)(2,1)}, bf16[1024,2048]{1,...) custom-call(bf16[8,256,512]{2,1,0:T(8,128)(2,1)} %bitcast.31, ...), custom_call_target="tpu_custom_call" | custom-call | tf_op jit(solution)/shard_map/attention_front/pallas_call | solution.py:475
  141.9 0.0 copy-done.2
  141.9 13.4 %fusion.12 = (f32[1024]{0:T(1024)S(1)}, f32[1024,2048]{1,0:T(8,128)S(1)}) fusion(f32[2048]{0:T(1024)S(1)} %copy-done.2, bf16[1024,2048]{1,0:T(8,128)(2,1)} %get-tuple-element.41.mixed_hbm, bf16[2048,2048]{1,0:T(8,128)(2,1)} %bitcast.49, bf16[1024,2048]{1,0:T(8,128)(2,1)} %in_hbm.3), kind=kOutput, calls=%fused_computation.24 | convolution fusion | flops 8598322176 | bytes 25178112 | tf_op jit(solution)/shard_map/dot_general | solution.py:26
  155.3 0.0 copy-start
  155.3 0.0 copy-start.3
  155.3 0.0 copy-start.4
  155.3 0.0 copy-start.5
  155.4 1.0 multiply_reduce_fusion
  156.3 0.0 copy-done.3
  156.3 0.0 copy-done.4
  156.4 0.0 copy-done.5
  156.4 24.0 %convert_reduce_fusion = (f32[2048]{0:T(1024)}, bf16[1024,2048]{1,0:T(8,128)(2,1)}, bf16[1024,2048]{1,0:T(8,128)(2,1)}) fusion(f32[1024,2048]{1,0:T(8,128)} %get-tuple-element.43, f32[2048]{0:T(1024)S(1)} %copy-done.3, bf16[2048,2048]{1,0:T(8,128)(2,1)} %w_up_hbm.1, f32[1024,2048]{1,0:T(8,128)S(1)} %get-tuple-element.112.mid_hbm, f32[2048]{0:T(1024)S(1)} %copy-done.4, ...), kind=kOutput, calls=%fused_computation.9 | convolution fusion | flops 8652847104 | bytes 33595392 | tf_op jit(solution)/shard_map/dot_general | solution.py:26
  180.4 0.0 copy-done
  180.4 14.8 %fusion.7 = f32[2048,2048]{1,0:T(8,128)} fusion(bf16[1024,2048]{1,0:T(8,128)(2,1)} %get-tuple-element.44.dh_hbm, f32[1024,2048]{1,0:T(8,128)S(1)} %get-tuple-element.112.mid_hbm, f32[2048]{0:T(1024)S(1)} %copy-done.4, f32[2048]{0:T(1024)S(1)} %copy-done.5, f32[1024]{0:T(1024)S(1)} %add_rsqrt_fusion, f32[1024]{0:T(1024)S(1)} %broadcast_multiply_fusion), kind=kOutput, calls=%fused_computation.20 | convolution fusion | flops 8600420352 | bytes 29384704 | tf_op jit(solution)/shard_map/td,tf->df/dot_general | solution.py:1450
  195.2 15.5 %fusion.13 = f32[2048,2048]{1,0:T(8,128)} fusion(bf16[1024,2048]{1,0:T(8,128)(2,1)} %get-tuple-element.100.acts_hbm, bf16[1024,2048]{1,0:T(8,128)(2,1)} %cot_hbm.3), kind=kOutput, calls=%fused_computation.25 | convolution fusion | flops 8589934592 | bytes 25165824 | tf_op jit(solution)/shard_map/tf,td->fd/dot_general | solution.py:1446
  210.7 0.0 reduce-scatter.4.cloned.1.call-update
  210.7 0.0 reduce-scatter.6.cloned.1.call-start
  210.8 0.7 reduce-scatter.6.cloned.1.call-update
  211.5 0.0 reduce-scatter.8.cloned.1.call-start
  211.5 261.7 %mlp_attend_back.1 = (f32[1024,2048]{1,0:T(8,128)}, bf16[1024,2048]{1,0:T(8,128)(2,1)}, f32[256,2048]{1,0:T(8,128)}, f32[1024,2048]{1,0:T(8,128)}, f32[1536,256]{1,0:T(8,128)}, /*index=5*/f32[5,8,2048]{2,1,0:T(8,128)}) custom-call(bf16[1024,2048]{1,0:T(8,128)(2,1)} %get-tuple-element.44.dh_hbm, bf16[2048,2048]{1,0:T(8,128)(2,1)} %w_up_hbm.1, ...), custom_call_target="tpu_custom_call" | custom-call | flops 199999995904 | bytes 33554432 | tf_op jit(solution)/shard_map/mlp_attend_back/pallas_call | solution.py:1012
  473.2 0.0 reduce-scatter.4.cloned.1.call-done
  473.2 0.0 reduce-scatter.6.cloned.1.call-done
  473.3 0.0 reduce-scatter.8.cloned.1.call-update
  473.3 166.5 %feed_and_input_grad.1 = (bf16[1024,2048]{1,0:T(8,128)(2,1)}, bf16[1024,2048]{1,0:T(8,128)(2,1)}, f32[256,2048]{1,0:T(8,128)}, f32[16,2048]{1,0:T(8,128)}) custom-call(bf16[1024,2048]{1,0:T(8,128)(2,1)} %get-tuple-element.100.acts_hbm, bf16[2048,2048]{1,0:T(8,128)(2,1)} %w_down_hbm.5, f32[1024,2048]{1,0:T(8,128)} %copy-done, ...), custom_call_target="tpu_custom_call" | custom-call | flops 199999995904 | bytes 33554432 | tf_op jit(solution)/shard_map/feed_and_input_grad/pallas_call | solution.py:1354
  639.8 2.9 copy.39
  642.7 1.9 fusion.11
  644.6 0.6 constant_dynamic-slice_fusion
  645.1 1.2 slice_bitcast_fusion.1
  646.3 0.0 reduce-scatter.8.cloned.1.call-done
  646.3 2.1 fusion.10
  648.4 1.0 copy.38
  649.4 0.0 copy-start.1
  649.4 4.9 copy.42
  654.3 0.0 copy-done.1
  654.3 2.0 copy.43
  (3 shorter events, 0.0 us)
Async XLA Ops:
  7.2 466.1 %reduce-scatter.4.cloned.1.call-start = ((), (), s32[]{:S(2)}) async-start(), calls=%async_computation.3 | async-start | bytes 18874368 | tf_op jit(solution)/shard_map/reduce_scatter | solution.py:1453
  9.1 132.8 %copy-start.2 = (f32[2048]{0:T(1024)S(1)}, f32[2048]{0:T(1024)}, u32[]{:S(2)}) copy-start(f32[2048]{0:T(1024)} %param.28) | copy-start | bytes 24580
  155.3 25.1 %copy-start = (f32[1024,2048]{1,0:T(8,128)}, f32[1024,2048]{1,0:T(8,128)S(1)}, u32[]{:S(2)}) copy-start(f32[1024,2048]{1,0:T(8,128)S(1)} %get-tuple-element.112.mid_hbm) | copy-start | bytes 25165828
  155.3 1.0 copy-start.3
  155.3 1.0 copy-start.4
  155.3 1.0 copy-start.5
  210.7 262.5 %reduce-scatter.6.cloned.1.call-start = ((), (), s32[]{:S(2)}) async-start(), calls=%async_computation.4 | async-start | bytes 18874368 | tf_op jit(solution)/shard_map/reduce_scatter | solution.py:1452
  211.5 434.8 %reduce-scatter.8.cloned.1.call-start = ((), (), s32[]{:S(2)}) async-start(), calls=%async_computation.5 | async-start | bytes 9437184 | tf_op jit(solution)/shard_map/reduce_scatter | solution.py:1460
  649.4 4.9 copy-start.1
Sparse Core Ops, SparseCore 0:
  210.9 118.0 reduce-scatter.3
  333.1 116.0 reduce-scatter.5
  473.4 73.5 reduce-scatter.7

commit v4 on v3

--- a/solution.py
+++ b/solution.py
@@ -742,11 +742,234 @@
     return jnp.sum(x.reshape(-1, 8, x.shape[-1]), axis=0)
 
 
+FEED_EARLY = 2
+
+GELU_A = math.sqrt(2.0 / math.pi)
+GELU_B = 0.044715
+
+
+def gelu_pair(u):
+    square = u * u
+    t = jnp.tanh(u * (GELU_A + GELU_A * GELU_B * square))
+    cdf = 0.5 * (1.0 + t)
+    slope = cdf + 0.5 * u * (1.0 - t * t) * (GELU_A + 3.0 * GELU_A * GELU_B * square)
+    return u * cdf, slope
+
+
+def mlp_kernel(
+    mixed_hbm, w_out_hbm, in_hbm, w_up_hbm, d_acts_hbm, cot_hbm,
+    b_out_ref, gain_ref, shift_ref, b_up_ref,
+    mid_hbm, acts_hbm, dh_hbm, down_hbm, up_hbm, first_hbm, b_up_sum,
+    w_out, w_up, normed, acts, dh, cot, mixed, xs, mid, d_acts, turned, tiles,
+    load_sem, out_sem, tile_sem, *line_refs,
+):
+    line = LineSum(line_refs)
+    seq, width = normed.shape
+    blocks = seq // BLOCK
+    hidden = w_up.shape[1]
+
+    def load(i, src, dst):
+        return pltpu.make_async_copy(src, dst, load_sem.at[i])
+
+    def load_block(c):
+        at = pl.ds(c * BLOCK, BLOCK)
+        return [
+            load(2, mixed_hbm.at[at], mixed),
+            load(3, in_hbm.at[at], xs),
+        ]
+
+    def load_d_acts(c):
+        return load(4, d_acts_hbm.at[pl.ds(c * BLOCK, BLOCK)], d_acts)
+
+    def store_mid(c):
+        return pltpu.make_async_copy(mid, mid_hbm.at[pl.ds(c * BLOCK, BLOCK)], out_sem.at[0])
+
+    store_acts = pltpu.make_async_copy(acts, acts_hbm, out_sem.at[1])
+    store_dh = pltpu.make_async_copy(dh, dh_hbm, out_sem.at[2])
+
+    load(0, w_out_hbm, w_out).start()
+    for i in load_block(0):
+        i.start()
+    load(1, w_up_hbm, w_up).start()
+    load_d_acts(0).start()
+    load(5, cot_hbm, cot).start()
+    line.greet()
+    b_up_sum[...] = jnp.zeros_like(b_up_sum)
+
+    def middle_step(c):
+        for i in load_block(c):
+            i.wait()
+        if c >= 1:
+            store_mid(c - 1).wait()
+
+        def cols(n, carry):
+            there = rows_at(n * COLS, COLS)
+            mid[:, there] = (
+                project(mixed[...], w_out[:, there]) + xs[:, there].astype(F32) + b_out_ref[:, there]
+            )
+            return carry
+
+        lax.fori_loop(0, width // COLS, cols, 0)
+        store_mid(c).start()
+        if c + 1 < blocks:
+            for i in load_block(c + 1):
+                i.start()
+
+    def norm_step(c):
+        def strip(i, carry):
+            at = rows_at(i * STRIP, STRIP)
+            put = rows_at(c * BLOCK + i * STRIP, STRIP)
+            normed[put, :] = norm_rows(mid[at, :], gain_ref[...], shift_ref[...]).astype(BF16)
+            return carry
+
+        lax.fori_loop(0, BLOCK // STRIP, strip, 0)
+
+    def hidden_step(c):
+        at = pl.ds(c * BLOCK, BLOCK)
+        load_d_acts(c).wait()
+
+        def cols(n, carry):
+            there = rows_at(n * COLS, COLS)
+            u = project(normed[at, :], w_up[:, there]) + b_up_ref[:, there]
+            value, slope = gelu_pair(u)
+            acts[at, there] = value.astype(BF16)
+            low = (d_acts[:, there] * slope).astype(BF16)
+            dh[at, there] = low
+            b_up_sum[:, there] += fold_rows(low.astype(F32))
+            return carry
+
+        lax.fori_loop(0, hidden // COLS, cols, 0)
+        if c + 1 < blocks:
+            load_d_acts(c + 1).start()
+        else:
+            store_acts.start()
+            store_dh.start()
+
+    def produce():
+        def cols(n, carry):
+            there = rows_at(n * COLS, COLS)
+            line.part[:, there] = dot_t(dh[pl.ds(0, BLOCK), :], w_up[there, :])
+            return carry
+
+        lax.fori_loop(0, width // COLS, cols, 0)
+
+    tile_rows, tile_cols = tiles.shape[1:]
+    tile_list = []
+    for left, right, out in ((acts, cot, down_hbm), (normed, dh, up_hbm)):
+        for row in range(0, left.shape[1], tile_rows):
+            for col in range(0, right.shape[1], tile_cols):
+                tile_list.append((left, right, out, row, col))
+
+    def store_tile(i):
+        _, _, out, row, col = tile_list[i]
+        return pltpu.make_async_copy(
+            tiles.at[i % 2], out.at[pl.ds(row, tile_rows), pl.ds(col, tile_cols)], tile_sem.at[i % 2]
+        )
+
+    def tile_step(i):
+        left, right, _, row, col = tile_list[i]
+        if col == 0:
+            turned[...] = left[:, pl.ds(row, tile_rows)].T
+        if i >= 2:
+            store_tile(i - 2).wait()
+
+        def cols(n, carry):
+            there, put = rows_at(col + n * COLS, COLS), rows_at(n * COLS, COLS)
+            tiles[i % 2, :, put] = project(turned[...], right[:, there])
+            return carry
+
+        lax.fori_loop(0, tile_cols // COLS, cols, 0)
+        store_tile(i).start()
+
+    load(0, w_out_hbm, w_out).wait()
+    middle_step(0)
+    norm_step(0)
+    load(1, w_up_hbm, w_up).wait()
+    hidden_step(0)
+    produce()
+    line.meet()
+    load(5, cot_hbm, cot).wait()
+    steps = []
+    for c in range(1, blocks):
+        steps.append([functools.partial(f, c) for f in (middle_step, norm_step)])
+        steps.append([functools.partial(hidden_step, c)])
+    slots = (line.pieces + LATE) // SLOT
+    count = len(tile_list)
+    per = -(-count // max(slots - len(steps), 1))
+    for i in range(0, count, per):
+        steps.append([functools.partial(tile_step, j) for j in range(i, min(i + per, count))])
+    for i in range(max(slots, len(steps))):
+        if i < slots:
+            line.slot(i)
+        if i < len(steps):
+            for step in steps[i]:
+                step()
+    store_first = pltpu.make_async_copy(line.total, first_hbm, out_sem.at[3])
+    store_first.start()
+    store_tile(count - 2).wait()
+    store_tile(count - 1).wait()
+    store_mid(blocks - 1).wait()
+    store_acts.wait()
+    store_dh.wait()
+    store_first.wait()
+    line.finish()
+
+
+def mlp(mixed, w_out, inputs, w_up, d_acts, cotangent, b_out, gain, shift, b_up):
+    seq, width = inputs.shape
+    hidden = w_up.shape[1]
+    vmem = pl.BlockSpec(memory_space=pltpu.VMEM)
+    dma = pltpu.SemaphoreType.DMA
+    shape = jax.ShapeDtypeStruct
+    block = lambda cols, dtype: pltpu.VMEM((BLOCK, cols), dtype)
+    return pl.pallas_call(
+        mlp_kernel,
+        out_shape=(
+            shape((seq, width), F32),
+            shape((seq, hidden), BF16),
+            shape((seq, hidden), BF16),
+            shape((hidden, width), F32),
+            shape((width, hidden), F32),
+            shape((BLOCK, width), F32),
+            shape((8, hidden), F32),
+        ),
+        in_specs=[HBM] * 6 + [vmem] * 4,
+        out_specs=(HBM,) * 6 + (vmem,),
+        scratch_shapes=[
+            pltpu.VMEM(w_out.shape, BF16),
+            pltpu.VMEM(w_up.shape, BF16),
+            pltpu.VMEM((seq, width), BF16),
+            pltpu.VMEM((seq, hidden), BF16),
+            pltpu.VMEM((seq, hidden), BF16),
+            pltpu.VMEM((seq, width), BF16),
+            block(w_out.shape[0], BF16),
+            block(width, BF16),
+            block(width, F32),
+            block(hidden, F32),
+            pltpu.VMEM((2 * BLOCK, seq), BF16),
+            pltpu.VMEM((2, 2 * BLOCK, width // 2), F32),
+            dma((6,)),
+            dma((4,)),
+            dma((2,)),
+        ]
+        + LineSum.scratch(BLOCK, BLOCK // PIECE, width),
+        compiler_params=pltpu.CompilerParams(
+            collective_id=3, has_side_effects=True, vmem_limit_bytes=VMEM_LIMIT
+        ),
+        cost_estimate=pl.CostEstimate(flops=60 * 10**9, bytes_accessed=2**26, transcendentals=0),
+        name="mlp",
+    )(
+        mixed, w_out, inputs, w_up, d_acts, cotangent, b_out.reshape(1, width),
+        gain.reshape(1, width), shift.reshape(1, width), b_up.reshape(1, hidden),
+    )
+
+
 def mlp_attend_back_kernel(
     heads,
     dh_hbm, w_up_hbm, w_out_hbm, mid_hbm, cot_hbm, q_hbm, acts_hbm, w_down_hbm, normed_hbm, mixed_hbm,
-    kv_ref, kt_ref, code_ref, doc_ref, lse_ref, gain_ref,
-    d_mid_hbm, dq_hbm, feed_hbm, grads_hbm, dkv_ref, sums_ref,
+    first_hbm,
+    kv_ref, kt_ref, code_ref, doc_ref, lse_ref, gain_ref, b_down_ref,
+    d_mid_hbm, dq_hbm, feed_out, grads_hbm, dkv_ref, sums_ref,
     w_up, w_out, dh, mid, cot, q, normed, mixed, d_branch, d_mixed, dq, grads, bias_ref,
     load_sem, out_sem, *line_refs,
 ):
@@ -765,8 +988,8 @@
     def load(i, src, dst):
         return pltpu.make_async_copy(src, dst, load_sem.at[i])
 
-    def load_dh(c):
-        return load(2, dh_hbm.at[rows_at(c * BLOCK, BLOCK)], dh)
+    def load_dh(b):
+        return load(2, dh_hbm.at[rows_at((b + 1) * BLOCK, BLOCK)], dh)
 
     def load_chunk(c):
         at = rows_at(c * BLOCK, BLOCK)
@@ -778,8 +1001,10 @@
             load(7, mixed_hbm.at[at, own], mixed),
         ]
 
-    def block_at(c):
-        return rows_at((c % ring) * BLOCK, BLOCK)
+    def block_at(b):
+        return rows_at((b % ring) * BLOCK, BLOCK)
+
+    load_first = load(8, first_hbm, line.total.at[block_at(ring - 1)])
 
     def store(i, src, dst, c):
         return pltpu.make_async_copy(src, dst.at[rows_at(c * BLOCK, BLOCK)], out_sem.at[i])
@@ -791,17 +1016,25 @@
     load(0, w_up_hbm, w_up).start()
     load_dh(0).start()
     load(1, w_out_hbm, w_out).start()
-    load_acts = load(2, acts_hbm.at[pl.ds(0, BLOCK)], dh)
+    load_first.start()
     load_down = load(0, w_down_hbm, w_up)
-    load_mid = load(3, mid_hbm.at[pl.ds(0, BLOCK)], mid)
+
+    def load_acts(j):
+        return load(2, acts_hbm.at[rows_at(j * BLOCK, BLOCK)], dh)
+
+    def load_mid(j):
+        return load(3, mid_hbm.at[rows_at(j * BLOCK, BLOCK)], mid)
+
     line.greet()
     dkv_ref[...] = jnp.zeros_like(dkv_ref)
     sums_ref[...] = jnp.zeros_like(sums_ref)
     grads[...] = jnp.zeros_like(grads)
 
-    def produce(c):
-        at = block_at(c)
-        load_dh(c).wait()
+    lines = chunks - 1
+
+    def produce(b):
+        at = block_at(b)
+        load_dh(b).wait()
 
         def cols(n, carry):
             there = rows_at(n * COLS, COLS)
@@ -810,20 +1043,23 @@
 
         lax.fori_loop(0, width // COLS, cols, 0)
 
-        @pl.when(c + 1 < chunks)
-        def _():
-            load_dh(c + 1).start()
-
-        @pl.when(c + 1 == chunks)
-        def _():
-            load_acts.start()
+        @pl.when(b + 1 < lines)
+        def _():
+            load_dh(b + 1).start()
+
+        @pl.when(b + 1 == lines)
+        def _():
+            load_acts(0).start()
             load_down.start()
 
-    def produce_feed():
-        at = block_at(chunks)
-        load_acts.wait()
-        load_down.wait()
-        load_mid.wait()
+    def produce_feed(j):
+        at = block_at(lines + j)
+        load_acts(j).wait()
+        load_mid(j).wait()
+
+        @pl.when(j == 0)
+        def _():
+            load_down.wait()
 
         def cols(n, carry):
             there = rows_at(n * COLS, COLS)
@@ -835,6 +1071,10 @@
         @pl.when(m == 0)
         def _():
             line.part[at, :] += mid[...]
+
+        @pl.when(j + 1 < FEED_EARLY)
+        def _():
+            load_acts(j + 1).start()
 
     def add_grads(first, left, right):
         at = pl.ds(first, own_cols)
@@ -850,7 +1090,7 @@
         def strip(i, carry):
             row = half * (BLOCK // 2) + i * STRIP
             at = rows_at(row, STRIP)
-            grad = line.total[rows_at((c % ring) * BLOCK + row, STRIP), :]
+            grad = line.total[rows_at(((c + ring - 1) % ring) * BLOCK + row, STRIP), :]
             d_in, weighted = norm_back_rows(mid[at, :], grad, gain_ref[...])
             cot_rows = cot[at, :].astype(F32)
             d_mid = cot_rows + d_in
@@ -907,102 +1147,92 @@
     for k in range(3):
         line.slot(k)
     load(1, w_out_hbm, w_out).wait()
-
-    def cycle(u, carry):
-        c = u - 1
-        base = u * slots + 3
-
-        @pl.when(u >= 2)
-        def _():
-            for i in stores(u - 2):
+    load_first.wait()
+
+    def cycle(c, carry):
+        base = c * slots + 3
+
+        @pl.when(c >= 1)
+        def _():
+            for i in stores(c - 1):
                 i.wait()
 
-        @pl.when(u + 1 == chunks)
-        def _():
-            load_mid.start()
+        @pl.when(c + 1 >= lines)
+        def _():
+            load_mid(c + 1 - lines).start()
 
         line.slot(base)
 
-        @pl.when(u >= 2)
-        def _():
-            line.free((u - 2) * (BLOCK // PIECE), BLOCK // PIECE)
-
-        @pl.when(u + 1 < chunks)
-        def _():
-            produce(u + 1)
-
-        @pl.when(u + 1 == chunks)
-        def _():
-            produce_feed()
-
-        @pl.when(u >= 1)
-        def _():
-            for i in load_chunk(c):
-                i.start()
-
+        @pl.when(c >= 2)
+        def _():
+            line.free((c - 2) * (BLOCK // PIECE), BLOCK // PIECE)
+
+        @pl.when(c + 1 < lines)
+        def _():
+            produce(c + 1)
+
+        @pl.when(c + 1 >= lines)
+        def _():
+            produce_feed(c + 1 - lines)
+
+        for i in load_chunk(c):
+            i.start()
         line.slot(base + 1)
-
-        @pl.when(u >= 1)
-        def _():
-            for i in load_chunk(c):
-                i.wait()
-            norm_step(c, 0)
-
+        for i in load_chunk(c):
+            i.wait()
+        norm_step(c, 0)
         line.slot(base + 2)
-
-        @pl.when(u >= 1)
-        def _():
-            norm_step(c, 1)
-            stores(c, (0,))[0].start()
-
+        norm_step(c, 1)
+        stores(c, (0,))[0].start()
         line.slot(base + 3)
-
-        @pl.when(u >= 1)
-        def _():
-            mixed_step(c)
-            add_grads(own_cols, mixed[...], d_branch)
+        mixed_step(c)
+        add_grads(own_cols, mixed[...], d_branch)
 
         def some_heads(g, carry):
             line.slot(base + 4 + g)
-
-            @pl.when(u >= 1)
-            def _():
-                heads_step(c, g)
-
+            heads_step(c, g)
             return carry
 
         lax.fori_loop(0, heads // GROUP, some_heads, 0)
-
-        @pl.when(u >= 1)
-        def _():
-            stores(c, (1,))[0].start()
-            add_grads(0, dq[:, own], normed)
-
-            def strip(i, carry):
-                sums_ref[4] += fold_rows(dq[rows_at(i * STRIP, STRIP), :].astype(F32))
-                return carry
-
-            lax.fori_loop(0, BLOCK // STRIP, strip, 0)
-
+        stores(c, (1,))[0].start()
+        add_grads(0, dq[:, own], normed)
+
+        def strip(i, carry):
+            sums_ref[4] += fold_rows(dq[rows_at(i * STRIP, STRIP), :].astype(F32))
+            return carry
+
+        lax.fori_loop(0, BLOCK // STRIP, strip, 0)
         return carry
 
-    lax.fori_loop(0, chunks + 1, cycle, 0)
-    for k in range((chunks + 1) * slots + 3, (line.pieces + LATE) // SLOT):
-        line.slot(k)
+    lax.fori_loop(0, chunks, cycle, 0)
     keep_grads = pltpu.make_async_copy(grads, grads_hbm, out_sem.at[3])
     keep_grads.start()
-    keep_feed = pltpu.make_async_copy(line.total.at[block_at(chunks)], feed_hbm, out_sem.at[2])
-    keep_feed.start()
+    for k in range(chunks * slots + 3, (line.pieces + LATE) // SLOT):
+        line.slot(k)
     for i in stores(chunks - 1):
         i.wait()
-    keep_feed.wait()
+    keep_feed = []
+    for j, low in enumerate((d_branch, d_mixed)):
+
+        def strip(i, carry, j=j, low=low):
+            total = line.total[rows_at((lines + j) % ring * BLOCK + i * STRIP, STRIP), :]
+            low[rows_at(i * STRIP, STRIP), :] = (total + b_down_ref[...]).astype(BF16)
+            return carry
+
+        lax.fori_loop(0, BLOCK // STRIP, strip, 0)
+        keep_feed.append(
+            pltpu.make_async_copy(low, feed_out.at[pl.ds(j * BLOCK, BLOCK)], out_sem.at[j])
+        )
+        keep_feed[j].start()
+    for i in keep_feed:
+        i.wait()
     keep_grads.wait()
-    line.finish((chunks - 1) * (BLOCK // PIECE))
+    line.finish((lines - 1) * (BLOCK // PIECE))
 
 
 def mlp_attend_back(
-    d_hidden, w_up, w_out, middle, cotangent, queries, acts, w_down, normed, mixed, own_cols,
-    keyval, keys_t, code_col, doc_row, lse, gain,
+    d_hidden, w_up, w_out, middle, cotangent, queries, acts, w_down, normed, mixed, first, own_cols,
+    keyval, keys_t, code_col, doc_row, lse, gain, b_down,
 ):
     seq, width = queries.shape
     heads = width // keys_t.shape[0]
@@ -1014,12 +1244,12 @@
         out_shape=(
             jax.ShapeDtypeStruct((seq, width), F32),
             jax.ShapeDtypeStruct((seq, width), BF16),
-            jax.ShapeDtypeStruct((BLOCK, width), F32),
+            jax.ShapeDtypeStruct((FEED_EARLY * BLOCK, width), BF16),
             jax.ShapeDtypeStruct((2 * own_cols, width), F32),
             jax.ShapeDtypeStruct(keyval.shape, F32),
             jax.ShapeDtypeStruct((5, 8, width), F32),
         ),
-        in_specs=[HBM] * 10 + [vmem] * 6,
+        in_specs=[HBM] * 11 + [vmem] * 7,
         out_specs=(HBM, HBM, HBM, HBM, vmem, vmem),
         scratch_shapes=[
             pltpu.VMEM(w_up.shape, BF16),
@@ -1035,10 +1265,10 @@
             block(BF16),
             pltpu.VMEM((2 * own_cols, width), F32),
             pltpu.VMEM((REACH * BLOCK, BLOCK), F32),
-            dma((8,)),
+            dma((9,)),
             dma((4,)),
         ]
-        + LineSum.scratch(min(3 * BLOCK, seq), (seq + BLOCK) // PIECE, width),
+        + LineSum.scratch(seq - BLOCK, (seq + (FEED_EARLY - 1) * BLOCK) // PIECE, width),
         compiler_params=pltpu.CompilerParams(
             collective_id=1, has_side_effects=True, vmem_limit_bytes=VMEM_LIMIT
         ),
@@ -1047,14 +1277,14 @@
         ),
         name="mlp_attend_back",
     )(
-        d_hidden, w_up, w_out, middle, cotangent, queries, acts, w_down, normed, mixed,
-        keyval, keys_t, code_col, doc_row, lse, gain.reshape(1, width),
+        d_hidden, w_up, w_out, middle, cotangent, queries, acts, w_down, normed, mixed, first,
+        keyval, keys_t, code_col, doc_row, lse, gain.reshape(1, width), b_down.reshape(1, width),
     )
 
 
 def feed_kernel(
     rounds,
-    acts_hbm, w_down_hbm, mid_hbm, dq_hbm, w_q_hbm, in_hbm, d_mid_hbm, normed_hbm, first_hbm,
+    acts_hbm, w_down_hbm, mid_hbm, dq_hbm, w_q_hbm, in_hbm, d_mid_hbm, normed_hbm,
     dkv_f_ref, w_kv_ref, gain_ref, bias_ref, sums_in, b_up_in,
     out_hbm, in_grad_hbm, table_out, vectors_out,
     w_down, w_q, acts, mid, dq, xs, d_mid, spread, low, in_grad, normed, dkv_ref, sums, trade, trade_in, table, table_in, table_all,
@@ -1062,7 +1292,7 @@
 ):
     line = LineSum(line_refs)
     rows, width = line.part.shape
-    seq = rows + BLOCK
+    seq = rows + FEED_EARLY * BLOCK
     blocks = seq // BLOCK
     chunks = rows // BLOCK
     slots = BLOCK // (PIECE * SLOT)
@@ -1075,7 +1305,7 @@
         return pltpu.make_async_copy(src, dst, load_sem.at[i])
 
     def load_feed(c):
-        at = rows_at((c + 1) * BLOCK, BLOCK)
+        at = rows_at((c + FEED_EARLY) * BLOCK, BLOCK)
         return [load(2, acts_hbm.at[at], acts), load(3, mid_hbm.at[at], mid)]
 
     def load_grad(c):
@@ -1092,11 +1322,9 @@
     def load_normed(c):
         return load(7, normed_hbm.at[rows_at(c * BLOCK, BLOCK)], normed)
 
-    load_first = load(8, first_hbm, spread)
     load(0, w_down_hbm, w_down).start()
     for i in load_feed(0):
         i.start()
-    load_first.start()
     load_normed(0).start()
     load(1, w_q_hbm, w_q).start()
     for i in load_grad(0):
@@ -1122,16 +1350,15 @@
         def _():
             line.part[at, :] += mid[...]
 
-        @pl.when(c + 1 < chunks)
-        def _():
+        if c + 1 < chunks:
             for i in load_feed(c + 1):
                 i.start()
 
-    def output_step(source, c):
+    def output_step(c):
         def strip(i, carry):
             at = rows_at(i * STRIP, STRIP)
             there = rows_at(c * BLOCK + i * STRIP, STRIP)
-            low[at, :] = (source[there, :] + bias_ref[...]).astype(BF16)
+            low[at, :] = (line.total[there, :] + bias_ref[...]).astype(BF16)
             return carry
 
         lax.fori_loop(0, BLOCK // STRIP, strip, 0)
@@ -1149,9 +1376,9 @@
 
         lax.fori_loop(0, width // COLS, cols, 0)
 
-    def norm_step(c, half):
+    def norm_step(c):
         def strip(i, carry):
-            at = rows_at(half * (BLOCK // 2) + i * STRIP, STRIP)
+            at = rows_at(i * STRIP, STRIP)
             grad = spread[at, :]
             d_in, weighted = norm_back_rows(xs[at, :].astype(F32), grad, gain_ref[...])
             in_grad[at, :] = (d_mid[at, :] + d_in).astype(BF16)
@@ -1159,7 +1386,7 @@
             sums[1] += fold_rows(grad)
             return carry
 
-        lax.fori_loop(0, BLOCK // 2 // STRIP, strip, 0)
+        lax.fori_loop(0, BLOCK // STRIP, strip, 0)
 
     def swap(r):
         return pltpu.make_async_remote_copy(
@@ -1253,87 +1480,49 @@
         line.slot(k)
     load(1, w_q_hbm, w_q).wait()
 
-    def grads(u, first):
-        v = 2 * u + (0 if first else 1)
-
-        def one():
-            @pl.when(v < blocks)
-            def _():
-                for i in load_grad(v):
-                    i.wait()
-                spread_step(v)
-
-        def two():
-            @pl.when(v < blocks)
-            def _():
-                @pl.when(v >= 1)
-                def _():
-                    store(1, in_grad, in_grad_hbm, v - 1).wait()
-
-                norm_step(v, 0)
-
-        def three():
-            @pl.when(v < blocks)
-            def _():
-                norm_step(v, 1)
-                store(1, in_grad, in_grad_hbm, v).start()
-
-                @pl.when(v + 1 < blocks)
-                def _():
-                    for i in load_grad(v + 1):
-                        i.start()
-
-        return one, two, three
-
-    def cycle(u, carry):
-        c = u - 1
-        base_tick = u * slots + 3
-
-        def produce_step():
-            @pl.when(u + 1 < chunks)
-            def _():
-                produce(u + 1)
-
-        def out_step():
-            @pl.when(u == 0)
-            def _():
-                load_first.wait()
-                output_step(spread, 0)
-                store(0, low, out_hbm, 0).start()
-
-            @pl.when(u >= 1)
-            def _():
-                store(0, low, out_hbm, u - 1).wait()
-                output_step(line.total, c)
-                store(0, low, out_hbm, u).start()
-
-        steps = [produce_step, out_step, *grads(u, True), *grads(u, False)]
-        for i, step in enumerate(steps):
-            line.slot(base_tick + i)
-            for v in range(chunks + 1):
-                at = v * slots + i
-                extra = []
-                if at % 2 == 0 and at // 2 < blocks:
-                    extra.append(functools.partial(table_block, at // 2))
-                if at % 2 == 0 and 0 <= at // 2 - blocks <= 2 * rounds:
-                    extra.append(functools.partial(table_step, at // 2 - blocks))
-                late = at - (blocks // 2) * slots
-                if late == 0:
-                    extra.append(vectors_first)
-                elif 0 < late <= rounds:
-                    extra.append(functools.partial(vectors_next, late - 1))
-                if extra:
-
-                    @pl.when(u == v)
-                    def _(extra=extra):
-                        for e in extra:
-                            e()
-
+    def spread_block(v):
+        for i in load_grad(v):
+            i.wait()
+        spread_step(v)
+
+    def norm_block(v):
+        if v >= 1:
+            store(1, in_grad, in_grad_hbm, v - 1).wait()
+        norm_step(v)
+        store(1, in_grad, in_grad_hbm, v).start()
+        if v + 1 < blocks:
+            for i in load_grad(v + 1):
+                i.start()
+
+    def output_block(c):
+        if c >= 1:
+            store(0, low, out_hbm, c - 1).wait()
+        output_step(c)
+        store(0, low, out_hbm, c).start()
+
+    slot_count = (line.pieces + LATE) // SLOT
+    steps = [[] for _ in range(max(slot_count, 4 * blocks + 8))]
+    for c in range(1, chunks):
+        steps[(c - 1) * slots + 3].append(functools.partial(produce, c))
+    for c in range(chunks):
+        steps[(c + 1) * slots - 1 + LATE // SLOT].append(functools.partial(output_block, c))
+    for v in range(blocks):
+        steps[3 + 2 * v].append(functools.partial(spread_block, v))
+        steps[4 + 2 * v].append(functools.partial(norm_block, v))
+        steps[2 + 2 * v].append(functools.partial(table_block, v))
+    done = 4 + 2 * blocks
+    for i in range(rounds + 1):
+        steps[done + i].append(vectors_first if i == 0 else functools.partial(vectors_next, i - 1))
+    first = 1 + 2 * blocks
+    apart = max(1, min(2, (len(steps) - 1 - first) // (2 * rounds)))
+    for i in range(2 * rounds + 1):
+        steps[first + i * apart].append(functools.partial(table_step, i))
+    for i, todo in enumerate(steps):
+        if i >= 3 and i < slot_count:
+            line.slot(i)
+        for step in todo:
             step()
-        return carry
-
-    lax.fori_loop(0, chunks + 1, cycle, 0)
-    store(0, low, out_hbm, chunks).wait()
+    store(0, low, out_hbm, chunks - 1).wait()
     store(1, in_grad, in_grad_hbm, blocks - 1).wait()
     store_table.wait()
     line.finish()
@@ -1341,25 +1530,25 @@
 
 def feed_and_input_grad(
     acts, w_down, middle, b_down, d_queries, all_query, d_keyval_sum, w_keyval, inputs, d_middle, gain,
-    normed, feed_first, sums, b_up,
+    normed, sums, b_up,
 ):
     seq, width = inputs.shape
     rounds = (lax.axis_size("dp") - 1).bit_length()
     vmem = pl.BlockSpec(memory_space=pltpu.VMEM)
     dma = pltpu.SemaphoreType.DMA
     block = lambda dtype: pltpu.VMEM((BLOCK, width), dtype)
-    rest = seq - BLOCK
+    rest = seq - FEED_EARLY * BLOCK
     shape = jax.ShapeDtypeStruct
     table = (w_keyval.shape[1], width)
     return pl.pallas_call(
         functools.partial(feed_kernel, rounds),
         out_shape=(
-            shape((seq, width), BF16),
+            shape((rest, width), BF16),
             shape((seq, width), BF16),
             shape(table, F32),
             shape((16, width), F32),
         ),
-        in_specs=[HBM] * 9 + [vmem] * 6,
+        in_specs=[HBM] * 8 + [vmem] * 6,
         out_specs=(HBM, HBM, HBM, vmem),
         scratch_shapes=[
             pltpu.VMEM(w_down.shape, BF16),
@@ -1380,7 +1569,7 @@
             pltpu.VMEM(table, F32),
             pltpu.VMEM(table, F32),
             pltpu.VMEM(table, F32),
-            dma((9,)),
+            dma((8,)),
             dma((3,)),
             dma((rounds,)),
             dma((rounds,)),
@@ -1394,11 +1583,11 @@
             collective_id=2, has_side_effects=True, vmem_limit_bytes=VMEM_LIMIT
         ),
         cost_estimate=pl.CostEstimate(
-            flops=200 * 10**9, bytes_accessed=2**25, transcendentals=0
+            flops=150 * 10**9, bytes_accessed=2**25, transcendentals=0
         ),
         name="feed_and_input_grad",
     )(
-        acts, w_down, middle, d_queries, all_query, inputs, d_middle, normed, feed_first,
+        acts, w_down, middle, d_queries, all_query, inputs, d_middle, normed,
         d_keyval_sum, w_keyval, gain.reshape(1, width), b_down.reshape(1, width), sums,
         b_up.reshape(1, width),
     )
@@ -1429,7 +1618,6 @@
     width = inputs.shape[1]
     own_cols = w_query.shape[1]
     own = lax.axis_index("mp") * own_cols
-    inputs_f = inputs.astype(F32)
     docs = doc_ids[0]
     codes = jnp.where(pad_mask[0] == 1, docs, -1)
     code_col = jnp.pad(codes, (FRONT, 0), constant_values=-2).reshape(-1, 1)
@@ -1439,29 +1627,24 @@
         inputs, w_query, b_query, w_keyval, b_value, w_out, attn_gain, attn_shift, code_col, doc_row,
         cotangent, w_down,
     )
-    middle = inputs_f + project(mixed, all_out) + b_out
-    normed_mlp = norm_rows(middle, mlp_gain, mlp_shift).astype(BF16)
-    hidden = project(normed_mlp, w_up) + b_up
-    acts = jax.nn.gelu(hidden, approximate=True).astype(BF16)
-    grad_w_down = jnp.einsum("tf,td->fd", acts, cotangent, preferred_element_type=F32)
-    _, gelu_pull = jax.vjp(functools.partial(jax.nn.gelu, approximate=True), hidden)
-    d_hidden = gelu_pull(d_acts)[0].astype(BF16)
-    grad_b_up = jnp.sum(d_hidden.astype(F32), axis=0)
-    grad_w_up = jnp.einsum("td,tf->df", normed_mlp, d_hidden, preferred_element_type=F32)
-    d_hidden, grad_w_up, grad_w_down = lax.optimization_barrier((d_hidden, grad_w_up, grad_w_down))
+    middle, acts, d_hidden, grad_w_down, grad_w_up, first, grad_b_up = mlp(
+        mixed, all_out, inputs, w_up, d_acts, cotangent, b_out, mlp_gain, mlp_shift, b_up
+    )
+    grad_b_up = jnp.sum(grad_b_up, axis=0)
     grad_w_up = lax.psum_scatter(grad_w_up, "dp", scatter_dimension=0, tiled=True)
     grad_w_down = lax.psum_scatter(grad_w_down, "dp", scatter_dimension=1, tiled=True)
 
-    d_middle, d_queries, feed_first, grads, d_keyval_sum, sums = mlp_attend_back(
-        d_hidden, w_up, all_out, middle, cotangent, queries, acts, w_down, normed_attn, mixed, own_cols,
-        keyval, keys_t, code_col, doc_row, lse, mlp_gain,
+    d_middle, d_queries, out_first, grads, d_keyval_sum, sums = mlp_attend_back(
+        d_hidden, w_up, all_out, middle, cotangent, queries, acts, w_down, normed_attn, mixed, first, own_cols,
+        keyval, keys_t, code_col, doc_row, lse, mlp_gain, b_down,
     )
     grads, grad_w_down, grad_w_up = lax.optimization_barrier((grads, grad_w_down, grad_w_up))
     grads = lax.psum_scatter(grads, "dp", scatter_dimension=1, tiled=True)
-    outputs, input_grad, grad_w_keyval, totals = feed_and_input_grad(
+    out_rest, input_grad, grad_w_keyval, totals = feed_and_input_grad(
         acts, w_down, middle, b_down, d_queries, all_query, d_keyval_sum, w_keyval, inputs, d_middle,
-        attn_gain, normed_attn, feed_first, sums, grad_b_up,
+        attn_gain, normed_attn, sums, grad_b_up,
     )
+    outputs = jnp.concatenate([out_first, out_rest], 0)
     grad_w_query, grad_w_out = grads[:own_cols].T, grads[own_cols:]
     grad_w_keyval = grad_w_keyval.T
     grad_attn_gain, grad_attn_shift, grad_mlp_gain, grad_mlp_shift = (totals[i] for i in range(4))

time: 673 us -> 646 us (0.960)
  matrix products: 67.7 us -> 0 us
  Pallas kernels: 561 us -> 599 us
    pallas_call x0 -> x1, Pallas kernels: none -> 87.3 us  [mlp(): pl.pallas_call(mlp_kernel, out_shape=(shape((seq, width), F32), shape((se...]
    dot_general x4 -> x0, matrix products: 67.7 us -> none  [the longest x2 37.4 us: project(): return jnp.dot(left, right, preferred_element_type=F32)]
    pallas_call x1, Pallas kernels: 166 us -> 123 us  [feed_and_input_grad(): pl.pallas_call(functools.partial(feed_kernel, rounds), out_shape=(shape((...]
  transfers between devices with their start and end apart: 3 -> 3, of which waited for: 0 -> 0; matrix products, arithmetic and copies ran while one was open for 1% -> 2% of each run, Pallas kernels for 65% -> 60%
where the time goes in v4:
time: 646 us; the launch traced here: 634 us
  Pallas kernels  599 us (93%)
  between operations  14.3 us (2%)
  local copies, waits for them, and re-layouts  13.9 us (2%)
    pallas_call x1, Pallas kernels, mlp_attend_back(): pl.pallas_call(functools.partial(mlp_attend_back_kernel, heads), out_shap...  257 us
    pallas_call x1, Pallas kernels, attention_front(): pl.pallas_call(functools.partial(front_kernel, heads), out_shape=(shape(f...  133 us
    pallas_call x1, Pallas kernels, feed_and_input_grad(): pl.pallas_call(functools.partial(feed_kernel, rounds), out_shape=(shape((...  123 us
    pallas_call x1, Pallas kernels, mlp(): pl.pallas_call(mlp_kernel, out_shape=(shape((seq, width), F32), shape((se...  87.3 us
  transfers between devices with their start and end apart: 3, of which 0 were waited for; matrix products, arithmetic and copies ran while one was open for 2% of the time, Pallas kernels for 60%

profile of v4, /device:TPU:0, one launch (start us, length us, event | category | flops | bytes accessed | tf_op | source)
XLA Modules:
  0.0 633.9 jit_solution(10049771363429141921)
XLA Ops:
  7.2 0.0 reduce-scatter.4.cloned.1.call-start
  7.2 0.7 compare_select_fusion
  7.9 1.2 reshape.100.code_ref
  9.1 132.7 %attention_front.1 = (bf16[4,8,256,512]{3,2,1,0:T(8,128)(2,1)}, bf16[4,8,64,2048]{3,2,1,0:T(8,128)(2,1)}, bf16[1024,2048]{1,0:T(8,128)(2,1)}, bf16[1024,2048]{1,...) custom-call(bf16[8,256,512]{2,1,0:T(8,128)(2,1)} %bitcast.28, ...), custom_call_target="tpu_custom_call" | custom-call | tf_op jit(solution)/shard_map/attention_front/pallas_call | solution.py:475
  141.8 87.3 %mlp.1 = (f32[1024,2048]{1,0:T(8,128)}, bf16[1024,2048]{1,0:T(8,128)(2,1)}, bf16[1024,2048]{1,0:T(8,128)(2,1)}, f32[2048,2048]{1,0:T(8,128)}, f32[2048,2048]{1,0...) custom-call(bf16[1024,2048]{1,0:T(8,128)(2,1)} %get-tuple-element.45.mixed_hbm, bf16[2048,2048]{1,0:T(8,128)(2,1)} %bitcast.47, ...), custom_call_target="tpu_custom_call" | custom-call | flops 60000002048 | bytes 67108864 | tf_op jit(solution)/shard_map/mlp/pallas_call | solution.py:925
  229.1 0.0 reduce-scatter.4.cloned.1.call-update
  229.1 0.0 reduce-scatter.6.cloned.1.call-start
  229.2 0.0 copy-start.1
  229.2 0.7 reduce-scatter.6.cloned.1.call-update
  229.9 0.0 reduce-scatter.8.cloned.1.call-start
  229.9 0.1 copy-done.1
  230.0 0.6 reduce_sum.9
  230.6 256.7 %mlp_attend_back.1 = (f32[1024,2048]{1,0:T(8,128)}, bf16[1024,2048]{1,0:T(8,128)(2,1)}, bf16[512,2048]{1,0:T(8,128)(2,1)}, f32[1024,2048]{1,0:T(8,128)}, f32[1536,256]{1,0:T(8,128)}, /*index=5*/f32[5,8,2048]{2,1,0:T(8,128)}) custom-call(bf16[1024,2048]{1,0:T(8,128)(2,1)} %get-tuple-element.48.dh_hbm, bf16[2048,2048]{1,0:T(8,128)(2,1)} %w_up_hbm.3, ...), custom_call_target="tpu_custom_call" | custom-call | flops 199999995904 | bytes 33554432 | tf_op jit(solution)/shard_map/mlp_attend_back/pallas_call | solution.py:1242
  487.4 0.0 reduce-scatter.4.cloned.1.call-done
  487.4 0.0 reduce-scatter.6.cloned.1.call-done
  487.5 0.0 reduce-scatter.8.cloned.1.call-update
  487.5 122.7 %feed_and_input_grad.1 = (bf16[512,2048]{1,0:T(8,128)(2,1)}, bf16[1024,2048]{1,0:T(8,128)(2,1)}, f32[256,2048]{1,0:T(8,128)}, f32[16,2048]{1,0:T(8,128)}) custom-call(bf16[1024,2048]{1,0:T(8,128)(2,1)} %get-tuple-element.51.acts_hbm, bf16[2048,2048]{1,0:T(8,128)(2,1)} %w_down_hbm.5, f32[1024,2048]{1,0:T(8,128)} %get-tuple-element.49.mid_hbm, ...), custom_call_target="tpu_custom_call" | custom-call | flops 149999992832 | bytes 33554432 | tf_op jit(solution)/shard_map/feed_and_input_grad/pallas_call | solution.py:1543
  610.1 0.0 copy-start.2
  610.2 0.0 copy-start
  610.2 3.0 copy.39
  613.2 0.0 copy-done.2
  613.2 0.7 fusion.1
  613.9 0.6 constant_dynamic-slice_fusion
  614.4 0.5 slice_bitcast_fusion.1
  615.0 0.0 copy-done
  615.0 4.2 pad_maximum_fusion
  619.1 0.0 reduce-scatter.8.cloned.1.call-done
  619.1 2.1 fusion
  621.2 1.0 copy.38
  622.2 4.8 copy.41
  (1 shorter events, 0.0 us)
Async XLA Ops:
  7.2 480.2 %reduce-scatter.4.cloned.1.call-start = ((), (), s32[]{:S(2)}) async-start(), calls=%async_computation.3 | async-start | bytes 18874368 | tf_op jit(solution)/shard_map/reduce_scatter | solution.py:1635
  229.1 258.3 %reduce-scatter.6.cloned.1.call-start = ((), (), s32[]{:S(2)}) async-start(), calls=%async_computation.4 | async-start | bytes 18874368 | tf_op jit(solution)/shard_map/reduce_scatter | solution.py:1634
  229.2 0.8 copy-start.1
  229.9 389.2 %reduce-scatter.8.cloned.1.call-start = ((), (), s32[]{:S(2)}) async-start(), calls=%async_computation.5 | async-start | bytes 9437184 | tf_op jit(solution)/shard_map/reduce_scatter | solution.py:1642
  610.1 3.1 copy-start.2
  610.2 4.8 copy-start
Sparse Core Ops, SparseCore 0:
  229.3 119.7 reduce-scatter.3
  353.2 115.9 reduce-scatter.5
  487.6 73.1 reduce-scatter.7

commit v5 on v4

--- a/solution.py
+++ b/solution.py
@@ -759,7 +759,7 @@
 def mlp_kernel(
     mixed_hbm, w_out_hbm, in_hbm, w_up_hbm, d_acts_hbm, cot_hbm,
     b_out_ref, gain_ref, shift_ref, b_up_ref,
-    mid_hbm, acts_hbm, dh_hbm, down_hbm, up_hbm, first_hbm, b_up_sum,
+    mid_hbm, acts_hbm, dh_hbm, down_hbm, up_hbm, first_hbm, next_hbm, b_up_sum,
     w_out, w_up, normed, acts, dh, cot, mixed, xs, mid, d_acts, turned, tiles,
     load_sem, out_sem, tile_sem, *line_refs,
 ):
@@ -845,13 +845,20 @@
             store_acts.start()
             store_dh.start()
 
-    def produce():
+    def produce(c, part):
         def cols(n, carry):
             there = rows_at(n * COLS, COLS)
-            line.part[:, there] = dot_t(dh[pl.ds(0, BLOCK), :], w_up[there, :])
+            part[:, there] = dot_t(dh[pl.ds(c * BLOCK, BLOCK), :], w_up[there, :])
             return carry
 
         lax.fori_loop(0, width // COLS, cols, 0)
+
+    store_next = pltpu.make_async_copy(mid, next_hbm, out_sem.at[0])
+
+    def produce_next():
+        store_mid(blocks - 1).wait()
+        produce(1, mid)
+        store_next.start()
 
     tile_rows, tile_cols = tiles.shape[1:]
     tile_list = []
@@ -886,13 +893,14 @@
     norm_step(0)
     load(1, w_up_hbm, w_up).wait()
     hidden_step(0)
-    produce()
+    produce(0, line.part)
     line.meet()
     load(5, cot_hbm, cot).wait()
     steps = []
     for c in range(1, blocks):
         steps.append([functools.partial(f, c) for f in (middle_step, norm_step)])
         steps.append([functools.partial(hidden_step, c)])
+    steps[-1].append(produce_next)
     slots = (line.pieces + LATE) // SLOT
     count = len(tile_list)
     per = -(-count // max(slots - len(steps), 1))
@@ -908,7 +916,7 @@
     store_first.start()
     store_tile(count - 2).wait()
     store_tile(count - 1).wait()
-    store_mid(blocks - 1).wait()
+    store_next.wait()
     store_acts.wait()
     store_dh.wait()
     store_first.wait()
@@ -931,10 +939,11 @@
             shape((hidden, width), F32),
             shape((width, hidden), F32),
             shape((BLOCK, width), F32),
+            shape((BLOCK, width), F32),
             shape((8, hidden), F32),
         ),
         in_specs=[HBM] * 6 + [vmem] * 4,
-        out_specs=(HBM,) * 6 + (vmem,),
+        out_specs=(HBM,) * 7 + (vmem,),
         scratch_shapes=[
             pltpu.VMEM(w_out.shape, BF16),
             pltpu.VMEM(w_up.shape, BF16),
@@ -967,9 +976,9 @@
 def mlp_attend_back_kernel(
     heads,
     dh_hbm, w_up_hbm, w_out_hbm, mid_hbm, cot_hbm, q_hbm, acts_hbm, w_down_hbm, normed_hbm, mixed_hbm,
-    first_hbm,
+    first_hbm, second_hbm,
     kv_ref, kt_ref, code_ref, doc_ref, lse_ref, gain_ref, b_down_ref,
-    d_mid_hbm, dq_hbm, feed_out, grads_hbm, dkv_ref, sums_ref,
+    d_mid_hbm, dq_hbm, feed_out, feed_next, grads_hbm, dkv_ref, sums_ref,
     w_up, w_out, dh, mid, cot, q, normed, mixed, d_branch, d_mixed, dq, grads, bias_ref,
     load_sem, out_sem, *line_refs,
 ):
@@ -1013,8 +1022,10 @@
         pairs = ((mid, d_mid_hbm), (dq, dq_hbm))
         return [store(i, *pairs[i], c) for i in which]
 
+    load_second = load(9, second_hbm, line.part.at[block_at(0)])
+    load_second.start()
     load(0, w_up_hbm, w_up).start()
-    load_dh(0).start()
+    load_dh(1).start()
     load(1, w_out_hbm, w_out).start()
     load_first.start()
     load_down = load(0, w_down_hbm, w_up)
@@ -1072,9 +1083,7 @@
         def _():
             line.part[at, :] += mid[...]
 
-        @pl.when(j + 1 < FEED_EARLY)
-        def _():
-            load_acts(j + 1).start()
+        load_acts(j + 1).start()
 
     def add_grads(first, left, right):
         at = pl.ds(first, own_cols)
@@ -1141,11 +1150,11 @@
         dkv_ref[keys, pl.ds(0, hd)] += dk * scale
         dkv_ref[keys, pl.ds(hd, hd)] += dv
 
-    load(0, w_up_hbm, w_up).wait()
-    produce(0)
+    load_second.wait()
     line.meet()
     for k in range(3):
         line.slot(k)
+    load(0, w_up_hbm, w_up).wait()
     load(1, w_out_hbm, w_out).wait()
     load_first.wait()
 
@@ -1207,10 +1216,25 @@
     lax.fori_loop(0, chunks, cycle, 0)
     keep_grads = pltpu.make_async_copy(grads, grads_hbm, out_sem.at[3])
     keep_grads.start()
+
+    stores(chunks - 1, (0,))[0].wait()
+    load_mid(FEED_EARLY).start()
+    load_acts(FEED_EARLY).wait()
+    load_mid(FEED_EARLY).wait()
+    share = jnp.where(m == 0, 1.0, 0.0)
+
+    def next_cols(n, carry):
+        there = rows_at(n * COLS, COLS)
+        mid[:, there] = project(dh[...], w_up[:, there]) + mid[:, there] * share
+        return carry
+
+    lax.fori_loop(0, width // COLS, next_cols, 0)
+    keep_next = pltpu.make_async_copy(mid, feed_next, out_sem.at[2])
+    keep_next.start()
     for k in range(chunks * slots + 3, (line.pieces + LATE) // SLOT):
         line.slot(k)
-    for i in stores(chunks - 1):
-        i.wait()
+    keep_next.wait()
+    stores(chunks - 1, (1,))[0].wait()
     keep_feed = []
     for j, low in enumerate((d_branch, d_mixed)):
 
@@ -1231,7 +1255,7 @@
 
 
 def mlp_attend_back(
-    d_hidden, w_up, w_out, middle, cotangent, queries, acts, w_down, normed, mixed, first, own_cols,
+    d_hidden, w_up, w_out, middle, cotangent, queries, acts, w_down, normed, mixed, first, second, own_cols,
     keyval, keys_t, code_col, doc_row, lse, gain, b_down,
 ):
     seq, width = queries.shape
@@ -1245,12 +1269,13 @@
             jax.ShapeDtypeStruct((seq, width), F32),
             jax.ShapeDtypeStruct((seq, width), BF16),
             jax.ShapeDtypeStruct((FEED_EARLY * BLOCK, width), BF16),
+            jax.ShapeDtypeStruct((BLOCK, width), F32),
             jax.ShapeDtypeStruct((2 * own_cols, width), F32),
             jax.ShapeDtypeStruct(keyval.shape, F32),
             jax.ShapeDtypeStruct((5, 8, width), F32),
         ),
-        in_specs=[HBM] * 11 + [vmem] * 7,
-        out_specs=(HBM, HBM, HBM, HBM, vmem, vmem),
+        in_specs=[HBM] * 12 + [vmem] * 7,
+        out_specs=(HBM, HBM, HBM, HBM, HBM, vmem, vmem),
         scratch_shapes=[
             pltpu.VMEM(w_up.shape, BF16),
             pltpu.VMEM(w_out.shape, BF16),
@@ -1265,7 +1290,7 @@
             block(BF16),
             pltpu.VMEM((2 * own_cols, width), F32),
             pltpu.VMEM((REACH * BLOCK, BLOCK), F32),
-            dma((9,)),
+            dma((10,)),
             dma((4,)),
         ]
         + LineSum.scratch(seq - BLOCK, (seq + (FEED_EARLY - 1) * BLOCK) // PIECE, width),
@@ -1277,14 +1302,14 @@
         ),
         name="mlp_attend_back",
     )(
-        d_hidden, w_up, w_out, middle, cotangent, queries, acts, w_down, normed, mixed, first,
+        d_hidden, w_up, w_out, middle, cotangent, queries, acts, w_down, normed, mixed, first, second,
         keyval, keys_t, code_col, doc_row, lse, gain.reshape(1, width), b_down.reshape(1, width),
     )
 
 
 def feed_kernel(
     rounds,
-    acts_hbm, w_down_hbm, mid_hbm, dq_hbm, w_q_hbm, in_hbm, d_mid_hbm, normed_hbm,
+    acts_hbm, w_down_hbm, mid_hbm, dq_hbm, w_q_hbm, in_hbm, d_mid_hbm, normed_hbm, next_hbm,
     dkv_f_ref, w_kv_ref, gain_ref, bias_ref, sums_in, b_up_in,
     out_hbm, in_grad_hbm, table_out, vectors_out,
     w_down, w_q, acts, mid, dq, xs, d_mid, spread, low, in_grad, normed, dkv_ref, sums, trade, trade_in, table, table_in, table_all,
@@ -1322,9 +1347,12 @@
     def load_normed(c):
         return load(7, normed_hbm.at[rows_at(c * BLOCK, BLOCK)], normed)
 
+    load_next = load(8, next_hbm, line.part.at[pl.ds(0, BLOCK)])
+    load_next.start()
     load(0, w_down_hbm, w_down).start()
-    for i in load_feed(0):
-        i.start()
+    if chunks > 1:
+        for i in load_feed(1):
+            i.start()
     load_normed(0).start()
     load(1, w_q_hbm, w_q).start()
     for i in load_grad(0):
@@ -1473,11 +1501,11 @@
         else:
             store_table.start()
 
-    load(0, w_down_hbm, w_down).wait()
-    produce(0)
+    load_next.wait()
     line.meet(peers)
     for k in range(3):
         line.slot(k)
+    load(0, w_down_hbm, w_down).wait()
     load(1, w_q_hbm, w_q).wait()
 
     def spread_block(v):
@@ -1530,7 +1558,7 @@
 
 def feed_and_input_grad(
     acts, w_down, middle, b_down, d_queries, all_query, d_keyval_sum, w_keyval, inputs, d_middle, gain,
-    normed, sums, b_up,
+    normed, feed_next, sums, b_up,
 ):
     seq, width = inputs.shape
     rounds = (lax.axis_size("dp") - 1).bit_length()
@@ -1548,7 +1576,7 @@
             shape(table, F32),
             shape((16, width), F32),
         ),
-        in_specs=[HBM] * 8 + [vmem] * 6,
+        in_specs=[HBM] * 9 + [vmem] * 6,
         out_specs=(HBM, HBM, HBM, vmem),
         scratch_shapes=[
             pltpu.VMEM(w_down.shape, BF16),
@@ -1569,7 +1597,7 @@
             pltpu.VMEM(table, F32),
             pltpu.VMEM(table, F32),
             pltpu.VMEM(table, F32),
-            dma((8,)),
+            dma((9,)),
             dma((3,)),
             dma((rounds,)),
             dma((rounds,)),
@@ -1587,7 +1615,7 @@
         ),
         name="feed_and_input_grad",
     )(
-        acts, w_down, middle, d_queries, all_query, inputs, d_middle, normed,
+        acts, w_down, middle, d_queries, all_query, inputs, d_middle, normed, feed_next,
         d_keyval_sum, w_keyval, gain.reshape(1, width), b_down.reshape(1, width), sums,
         b_up.reshape(1, width),
     )
@@ -1627,22 +1655,23 @@
         inputs, w_query, b_query, w_keyval, b_value, w_out, attn_gain, attn_shift, code_col, doc_row,
         cotangent, w_down,
     )
-    middle, acts, d_hidden, grad_w_down, grad_w_up, first, grad_b_up = mlp(
+    middle, acts, d_hidden, grad_w_down, grad_w_up, first, second, grad_b_up = mlp(
         mixed, all_out, inputs, w_up, d_acts, cotangent, b_out, mlp_gain, mlp_shift, b_up
     )
     grad_b_up = jnp.sum(grad_b_up, axis=0)
     grad_w_up = lax.psum_scatter(grad_w_up, "dp", scatter_dimension=0, tiled=True)
     grad_w_down = lax.psum_scatter(grad_w_down, "dp", scatter_dimension=1, tiled=True)
 
-    d_middle, d_queries, out_first, grads, d_keyval_sum, sums = mlp_attend_back(
-        d_hidden, w_up, all_out, middle, cotangent, queries, acts, w_down, normed_attn, mixed, first, own_cols,
+    d_middle, d_queries, out_first, feed_next, grads, d_keyval_sum, sums = mlp_attend_back(
+        d_hidden, w_up, all_out, middle, cotangent, queries, acts, w_down, normed_attn, mixed, first, second,
+        own_cols,
         keyval, keys_t, code_col, doc_row, lse, mlp_gain, b_down,
     )
     grads, grad_w_down, grad_w_up = lax.optimization_barrier((grads, grad_w_down, grad_w_up))
     grads = lax.psum_scatter(grads, "dp", scatter_dimension=1, tiled=True)
     out_rest, input_grad, grad_w_keyval, totals = feed_and_input_grad(
         acts, w_down, middle, b_down, d_queries, all_query, d_keyval_sum, w_keyval, inputs, d_middle,
-        attn_gain, normed_attn, sums, grad_b_up,
+        attn_gain, normed_attn, feed_next, sums, grad_b_up,
     )
     outputs = jnp.concatenate([out_first, out_rest], 0)
     grad_w_query, grad_w_out = grads[:own_cols].T, grads[own_cols:]

time: 646 us -> 642 us (level)
  transfers between devices with their start and end apart: 3 -> 3, of which waited for: 0 -> 0; matrix products, arithmetic and copies ran while one was open for 2% -> 2% of each run, Pallas kernels for 60% -> 59%
where the time goes in v5:
time: 642 us; the launch traced here: 631 us
  Pallas kernels  597 us (93%)
  between operations  14.3 us (2%)
  local copies, waits for them, and re-layouts  13.9 us (2%)
    pallas_call x1, Pallas kernels, mlp_attend_back(): pl.pallas_call(functools.partial(mlp_attend_back_kernel, heads), out_shap...  258 us
    pallas_call x1, Pallas kernels, attention_front(): pl.pallas_call(functools.partial(front_kernel, heads), out_shape=(shape(f...  133 us
    pallas_call x1, Pallas kernels, feed_and_input_grad(): pl.pallas_call(functools.partial(feed_kernel, rounds), out_shape=(shape((...  117 us
    pallas_call x1, Pallas kernels, mlp(): pl.pallas_call(mlp_kernel, out_shape=(shape((seq, width), F32), shape((se...  89 us
  transfers between devices with their start and end apart: 3, of which 0 were waited for; matrix products, arithmetic and copies ran while one was open for 2% of the time, Pallas kernels for 59%

profile of v5, /device:TPU:0, one launch (start us, length us, event | category | flops | bytes accessed | tf_op | source)
XLA Modules:
  0.0 631.3 jit_solution(4117617320549045636)
XLA Ops:
  7.2 0.0 reduce-scatter.4.cloned.1.call-start
  7.2 0.7 compare_select_fusion
  7.9 1.2 reshape.100.code_ref
  9.1 132.7 %attention_front.1 = (bf16[4,8,256,512]{3,2,1,0:T(8,128)(2,1)}, bf16[4,8,64,2048]{3,2,1,0:T(8,128)(2,1)}, bf16[1024,2048]{1,0:T(8,128)(2,1)}, bf16[1024,2048]{1,...) custom-call(bf16[8,256,512]{2,1,0:T(8,128)(2,1)} %bitcast.28, ...), custom_call_target="tpu_custom_call" | custom-call | tf_op jit(solution)/shard_map/attention_front/pallas_call | solution.py:475
  141.8 89.0 %mlp.1 = (f32[1024,2048]{1,0:T(8,128)}, bf16[1024,2048]{1,0:T(8,128)(2,1)}, bf16[1024,2048]{1,0:T(8,128)(2,1)}, f32[2048,2048]{1,0:T(8,128)}, f32[2048,2048]{1,0...) custom-call(bf16[1024,2048]{1,0:T(8,128)(2,1)} %get-tuple-element.47.mixed_hbm, ...), custom_call_target="tpu_custom_call" | custom-call | flops 60000002048 | bytes 67108864 | tf_op jit(solution)/shard_map/mlp/pallas_call | solution.py:933
  230.8 0.0 reduce-scatter.4.cloned.1.call-update
  230.9 0.0 reduce-scatter.6.cloned.1.call-start
  230.9 0.0 copy-start.1
  230.9 0.7 reduce-scatter.6.cloned.1.call-update
  231.6 0.0 reduce-scatter.8.cloned.1.call-start
  231.7 0.1 copy-done.1
  231.8 0.6 reduce_sum.9
  232.4 258.0 %mlp_attend_back.1 = (f32[1024,2048]{1,0:T(8,128)}, bf16[1024,2048]{1,0:T(8,128)(2,1)}, bf16[512,2048]{1,0:T(8,128)(2,1)}, f32[256,2048]{1,0:T(8,128)}, f32[1024...) custom-call(bf16[1024,2048]{1,0:T(8,128)(2,1)} %get-tuple-element.50.dh_hbm, ...), custom_call_target="tpu_custom_call" | custom-call | flops 199999995904 | bytes 33554432 | tf_op jit(solution)/shard_map/mlp_attend_back/pallas_call | solution.py:1266
  490.4 0.0 reduce-scatter.4.cloned.1.call-done
  490.4 0.0 reduce-scatter.6.cloned.1.call-done
  490.4 0.0 reduce-scatter.8.cloned.1.call-update
  490.4 117.1 %feed_and_input_grad.1 = (bf16[512,2048]{1,0:T(8,128)(2,1)}, bf16[1024,2048]{1,0:T(8,128)(2,1)}, f32[256,2048]{1,0:T(8,128)}, f32[16,2048]{1,0:T(8,128)}) custom-call(bf16[1024,2048]{1,0:T(8,128)(2,1)} %get-tuple-element.53.acts_hbm, bf16[2048,2048]{1,0:T(8,128)(2,1)} %w_down_hbm.5, f32[1024,2048]{1,0:T(8,128)} %get-tuple-element.51.mid_hbm, ...), custom_call_target="tpu_custom_call" | custom-call | flops 149999992832 | bytes 33554432 | tf_op jit(solution)/shard_map/feed_and_input_grad/pallas_call | solution.py:1571
  607.6 0.0 copy-start.2
  607.6 0.0 copy-start
  607.6 3.0 copy.39
  610.6 0.0 copy-done.2
  610.6 0.7 fusion.1
  611.3 0.6 constant_dynamic-slice_fusion
  611.8 0.5 slice_bitcast_fusion.1
  612.4 0.0 copy-done
  612.4 4.2 pad_maximum_fusion
  616.5 0.0 reduce-scatter.8.cloned.1.call-done
  616.5 2.1 fusion
  618.6 1.0 copy.38
  619.6 4.8 copy.41
  (1 shorter events, 0.0 us)
Async XLA Ops:
  7.2 483.2 %reduce-scatter.4.cloned.1.call-start = ((), (), s32[]{:S(2)}) async-start(), calls=%async_computation.3 | async-start | bytes 18874368 | tf_op jit(solution)/shard_map/reduce_scatter | solution.py:1663
  230.9 259.5 %reduce-scatter.6.cloned.1.call-start = ((), (), s32[]{:S(2)}) async-start(), calls=%async_computation.4 | async-start | bytes 18874368 | tf_op jit(solution)/shard_map/reduce_scatter | solution.py:1662
  230.9 0.8 copy-start.1
  231.6 384.9 %reduce-scatter.8.cloned.1.call-start = ((), (), s32[]{:S(2)}) async-start(), calls=%async_computation.5 | async-start | bytes 9437184 | tf_op jit(solution)/shard_map/reduce_scatter | solution.py:1671
  607.6 3.1 copy-start.2
  607.6 4.8 copy-start
Sparse Core Ops, SparseCore 0:
  231.0 120.4 reduce-scatter.3
  355.6 116.0 reduce-scatter.5
  490.6 77.2 reduce-scatter.7

commit v6 on v5

--- a/solution.py
+++ b/solution.py
@@ -1312,7 +1312,7 @@
     acts_hbm, w_down_hbm, mid_hbm, dq_hbm, w_q_hbm, in_hbm, d_mid_hbm, normed_hbm, next_hbm,
     dkv_f_ref, w_kv_ref, gain_ref, bias_ref, sums_in, b_up_in,
     out_hbm, in_grad_hbm, table_out, vectors_out,
-    w_down, w_q, acts, mid, dq, xs, d_mid, spread, low, in_grad, normed, dkv_ref, sums, trade, trade_in, table, table_in, table_all,
+    w_down, w_q, acts, mid, dq, xs, d_mid, spread, low, in_grad, normed, dkv_ref, sums, trade, trade_in, table, table_in, table_all, turned,
     load_sem, out_sem, t_send, t_recv, h_send, h_recv, d_send, d_recv, *line_refs,
 ):
     line = LineSum(line_refs)
@@ -1481,7 +1481,7 @@
             device_id=peers[r], device_id_type=MESH,
         )
 
-    store_table = pltpu.make_async_copy(table_all, table_out, out_sem.at[2])
+    store_table = pltpu.make_async_copy(turned, table_out, out_sem.at[2])
 
     def table_step(i):
         if 1 <= i <= rounds:
@@ -1499,6 +1499,9 @@
         elif i < 2 * rounds:
             double(2 * rounds - 1 - i, True).start()
         else:
+            for n in range(width // COLS):
+                at = pl.ds(n * COLS, COLS)
+                turned[at, :] = table_all[:, at].T
             store_table.start()
 
     load_next.wait()
@@ -1573,7 +1576,7 @@
         out_shape=(
             shape((rest, width), BF16),
             shape((seq, width), BF16),
-            shape(table, F32),
+            shape(table[::-1], F32),
             shape((16, width), F32),
         ),
         in_specs=[HBM] * 9 + [vmem] * 6,
@@ -1597,6 +1600,7 @@
             pltpu.VMEM(table, F32),
             pltpu.VMEM(table, F32),
             pltpu.VMEM(table, F32),
+            pltpu.VMEM(table[::-1], F32),
             dma((9,)),
             dma((3,)),
             dma((rounds,)),
@@ -1675,7 +1679,6 @@
     )
     outputs = jnp.concatenate([out_first, out_rest], 0)
     grad_w_query, grad_w_out = grads[:own_cols].T, grads[own_cols:]
-    grad_w_keyval = grad_w_keyval.T
     grad_attn_gain, grad_attn_shift, grad_mlp_gain, grad_mlp_shift = (totals[i] for i in range(4))
     grad_b_out, grad_b_down, grad_b_query, grad_b_up = (totals[i] for i in range(4, 8))
     grad_b_query = lax.dynamic_slice_in_dim(grad_b_query, own, own_cols, 0)

time: 642 us -> 644 us (level)
  transfers between devices with their start and end apart: 3 -> 3, of which waited for: 0 -> 0; matrix products, arithmetic and copies ran while one was open for 2% -> 1% of each run, Pallas kernels for 59% -> 59%
where the time goes in v6:
time: 644 us; the launch traced here: 632 us
  Pallas kernels  597 us (93%)
  local copies, waits for them, and re-layouts  14.5 us (2%)
  between operations  14.3 us (2%)
    pallas_call x1, Pallas kernels, mlp_attend_back(): pl.pallas_call(functools.partial(mlp_attend_back_kernel, heads), out_shap...  258 us
    pallas_call x1, Pallas kernels, attention_front(): pl.pallas_call(functools.partial(front_kernel, heads), out_shape=(shape(f...  133 us
    pallas_call x1, Pallas kernels, feed_and_input_grad(): pl.pallas_call(functools.partial(feed_kernel, rounds), out_shape=(shape((...  118 us
    pallas_call x1, Pallas kernels, mlp(): pl.pallas_call(mlp_kernel, out_shape=(shape((seq, width), F32), shape((se...  89 us
  transfers between devices with their start and end apart: 3, of which 0 were waited for; matrix products, arithmetic and copies ran while one was open for 1% of the time, Pallas kernels for 59%

profile of v6, /device:TPU:0, one launch (start us, length us, event | category | flops | bytes accessed | tf_op | source)
XLA Modules:
  0.0 632.4 jit_solution(17456356457786760933)
XLA Ops:
  7.2 0.0 reduce-scatter.4.cloned.1.call-start
  7.2 0.7 compare_select_fusion
  7.9 1.2 reshape.100.code_ref
  9.1 132.7 %attention_front.1 = (bf16[4,8,256,512]{3,2,1,0:T(8,128)(2,1)}, bf16[4,8,64,2048]{3,2,1,0:T(8,128)(2,1)}, bf16[1024,2048]{1,0:T(8,128)(2,1)}, bf16[1024,2048]{1,...) custom-call(bf16[8,256,512]{2,1,0:T(8,128)(2,1)} %bitcast.27, ...), custom_call_target="tpu_custom_call" | custom-call | tf_op jit(solution)/shard_map/attention_front/pallas_call | solution.py:475
  141.8 89.0 %mlp.1 = (f32[1024,2048]{1,0:T(8,128)}, bf16[1024,2048]{1,0:T(8,128)(2,1)}, bf16[1024,2048]{1,0:T(8,128)(2,1)}, f32[2048,2048]{1,0:T(8,128)}, f32[2048,2048]{1,0...) custom-call(bf16[1024,2048]{1,0:T(8,128)(2,1)} %get-tuple-element.47.mixed_hbm, ...), custom_call_target="tpu_custom_call" | custom-call | flops 60000002048 | bytes 67108864 | tf_op jit(solution)/shard_map/mlp/pallas_call | solution.py:933
  230.8 0.0 reduce-scatter.4.cloned.1.call-update
  230.9 0.0 reduce-scatter.6.cloned.1.call-start
  230.9 0.0 copy-start.2
  230.9 0.7 reduce-scatter.6.cloned.1.call-update
  231.6 0.0 reduce-scatter.8.cloned.1.call-start
  231.7 0.1 copy-done.2
  231.8 0.6 reduce_sum.9
  232.4 258.0 %mlp_attend_back.1 = (f32[1024,2048]{1,0:T(8,128)}, bf16[1024,2048]{1,0:T(8,128)(2,1)}, bf16[512,2048]{1,0:T(8,128)(2,1)}, f32[256,2048]{1,0:T(8,128)}, f32[1024...) custom-call(bf16[1024,2048]{1,0:T(8,128)(2,1)} %get-tuple-element.50.dh_hbm, ...), custom_call_target="tpu_custom_call" | custom-call | flops 199999995904 | bytes 33554432 | tf_op jit(solution)/shard_map/mlp_attend_back/pallas_call | solution.py:1266
  490.4 0.0 reduce-scatter.4.cloned.1.call-done
  490.4 0.0 reduce-scatter.6.cloned.1.call-done
  490.4 0.0 reduce-scatter.8.cloned.1.call-update
  490.4 0.0 copy-start.1
  490.4 117.6 %feed_and_input_grad.1 = (bf16[512,2048]{1,0:T(8,128)(2,1)}, bf16[1024,2048]{1,0:T(8,128)(2,1)}, f32[2048,256]{1,0:T(8,128)}, f32[16,2048]{1,0:T(8,128)}) custom-call(bf16[1024,2048]{1,0:T(8,128)(2,1)} %get-tuple-element.53.acts_hbm, bf16[2048,2048]{1,0:T(8,128)(2,1)} %w_down_hbm.5, f32[1024,2048]{1,0:T(8,128)} %get-tuple-element.51.mid_hbm, ...), custom_call_target="tpu_custom_call" | custom-call | flops 149999992832 | bytes 33554432 | tf_op jit(solution)/shard_map/feed_and_input_grad/pallas_call | solution.py:1574
  608.0 2.1 fusion.1
  610.1 0.6 constant_dynamic-slice_fusion
  610.7 1.2 slice_bitcast_fusion.1
  611.9 0.0 copy-done.1
  611.9 4.2 pad_maximum_fusion
  616.1 0.0 reduce-scatter.8.cloned.1.call-done
  616.1 2.1 fusion
  618.1 1.0 copy.37
  619.1 0.0 copy-start
  619.1 4.9 copy.40
  624.1 0.0 copy-done
  624.1 1.3 copy.41
  (1 shorter events, 0.0 us)
Async XLA Ops:
  7.2 483.2 %reduce-scatter.4.cloned.1.call-start = ((), (), s32[]{:S(2)}) async-start(), calls=%async_computation.3 | async-start | bytes 18874368 | tf_op jit(solution)/shard_map/reduce_scatter | solution.py:1667
  230.9 259.5 %reduce-scatter.6.cloned.1.call-start = ((), (), s32[]{:S(2)}) async-start(), calls=%async_computation.4 | async-start | bytes 18874368 | tf_op jit(solution)/shard_map/reduce_scatter | solution.py:1666
  230.9 0.8 copy-start.2
  231.6 384.4 %reduce-scatter.8.cloned.1.call-start = ((), (), s32[]{:S(2)}) async-start(), calls=%async_computation.5 | async-start | bytes 9437184 | tf_op jit(solution)/shard_map/reduce_scatter | solution.py:1675
  490.4 121.5 %copy-start.1 = (bf16[512,2048]{1,0:T(8,128)(2,1)S(1)}, bf16[512,2048]{1,0:T(8,128)(2,1)}, u32[]{:S(2)}) copy-start(bf16[512,2048]{1,0:T(8,128)(2,1)} %get-tuple-element.60) | copy-start | bytes 6291460
  619.1 4.9 copy-start
Sparse Core Ops, SparseCore 0:
  231.0 120.4 reduce-scatter.3
  355.6 116.0 reduce-scatter.5
  490.6 77.2 reduce-scatter.7
